TPU v7x, 32 devices: a whole 2x2x4 slice. The times are simulated.
32 devices in a mesh: track: 4 (over y, x), lateral: 4 (over z), depth: 2 (over core).
Axes of the slice: x: 2, y: 2, z: 4, core: 2. Of those that a mesh axis runs over, the one named last changes fastest.
Arguments:
- rhs: float32 [32, 8, 2, 64, 256], P('track', 'lateral', None, None, 'depth'), may hold values from -6 to 6
- start: float32 [32, 8, 2, 64, 256], P('track', 'lateral', None, None, 'depth'), may hold values from -6 to 6
- fine_blocks: bfloat16 [32, 8, 2, 27, 4096], P('track', 'lateral'), may hold values from -0.15625 to 0.15625
- fine_cols: int32 [32, 8, 2, 27], P('track', 'lateral'), may hold values from 0 to 26, each once within a row
- fine_mass: bfloat16 [32, 8, 2, 64], P('track', 'lateral'), may hold values from 4 to 8
- fine_smoother: bfloat16 [32, 8, 2, 4096], P('track', 'lateral'), may hold values from -0.05 to 0.25
- transfer: bfloat16 [32, 8, 2, 4096], P('track', 'lateral'), may hold values from -0.75 to 0.75
- aggregate: int32 [32, 8, 2], P('track', 'lateral'), may hold values from 0 to 31, as said below
- coarse_blocks: bfloat16 [32, 4, 2, 27, 4096], P(('track', 'lateral'), None, 'depth'), may hold values from -0.15625 to 0.15625
- coarse_cols: int32 [32, 4, 2, 27], P(('track', 'lateral'), None, 'depth'), may hold values from 0 to 26, each once within a row
- coarse_mass: bfloat16 [32, 4, 2, 64], P(('track', 'lateral'), None, 'depth'), may hold values from 1.5 to 3
- coarse_smoother: bfloat16 [32, 4, 2, 4096], P(('track', 'lateral'), None, 'depth'), may hold values from -0.2 to 1
Outputs:
- solution: float32 [32, 8, 2, 64, 256], P('track', 'lateral', None, None, 'depth')
Inputs may be any that keep to these rules, and one draw needn't show every extreme that they name: `fine_cols`: each row lists every neighbour code once. `coarse_cols`: each row lists every neighbour code once. `aggregate`: for every y and z, the entries at x = 8 * q to 8 * q + 7 are a permutation of those same x.
All inputs are finite; a program needn't handle non-finite values.
Results may differ from a plain program's by a relative error of at most 0.01.
The roundings to bfloat16 on the way count: a program that leaves them out, or rounds other values in their place, can miss the bound.
Values may be sent and summed in bfloat16 or wider, within the bound.
No kernel may reach another device: no remote copies, remote signals or barrier semaphores. Data moves between devices by JAX's collectives and lax.ppermute only.
A program may use at most 128 MiB of HBM per device.

v0:
```python
import functools

import jax
import jax.numpy as jnp
from jax import lax
from jax.experimental import pallas as pl
from jax.experimental.pallas import tpu as pltpu
from jax.sharding import PartitionSpec as P

SWEEPS = 2
DAMPING = 0.8
HALF = 32
LANES = 128
WIDE = 256
STEPS = 9
BF16 = jnp.bfloat16
F32 = jnp.float32
LIMIT = 8 * 1024 * 1024


def listed_at(cols_ref, slots, index, groups):
    for group in range(groups):
        codes = [cols_ref[index * groups + group, slot] for slot in range(27)]
        for slot, code in enumerate(codes):
            slots[group, code] = slot


def diagonal(mass, rows, groups):
    row = lax.broadcasted_iota(jnp.int32, (rows, LANES), 0)
    lane = lax.broadcasted_iota(jnp.int32, (rows, LANES), 1)
    spread = jnp.zeros((rows, LANES), F32)
    for group in range(groups):
        spread = jnp.where(row % groups == group, mass[group : group + 1], spread)
    return jnp.where(lane % 64 == 2 * (row // groups) + lane // 64, spread, 0.0)


def fine_sort_kernel(cols_ref, mass_ref, blocks_ref, out_ref, slots):
    second = lax.broadcasted_iota(jnp.int32, (2 * HALF, LANES), 0) % 2 == 1
    count = out_ref.shape[0]

    def column(index, carry):
        listed_at(cols_ref, slots, pl.program_id(0) * count + index, 2)
        for step in range(STEPS):
            for side in range(2):
                upper = blocks_ref[index, slots[0, 3 * step + side + 1]]
                lower = blocks_ref[index, slots[1, 3 * step + side]]
                span = slice(side * LANES, (side + 1) * LANES)
                out_ref[index, step * 2 * HALF : (step + 1) * 2 * HALF, span] = jnp.where(second, lower, upper)
        mass = mass_ref[index].astype(F32)
        mass = diagonal(jnp.concatenate([mass, mass], axis=1), 2 * HALF, 2)
        for side in range(2):
            span = slice(side * LANES, (side + 1) * LANES)
            out_ref[index, STEPS * 2 * HALF :, span] = jnp.where(second == (side == 1), mass, 0.0).astype(BF16)
        return carry

    lax.fori_loop(0, count, column, 0)


def coarse_sort_kernel(where_ref, cols_ref, mass_ref, smoother_ref, blocks_ref, *refs):
    pieces, (slots, scratch) = refs[:-2], refs[-2:]
    groups = blocks_ref.shape[2] // HALF
    each = groups // len(pieces)
    rows = groups * HALF
    kind = lax.broadcasted_iota(jnp.int32, (rows, LANES), 0) % groups

    def hand_out(values, first, span):
        scratch[...] = values
        for step, piece in enumerate(pieces):
            for part in range(each):
                y = lax.bitwise_xor(where_ref[1], step) * each + part
                taken = scratch[pl.ds(y, HALF, stride=groups), :]
                piece[part, first : first + HALF, span] = taken.astype(BF16)

    listed_at(cols_ref, slots, pl.program_id(0), groups)
    for step in range(STEPS):
        for side in range(2):
            code = 3 * step + side + 1 - where_ref[0]
            values = blocks_ref[0, slots[0, code]]
            for group in range(1, groups):
                values = jnp.where(kind == group, blocks_ref[0, slots[group, code]], values)
            hand_out(values.astype(F32), step * HALF, slice(side * LANES, (side + 1) * LANES))
    hand_out(smoother_ref[0].astype(F32), STEPS * HALF, slice(0, LANES))
    mass = mass_ref[0].astype(F32)
    mass = diagonal(jnp.concatenate([mass, mass], axis=1), rows, groups)
    hand_out(mass, STEPS * HALF, slice(LANES, WIDE))


def in_hbm(array):
    return pltpu.with_memory_space_constraint(array, pltpu.HBM)


def sort_fine(blocks, cols, mass):
    size_x, size_y, layers = blocks.shape[:3]
    columns = size_x * size_y
    paired = blocks.reshape(size_x, size_y, layers, 27, HALF, LANES).transpose(0, 1, 3, 4, 2, 5)
    batch = size_y
    rows = (STEPS + 1) * 2 * HALF
    return pl.pallas_call(
        fine_sort_kernel,
        grid=(columns // batch // 2,),
        in_specs=[
            SMEM,
            pl.BlockSpec((2 * batch, layers, 64), lambda i: (i, 0, 0)),
            pl.BlockSpec((2 * batch, 27, layers * HALF, LANES), lambda i: (i, 0, 0, 0)),
        ],
        out_specs=pl.BlockSpec((2 * batch, rows, WIDE), lambda i: (i, 0, 0)),
        out_shape=jax.ShapeDtypeStruct((columns, rows, WIDE), BF16),
        scratch_shapes=[pltpu.SMEM((2, 27), jnp.int32)],
        compiler_params=pltpu.CompilerParams(vmem_limit_bytes=LIMIT),
        name="sort_fine",
    )(
        cols.reshape(columns * layers, 27),
        in_hbm(mass.reshape(columns, layers, 64)),
        in_hbm(paired.reshape(columns, 27, layers * HALF, LANES)),
    )


def sort_coarse(where, blocks, cols, mass, smoother, count):
    size_x, size_y = blocks.shape[:2]
    paired = blocks.reshape(size_x, size_y, 27, HALF, LANES).transpose(0, 2, 3, 1, 4)
    smoothers = smoother.reshape(size_x, size_y, HALF, LANES).transpose(0, 2, 1, 3)
    each = size_y // count
    rows = (STEPS + 1) * HALF
    piece = jax.ShapeDtypeStruct((size_x * each, rows, WIDE), BF16)
    return pl.pallas_call(
        coarse_sort_kernel,
        grid=(size_x,),
        in_specs=[
            SMEM,
            SMEM,
            pl.BlockSpec((1, size_y, 64), lambda i: (i, 0, 0)),
            pl.BlockSpec((1, size_y * HALF, LANES), lambda i: (i, 0, 0)),
            pl.BlockSpec((1, 27, size_y * HALF, LANES), lambda i: (i, 0, 0, 0)),
        ],
        out_specs=[pl.BlockSpec((each, rows, WIDE), lambda i: (i, 0, 0))] * count,
        out_shape=[piece] * count,
        scratch_shapes=[pltpu.SMEM((size_y, 27), jnp.int32), pltpu.VMEM((size_y * HALF, LANES), F32)],
        compiler_params=pltpu.CompilerParams(vmem_limit_bytes=LIMIT),
        name="sort_coarse",
    )(
        where,
        cols.reshape(size_x * size_y, 27),
        in_hbm(mass.reshape(size_x, size_y, 64)),
        in_hbm(smoothers.reshape(size_x, size_y * HALF, LANES)),
        in_hbm(paired.reshape(size_x, 27, size_y * HALF, LANES)),
    )


def two_sided(block):
    none = jnp.zeros_like(block)
    return jnp.concatenate(
        [jnp.concatenate([block, none], axis=1), jnp.concatenate([none, block], axis=1)], axis=0
    )


def mask_layers(block, kind):
    none = jnp.zeros_like(block)
    return jnp.concatenate([jnp.where(kind == 0, block, none), jnp.where(kind == 1, block, none)], axis=1)


class Fine:
    def __init__(self, ops_ref, size_y):
        self.ops_ref, self.size_y = ops_ref, size_y

    def kind(self):
        return lax.broadcasted_iota(jnp.int32, (2 * HALF, LANES), 0) % 2

    def step(self, x, y, step):
        return self.ops_ref[x * self.size_y + y, step * 2 * HALF : (step + 1) * 2 * HALF, :]

    def mass(self, x, y):
        return self.step(x, y, STEPS)

    def half(self, total, place, z, parity):
        return total[(*place, parity, pl.ds(z, HALF, stride=2), slice(None))]


class Coarse(Fine):
    def kind(self):
        return lax.broadcasted_iota(jnp.int32, (2 * HALF, LANES), 0) // HALF

    def smoother(self, x, y):
        return self.step(x, y, STEPS)[:, :LANES]

    def mass(self, x, y):
        return mask_layers(self.step(x, y, STEPS)[:, LANES:], self.kind())

    def half(self, total, place, z, parity):
        return total[(*place, parity, pl.ds(z * HALF, HALF), slice(None))]


def join_coarse(where_ref, pieces, ops_ref, size_y):
    count = len(pieces) // 2
    each = pieces[0].shape[0] // size_y
    for index, piece in enumerate(pieces):
        layer = lax.bitwise_xor(where_ref[0], index // count)
        group = lax.bitwise_xor(where_ref[1], index % count)
        for part in range(piece.shape[0]):
            for step in range(STEPS + 1):
                rows = pl.ds(pl.multiple_of(step * 2 * HALF + layer * HALF, HALF), HALF)
                ops_ref[group * each * size_y + part, rows, :] = piece[part, step * HALF : (step + 1) * HALF, :]


def both_layers(cells):
    return jnp.concatenate([two_sided(cells[0]), two_sided(cells[1])], axis=0)


def add_from(total_ref, rows, cells, targets, own=None):
    left = [rows.step(*target) for target in targets]
    if own is not None:
        left.append(rows.mass(*own))
    given = jnp.dot(jnp.concatenate(left, axis=0), both_layers(cells), preferred_element_type=F32)
    parts = [given[index * 2 * HALF : (index + 1) * 2 * HALF] for index in range(len(left))]
    for (x, y, _), part in zip(targets, parts):
        if own is not None and own[0] is x and own[1] == y:
            part = part + parts[-1]
        for parity in range(2):
            total_ref[x, y, parity] += part[:, parity * LANES : (parity + 1) * LANES]


def natural(rows, total, place, scratch):
    blocks = []
    for z in range(2):
        for parity in range(2):
            scratch[z, pl.ds(parity, HALF, stride=2), :] = rows.half(total, place, z, parity)
        blocks.append(scratch[z])
    return blocks


def smoothed(rows, left, cells, total, place, scratch):
    given = jnp.dot(left, both_layers([cell.astype(BF16) for cell in cells]), preferred_element_type=F32)
    for parity in range(2):
        total[(*place, parity)] = given[:, parity * LANES : (parity + 1) * LANES]
    return natural(rows, total, place, scratch)


def over_columns(size_x, column):
    column(0, (-1, 0))
    lax.fori_loop(1, size_x - 1, lambda x, c: (column(x, (-1, 0, 1)), c)[1], 0)
    column(size_x - 1, (0, 1))


def inner_kernel(cells_ref, ops_ref, total_ref, *, grid):
    size_x, size_y = cells_ref.shape[:2]
    rows = grid(ops_ref, size_y)
    total_ref[...] = jnp.zeros_like(total_ref)

    def column(x, shifts):
        for near in range(size_y):
            targets = []
            for shift in shifts:
                own = x - shift if shift else x
                targets += [(own, y, (shift + 1) * 3 + near - y + 1) for y in range(size_y)]
            add_from(total_ref, rows, cells_ref[x, near], targets, (x, near))

    over_columns(size_x, column)


def beside_kernel(where_ref, one_ref, two_ref, ops_ref, given_ref, total_ref, *, grid):
    size_x, size_y = total_ref.shape[:2]
    rows = grid(ops_ref, size_y)
    total_ref[...] = given_ref[...]

    def side(ref, y, step):
        def column(x, shifts):
            add_from(total_ref, rows, ref[x], [(x - shift, y, (shift + 1) * 3 + step) for shift in shifts])

        over_columns(size_x, column)

    for odd, low_ref, high_ref in ((0, one_ref, two_ref), (1, two_ref, one_ref)):
        pl.when((where_ref[0] == odd) & (where_ref[1] > 0))(functools.partial(side, low_ref, 0, 0))
        pl.when((where_ref[0] == odd) & (where_ref[1] < where_ref[4] - 1))(functools.partial(side, high_ref, size_y - 1, 2))


def give_faces(where_ref, cells, one_ref, two_ref, x):
    even = where_ref[0] % 2 == 0
    for z in range(2):
        low, high = (cells[0][z], cells[-1][z]) if isinstance(cells, list) else (cells[0, z], cells[cells.shape[0] - 1, z])
        one_ref[x, z] = jnp.where(even, high, low)
        two_ref[x, z] = jnp.where(even, low, high)


def round_kernel(where_ref, start_ref, round_ref, one_ref, two_ref):
    for x in range(start_ref.shape[0]):
        cells = [[start_ref[x, y, z].astype(BF16) for z in range(2)] for y in range(start_ref.shape[1])]
        for y, column in enumerate(cells):
            for z in range(2):
                round_ref[x, y, z] = column[z]
        give_faces(where_ref, cells, one_ref, two_ref, x)


def round_start(where, start):
    size_x, size_y, layers, width, loads = start.shape
    batch = size_x // 4
    side = pl.BlockSpec((batch, layers, width, loads), lambda i: (i, 0, 0, 0))
    whole = pl.BlockSpec((batch, size_y, layers, width, loads), lambda i: (i, 0, 0, 0, 0))
    face = jax.ShapeDtypeStruct((size_x, layers, width, loads), BF16)
    return pl.pallas_call(
        round_kernel,
        grid=(4,),
        in_specs=[SMEM, whole],
        out_specs=[whole, side, side],
        out_shape=[jax.ShapeDtypeStruct(start.shape, BF16), face, face],
        compiler_params=pltpu.CompilerParams(vmem_limit_bytes=LIMIT),
        name="round_start",
    )(where, in_hbm(start))


def add_ends(where_ref, before_ref, after_ref, rows, total):
    size_x, size_y = total.shape[:2]
    for near in range(-1, size_y + 1):
        ys = [y for y in range(size_y) if abs(near - y) <= 1]
        place = near + 1
        if near in (-1, size_y):
            odd = where_ref[0] % 2
            place = odd * (size_y + 1) if near < 0 else (1 - odd) * (size_y + 1)
        inside = True
        if near < 0:
            inside = where_ref[1] > 0
        if near == size_y:
            inside = where_ref[1] < where_ref[4] - 1
        before, after = before_ref[place], after_ref[place]
        before = jnp.where((where_ref[2] > 0) & inside, before, jnp.zeros_like(before))
        after = jnp.where((where_ref[2] < where_ref[3] - 1) & inside, after, jnp.zeros_like(after))
        add_from(total, rows, before, [(0, y, near - y + 1) for y in ys])
        add_from(total, rows, after, [(size_x - 1, y, 6 + near - y + 1) for y in ys])


def per_column(size_x, size_y, body, after=None):
    def step(x, carry):
        for y in range(size_y):
            body(x, y)
        if after is not None:
            after(x)
        return carry

    lax.fori_loop(0, size_x, step, 0)


def smooth_kernel(
    where_ref, before_ref, after_ref, ops_ref, smoother_ref, given_ref, rhs_ref, old_ref, new_ref, round_ref, one_ref, two_ref,
    total, scratch,
):
    size_x, size_y = total.shape[:2]
    rows = Fine(ops_ref, size_y)
    total[...] = given_ref[...]
    add_ends(where_ref, before_ref, after_ref, rows, total)

    def body(x, y):
        applied = natural(rows, total, (x, y), scratch.at[0, y])
        residual = [rhs_ref[x, y, z] - applied[z] for z in range(2)]
        left = mask_layers(smoother_ref[x * size_y + y], rows.kind())
        change = smoothed(rows, left, residual, total, (x, y), scratch.at[1, y])
        for z in range(2):
            value = old_ref[x, y, z] + DAMPING * change[z]
            new_ref[x, y, z] = value
            round_ref[x, y, z] = value.astype(BF16)

    per_column(size_x, size_y, body, lambda x: give_faces(where_ref, round_ref.at[x], one_ref, two_ref, x))


def restrict_kernel(
    where_ref, group_ref, before_ref, after_ref, ops_ref, transfer_ref, given_ref, rhs_ref, *refs
):
    pieces = refs[:-8]
    coarse_ref, first_ref, round_ref, one_ref, two_ref, coarse_ops_ref, total, scratch = refs[-8:]
    size_x, size_y = total.shape[:2]
    coarse_y = coarse_ref.shape[1]
    rows = Fine(ops_ref, size_y)
    total[...] = given_ref[...]
    coarse_ref[...] = jnp.zeros_like(coarse_ref)
    add_ends(where_ref, before_ref, after_ref, rows, total)

    def body(x, y):
        applied = natural(rows, total, (x, y), scratch.at[0, y])
        for z in range(2):
            scratch[1, y, z] = rhs_ref[x, y, z] - applied[z]
            for parity in range(2):
                total[x, y, parity, pl.ds(z, HALF, stride=2), :] = scratch[1, y, z, pl.ds(parity, HALF, stride=2), :]
        left = mask_layers(transfer_ref[x * size_y + y], rows.kind())
        right = jnp.concatenate([total[x, y, 0], total[x, y, 1]], axis=1).astype(BF16)
        both = lax.dot_general(left, right, (((0,), (0,)), ((), ())), preferred_element_type=F32)
        for z in range(2):
            target = group_ref[(x * size_y + y) * 2 + z] - where_ref[2] * size_x
            own = both[z * LANES : (z + 1) * LANES]
            coarse_ref[target, y // 2, z] += own[:64, :LANES] + own[64:, LANES:]

    per_column(size_x, size_y, body)
    join_coarse(where_ref, pieces, coarse_ops_ref, coarse_y)
    coarse_rows = Coarse(coarse_ops_ref, coarse_y)

    def first(x, y):
        left = mask_layers(coarse_rows.smoother(x, y), coarse_rows.kind())
        cells = [coarse_ref[x, y, z] for z in range(2)]
        change = smoothed(coarse_rows, left, cells, total, (x, y), scratch.at[0, y])
        for z in range(2):
            value = DAMPING * change[z]
            first_ref[x, y, z] = value
            round_ref[x, y, z] = value.astype(BF16)

    per_column(size_x, coarse_y, first, lambda x: give_faces(where_ref, round_ref.at[x], one_ref, two_ref, x))


def correct_kernel(
    where_ref, group_ref, before_ref, after_ref, coarse_ops_ref, given_ref, coarse_ref, first_ref, transfer_ref,
    iterate_ref, out_ref, total, correction, scratch,
):
    size_x, coarse_y = total.shape[:2]
    size_y = out_ref.shape[1]
    coarse_rows = Coarse(coarse_ops_ref, coarse_y)
    total[...] = given_ref[...]
    add_ends(where_ref, before_ref, after_ref, coarse_rows, total)

    def second(x, y):
        applied = natural(coarse_rows, total, (x, y), scratch.at[0, y])
        remain = [coarse_ref[x, y, z] - applied[z] for z in range(2)]
        left = mask_layers(coarse_rows.smoother(x, y), coarse_rows.kind())
        change = smoothed(coarse_rows, left, remain, total, (x, y), scratch.at[1, y])
        for z in range(2):
            correction[x, y, z] = (first_ref[x, y, z] + DAMPING * change[z]).astype(BF16)

    per_column(size_x, coarse_y, second)
    rows = Fine(None, size_y)

    def added(x, y):
        sources = [group_ref[(x * size_y + y) * 2 + z] - where_ref[2] * size_x for z in range(2)]
        cells = [correction[sources[z], y // 2, z] for z in range(2)]
        left = mask_layers(transfer_ref[x * size_y + y], rows.kind())
        change = smoothed(rows, left, cells, total, (x, 0), scratch.at[0, y])
        for z in range(2):
            out_ref[x, y, z] = iterate_ref[x, y, z] + change[z]

    per_column(size_x, size_y, added)


SMEM = pl.BlockSpec(memory_space=pltpu.SMEM)
VMEM = pl.BlockSpec(memory_space=pltpu.VMEM)


def call(kernel, name, scalars, operands, out_shape, scratch=()):
    return pl.pallas_call(
        kernel,
        in_specs=[SMEM] * len(scalars) + [VMEM] * len(operands),
        out_specs=jax.tree.map(lambda _: VMEM, out_shape),
        out_shape=out_shape,
        scratch_shapes=list(scratch),
        compiler_params=pltpu.CompilerParams(vmem_limit_bytes=LIMIT),
        name=name,
    )(*scalars, *operands)


def swap_sides(one, two):
    lateral, depth = lax.axis_size("lateral"), lax.axis_size("depth")
    ring = [i * depth for i in range(lateral)] + [i * depth + 1 for i in reversed(range(lateral))]
    onward = list(zip(ring, ring[1:] + ring[:1]))
    back = [(b, a) for a, b in onward]
    return lax.ppermute(one, ("lateral", "depth"), onward), lax.ppermute(two, ("lateral", "depth"), back)


def swap_ends(cells, one, two):
    count = lax.axis_size("track")
    first = jnp.concatenate([one[:1], cells[0], two[:1]], axis=0)
    last = jnp.concatenate([one[-1:], cells[-1], two[-1:]], axis=0)
    before = lax.ppermute(last, "track", [(i, (i + 1) % count) for i in range(count)])
    after = lax.ppermute(first, "track", [((i + 1) % count, i) for i in range(count)])
    return before, after


def send_coarse(piece, step):
    count = lax.axis_size("lateral")
    return lax.ppermute(piece, "lateral", [(i, i ^ step) for i in range(count)])


def per_device(
    rhs,
    start,
    fine_blocks,
    fine_cols,
    fine_mass,
    fine_smoother,
    transfer,
    aggregate,
    coarse_blocks,
    coarse_cols,
    coarse_mass,
    coarse_smoother,
):
    size_x, size_y, size_z, width, loads = rhs.shape
    track, lateral, depth = (lax.axis_index(a) for a in ("track", "lateral", "depth"))
    count = lax.axis_size("lateral")
    where = jnp.stack([depth, lateral, track, jnp.int32(lax.axis_size("track")), jnp.int32(count)]).astype(jnp.int32)
    groups = aggregate.reshape(-1)
    part_x = coarse_blocks.shape[0]
    coarse_y = size_y // 2

    paired = lambda a: a.reshape(size_x, size_y, size_z, HALF, LANES).transpose(0, 1, 3, 2, 4).reshape(-1, 2 * HALF, LANES)
    smoothers, transfers = paired(fine_smoother), paired(transfer)
    field = (size_x, size_y, size_z, width, loads)
    coarse_field = (size_x, coarse_y, size_z, width, loads)
    sums = lambda shape: shape[:2] + (2, 2 * HALF, LANES)
    full = jax.ShapeDtypeStruct
    scratch = [pltpu.VMEM((2, size_y, 2, width, loads), F32)]

    def outer(cells, ops, grid, one, two, *others):
        shape = full(sums(cells.shape), F32)
        inner = call(functools.partial(inner_kernel, grid=grid), "inner", [], [cells, ops], shape)
        inner, one, two, *others = lax.optimization_barrier((inner, one, two, *others))
        before, after = swap_ends(cells, one, two)
        beside = call(functools.partial(beside_kernel, grid=grid), "beside", [where], [one, two, ops, inner], shape)
        return before, after, beside, *others

    face = full((size_x, size_z, width, loads), BF16)
    rounded, one, two = round_start(where, start)
    iterate = start
    later, one, two = lax.optimization_barrier((where, one, two))
    one, two = swap_sides(one, two)
    pieces = sort_coarse(later, coarse_blocks, coarse_cols, coarse_mass, coarse_smoother, count)
    fine_cols, *pieces = lax.optimization_barrier((fine_cols, *pieces))
    middle = count // 2 + 1
    pieces[1:middle] = [send_coarse(pieces[step], step) for step in range(1, middle)]
    fine_ops = sort_fine(fine_blocks, fine_cols, fine_mass)
    fine_total = [pltpu.VMEM(sums(field), F32)] + scratch
    for sweep in range(SWEEPS):
        last = sweep == SWEEPS - 1
        before, after, beside, *held = outer(rounded, fine_ops, Fine, one, two, *(pieces[middle:] if last else ()))
        if last:
            pieces[middle:] = [send_coarse(piece, middle + index) for index, piece in enumerate(held)]
        iterate, rounded, one, two = call(
            smooth_kernel, "smooth", [where], [before, after, fine_ops, smoothers, beside, rhs, iterate],
            [full(field, F32), full(field, BF16), face, face], fine_total,
        )
        if sweep == 0:
            one, *pieces[1:middle] = lax.optimization_barrier((one, *pieces[1:middle]))
        one, two = swap_sides(one, two)
    before, after, beside, *pieces[middle:] = outer(rounded, fine_ops, Fine, one, two, *pieces[middle:])
    pieces = pieces + [lax.ppermute(piece, "depth", [(0, 1), (1, 0)]) for piece in pieces]
    coarse_rows = full((size_x * coarse_y, (STEPS + 1) * 2 * HALF, WIDE), BF16)
    coarse_res, first, rounded, one, two, coarse_ops = call(
        restrict_kernel, "restrict", [where, groups], [before, after, fine_ops, transfers, beside, rhs, *pieces],
        [full(coarse_field, F32), full(coarse_field, F32), full(coarse_field, BF16), face, face, coarse_rows],
        fine_total,
    )
    one, two = swap_sides(one, two)
    before, after, beside = outer(rounded, coarse_ops, Coarse, one, two)
    return call(
        correct_kernel, "correct", [where, groups],
        [before, after, coarse_ops, beside, coarse_res, first, transfers, iterate],
        full(field, F32),
        [pltpu.VMEM(sums(coarse_field), F32), pltpu.VMEM(coarse_field, BF16)] + scratch,
    )


def solution(mesh):
    in_specs = (
        P("track", "lateral", None, None, "depth"),
        P("track", "lateral", None, None, "depth"),
        P("track", "lateral", None, None, None),
        P("track", "lateral", None, None),
        P("track", "lateral", None, None),
        P("track", "lateral", None, None),
        P("track", "lateral", None, None),
        P("track", "lateral", None),
        P(("track", "lateral"), None, "depth", None, None),
        P(("track", "lateral"), None, "depth", None),
        P(("track", "lateral"), None, "depth", None),
        P(("track", "lateral"), None, "depth", None),
    )
    out_specs = P("track", "lateral", None, None, "depth")
    return jax.shard_map(
        per_device, mesh=mesh, in_specs=in_specs, out_specs=out_specs, check_vma=False
    )
```

profile of v0, /device:TPU:0, one launch (start us, length us, event | category | flops | bytes accessed | tf_op | source)
XLA Modules:
  0.0 103.9 jit_solution(15759330573894343423)
XLA Ops:
  0.1 2.1 %round_start.1 = (bf16[8,2,2,64,128]{4,3,2,1,0:T(8,128)(2,1)S(1)}, bf16[8,2,64,128]{3,2,1,0:T(8,128)(2,1)S(1)}, bf16[8,2,64,128]{3,2,1,0:T(8,128)(2,1)S(1)}) custom-call(s32[5]{0:T(128)S(1)} %pad_add_fusion.where_ref, f32[8,2,2,64,128]{4,3,2,1,0:T(8,128)} %old_ref.1), custom_call_target="tpu_custom_call" | custom-call | tf_op jit(solution)/shard_map/round_start/pallas_call | solution.py:298
  2.2 3.0 %collective-permute-start = (bf16[8,2,64,128]{3,2,1,0:T(8,128)(2,1)S(1)}, bf16[8,2,64,128]{3,2,1,0:T(8,128)(2,1)S(1)}, u32[]{:S(2)}, u32[]{:S(2)}) collective-permute-start(bf16[8,2,64,128]{3,2,1,0:T(8,128)(2,1)S(1)} %get-tuple-element.60), channel_id=1, source_target_pairs={{0,2},{2,4},{4,6},{6,7},{7,5},{5,3},{3,1},{1,0},{8,10},{10,12},{12... | collective-permute-start | bytes 786440 | tf_op jit(solution)/shard_map/ppermute | solution.py:457
  5.9 3.2 %sort_coarse.1 = (bf16[2,320,256]{2,1,0:T(8,128)(2,1)S(1)}, bf16[2,320,256]{2,1,0:T(8,128)(2,1)S(1)}, bf16[2,320,256]{2,1,0:T(8,128)(2,1)S(1)}, bf16[2,320,256]{2,1,0:T(8,128)(2,1)S(1)}) custom-call(s32[5]{0:T(128)S(1)} %pad_add_fusion.where_ref, s32[8,27]{1,0:T(8,128)S(1)} %bitcast.53, bf16[2,4,64]{2,1,0:T(4,128)(2,1)} %bitcast.58, ...), custom_call_target="tpu_custom_call" | custom-call | tf_op jit(solution)/shard_map/sort_coarse/pallas_call | solution.py:125
  9.1 2.1 %collective-permute-start.4 = (bf16[2,320,256]{2,1,0:T(8,128)(2,1)S(1)}, bf16[2,320,256]{2,1,0:T(8,128)(2,1)}, u32[]{:S(2)}, u32[]{:S(2)}) collective-permute-start(bf16[2,320,256]{2,1,0:T(8,128)(2,1)S(1)} %get-tuple-element.67), channel_id=1, source_target_pairs={{0,2},{2,0},{4,6},{6,4},{1,3},{3,1},{5,7},{7,5},{8,10},{10,8},{12,... | collective-permute-start | bytes 983048 | tf_op jit(solution)/shard_map/ppermute | solution.py:471
  11.2 2.6 %collective-permute-start.5 = (bf16[2,320,256]{2,1,0:T(8,128)(2,1)S(1)}, bf16[2,320,256]{2,1,0:T(8,128)(2,1)}, u32[]{:S(2)}, u32[]{:S(2)}) collective-permute-start(bf16[2,320,256]{2,1,0:T(8,128)(2,1)S(1)} %get-tuple-element.68), channel_id=1, source_target_pairs={{0,4},{2,6},{4,0},{6,2},{1,5},{3,7},{5,1},{7,3},{8,12},{10,14},{12... | collective-permute-start | bytes 983048 | tf_op jit(solution)/shard_map/ppermute | solution.py:471
  14.5 6.1 %sort_fine.1.ops_ref = bf16[16,640,256]{2,1,0:T(8,128)(2,1)S(1)} custom-call(s32[32,27]{1,0:T(8,128)S(1)} %bitcast.52, bf16[16,2,64]{2,1,0:T(2,128)(2,1)} %bitcast.57, bf16[16,27,64,128]{3,2,1,0:T(8,128)(2,1)} %bitcast.54), custom_call_target="tpu_custom_call" | custom-call | tf_op jit(solution)/shard_map/sort_fine/pallas_call | solution.py:98
  20.6 2.5 %inner.4.given_ref = f32[8,2,2,64,128]{4,3,2,1,0:T(8,128)S(1)} custom-call(bf16[8,2,2,64,128]{4,3,2,1,0:T(8,128)(2,1)S(1)} %get-tuple-element.51.cells_ref, bf16[16,640,256]{2,1,0:T(8,128)(2,1)S(1)} %sort_fine.1.ops_ref), custom_call_target="tpu_custom_call" | custom-call | tf_op jit(solution)/shard_map/inner/pallas_call | solution.py:441
  26.2 2.1 %beside.4.given_ref = f32[8,2,2,64,128]{4,3,2,1,0:T(8,128)S(1)} custom-call(s32[5]{0:T(128)S(1)} %pad_add_fusion.where_ref, bf16[8,2,64,128]{3,2,1,0:T(8,128)(2,1)S(1)} %collective-permute-done.one_ref, bf16[8,2,64,128]{3,2,1,0:T(8,128)(2,1)S(1)} %collective-permute-done.1.two_ref, bf16[16,640,256]{2,1,0:T(8,128)(2,1)S(1)} %sort_fine.1.ops_ref, ...), custom_call_target="tpu_custom_call" | custom-call | tf_op jit(solution)/shard_map/beside/pallas_call | solution.py:441
  30.6 2.8 %smooth.2 = (f32[8,2,2,64,128]{4,3,2,1,0:T(8,128)S(1)}, bf16[8,2,2,64,128]{4,3,2,1,0:T(8,128)(2,1)S(1)}, bf16[8,2,64,128]{3,2,1,0:T(8,128)(2,1)S(1)}, bf16[8,2,64,128]{3,2,1,0:T(8,128)(2,1)S(1)}) custom-call(s32[5]{0:T(128)S(1)} %pad_add_fusion.where_ref, bf16[4,2,64,128]{3,2,1,0:T(8,128)(2,1)S(1)} %collective-permute-done.2.before_ref, ...), custom_call_target="tpu_custom_call" | custom-call | tf_op jit(solution)/shard_map/smooth/pallas_call | solution.py:441
  34.4 2.5 %inner.5.given_ref = f32[8,2,2,64,128]{4,3,2,1,0:T(8,128)S(1)} custom-call(bf16[8,2,2,64,128]{4,3,2,1,0:T(8,128)(2,1)S(1)} %get-tuple-element.65.cells_ref, bf16[16,640,256]{2,1,0:T(8,128)(2,1)S(1)} %sort_fine.1.ops_ref), custom_call_target="tpu_custom_call" | custom-call | tf_op jit(solution)/shard_map/inner/pallas_call | solution.py:441
  36.9 3.0 %collective-permute-done.6.one_ref = bf16[8,2,64,128]{3,2,1,0:T(8,128)(2,1)S(1)} collective-permute-done((bf16[8,2,64,128]{3,2,1,0:T(8,128)(2,1)S(1)}, bf16[8,2,64,128]{3,2,1,0:T(8,128)(2,1)S(1)}, u32[]{:S(2)}, u32[]{:S(2)}) %collective-permute-start.6) | collective-permute-done | bytes 262176 | tf_op jit(solution)/shard_map/ppermute | solution.py:457
  44.6 2.1 %beside.5.given_ref = f32[8,2,2,64,128]{4,3,2,1,0:T(8,128)S(1)} custom-call(s32[5]{0:T(128)S(1)} %pad_add_fusion.where_ref, bf16[8,2,64,128]{3,2,1,0:T(8,128)(2,1)S(1)} %collective-permute-done.6.one_ref, bf16[8,2,64,128]{3,2,1,0:T(8,128)(2,1)S(1)} %collective-permute-done.7.two_ref, bf16[16,640,256]{2,1,0:T(8,128)(2,1)S(1)} %sort_fine.1.ops_ref, ...), custom_call_target="tpu_custom_call" | custom-call | tf_op jit(solution)/shard_map/beside/pallas_call | solution.py:441
  47.5 2.7 %smooth.3 = (f32[8,2,2,64,128]{4,3,2,1,0:T(8,128)S(1)}, bf16[8,2,2,64,128]{4,3,2,1,0:T(8,128)(2,1)S(1)}, bf16[8,2,64,128]{3,2,1,0:T(8,128)(2,1)S(1)}, bf16[8,2,64,128]{3,2,1,0:T(8,128)(2,1)S(1)}) custom-call(s32[5]{0:T(128)S(1)} %pad_add_fusion.where_ref, bf16[4,2,64,128]{3,2,1,0:T(8,128)(2,1)S(1)} %collective-permute-done.8.before_ref, ...), custom_call_target="tpu_custom_call" | custom-call | tf_op jit(solution)/shard_map/smooth/pallas_call | solution.py:441
  50.3 2.5 %collective-permute-start.10 = (bf16[8,2,64,128]{3,2,1,0:T(8,128)(2,1)S(1)}, bf16[8,2,64,128]{3,2,1,0:T(8,128)(2,1)S(1)}, u32[]{:S(2)}, u32[]{:S(2)}) collective-permute-start(bf16[8,2,64,128]{3,2,1,0:T(8,128)(2,1)S(1)} %get-tuple-element.77), channel_id=1, source_target_pairs={{0,2},{2,4},{4,6},{6,7},{7,5},{5,3},{3,1},{1,0},{8,10},{10,12},{12... | collective-permute-start | bytes 786440 | tf_op jit(solution)/shard_map/ppermute | solution.py:457
  53.3 2.5 %inner.6.given_ref = f32[8,2,2,64,128]{4,3,2,1,0:T(8,128)S(1)} custom-call(bf16[8,2,2,64,128]{4,3,2,1,0:T(8,128)(2,1)S(1)} %get-tuple-element.76.cells_ref, bf16[16,640,256]{2,1,0:T(8,128)(2,1)S(1)} %sort_fine.1.ops_ref), custom_call_target="tpu_custom_call" | custom-call | tf_op jit(solution)/shard_map/inner/pallas_call | solution.py:441
  56.8 2.3 %collective-permute-done.11.two_ref = bf16[8,2,64,128]{3,2,1,0:T(8,128)(2,1)S(1)} collective-permute-done((bf16[8,2,64,128]{3,2,1,0:T(8,128)(2,1)S(1)}, bf16[8,2,64,128]{3,2,1,0:T(8,128)(2,1)S(1)}, u32[]{:S(2)}, u32[]{:S(2)}) %collective-permute-start.11) | collective-permute-done | bytes 262176 | tf_op jit(solution)/shard_map/ppermute | solution.py:457
  65.8 2.5 %copy-done.1 = bf16[16,640,256]{2,1,0:T(8,128)(2,1)S(1)} copy-done((bf16[16,640,256]{2,1,0:T(8,128)(2,1)S(1)}, bf16[16,640,256]{2,1,0:T(8,128)(2,1)}, u32[]{:S(2)}) %copy-start.1) | copy-done | bytes 5242904
  70.2 2.1 %beside.6.given_ref = f32[8,2,2,64,128]{4,3,2,1,0:T(8,128)S(1)} custom-call(s32[5]{0:T(128)S(1)} %pad_add_fusion.where_ref, bf16[8,2,64,128]{3,2,1,0:T(8,128)(2,1)S(1)} %copy-done.7, bf16[8,2,64,128]{3,2,1,0:T(8,128)(2,1)S(1)} %copy-done.9, bf16[16,640,256]{2,1,0:T(8,128)(2,1)S(1)} %copy-done.1, f32[8,2,2,64,128]{4,3,2,1,0:T(8,128)S(1)} %inner.6.given_ref), custom_call_target="tpu_custom_call" | custom-call | tf_op jit(solution)/shard_map/beside/pallas_call | solution.py:441
  72.4 5.7 %restrict.1 = (f32[8,1,2,64,128]{4,3,2,1,0:T(8,128)S(1)}, f32[8,1,2,64,128]{4,3,2,1,0:T(8,128)S(1)}, bf16[8,1,2,64,128]{4,3,2,1,0:T(8,128)(2,1)S(1)}, bf16[8,2,6...) custom-call(s32[5]{0:T(128)S(1)} %pad_add_fusion.where_ref, ...), custom_call_target="tpu_custom_call" | custom-call | tf_op jit(solution)/shard_map/restrict/pallas_call | solution.py:441
  78.1 8.3 %collective-permute-start.19 = (bf16[8,2,64,128]{3,2,1,0:T(8,128)(2,1)S(1)}, bf16[8,2,64,128]{3,2,1,0:T(8,128)(2,1)S(1)}, u32[]{:S(2)}, u32[]{:S(2)}) collective-permute-start(bf16[8,2,64,128]{3,2,1,0:T(8,128)(2,1)S(1)} %get-tuple-element.89), channel_id=1, source_target_pairs={{0,2},{2,4},{4,6},{6,7},{7,5},{5,3},{3,1},{1,0},{8,10},{10,12},{12... | collective-permute-start | bytes 786440 | tf_op jit(solution)/shard_map/ppermute | solution.py:457
  88.0 4.1 %collective-permute-done.19.one_ref = bf16[8,2,64,128]{3,2,1,0:T(8,128)(2,1)S(1)} collective-permute-done((bf16[8,2,64,128]{3,2,1,0:T(8,128)(2,1)S(1)}, bf16[8,2,64,128]{3,2,1,0:T(8,128)(2,1)S(1)}, u32[]{:S(2)}, u32[]{:S(2)}) %collective-permute-start.19) | collective-permute-done | bytes 262176 | tf_op jit(solution)/shard_map/ppermute | solution.py:457
  93.0 3.0 %collective-permute-start.22 = (bf16[3,2,64,128]{3,2,1,0:T(8,128)(2,1)S(1)}, bf16[3,2,64,128]{3,2,1,0:T(8,128)(2,1)S(1)}, u32[]{:S(2)}, u32[]{:S(2)}) collective-permute-start(bf16[3,2,64,128]{3,2,1,0:T(8,128)(2,1)S(1)} %pad_maximum_fusion.7), channel_id=1, source_target_pairs={{8,0},{16,8},{24,16},{0,24},{9,1},{17,9},{25,17},{1,25},{10,2},{18... | collective-permute-start | bytes 294920 | tf_op jit(solution)/shard_map/ppermute | solution.py:465
  95.9 2.0 %beside.7.given_ref = f32[8,1,2,64,128]{4,3,2,1,0:T(8,128)S(1)} custom-call(s32[5]{0:T(128)S(1)} %pad_add_fusion.where_ref, bf16[8,2,64,128]{3,2,1,0:T(8,128)(2,1)S(1)} %collective-permute-done.19.one_ref, bf16[8,2,64,128]{3,2,1,0:T(8,128)(2,1)S(1)} %collective-permute-done.20.two_ref, bf16[8,640,256]{2,1,0:T(8,128)(2,1)S(1)} %get-tuple-element.88.ops_ref.coarse_ops_ref, ...), custom_call_target="tpu_custom_call" | custom-call | tf_op jit(solution)/shard_map/beside/pallas_call | solution.py:441
  99.0 4.9 %correct.1 = f32[8,2,2,64,128]{4,3,2,1,0:T(8,128)} custom-call(s32[5]{0:T(128)S(1)} %pad_add_fusion.where_ref, s32[32]{0:T(128)S(1)} %reshape.45.group_ref, bf16[3,2,64,128]{3,2,1,0:T(8,128)(2,1)S(1)} %collective-permute-done.21.before_ref, bf16[3,2,64,128]{3,2,1,0:T(8,128)(2,1)S(1)} %collective-permute-done.22.after_ref, ...), custom_call_target="tpu_custom_call" | custom-call | tf_op jit(solution)/shard_map/correct/pallas_call | solution.py:441
  (94 shorter events, 26.9 us)
Async XLA Ops:
  2.2 20.9 %collective-permute-start = (bf16[8,2,64,128]{3,2,1,0:T(8,128)(2,1)S(1)}, bf16[8,2,64,128]{3,2,1,0:T(8,128)(2,1)S(1)}, u32[]{:S(2)}, u32[]{:S(2)}) collective-permute-start(bf16[8,2,64,128]{3,2,1,0:T(8,128)(2,1)S(1)} %get-tuple-element.60), channel_id=1, source_target_pairs={{0,2},{2,4},{4,6},{6,7},{7,5},{5,3},{3,1},{1,0},{8,10},{10,12},{12... | collective-permute-start | bytes 786440 | tf_op jit(solution)/shard_map/ppermute | solution.py:457
  5.2 17.9 %collective-permute-start.1 = (bf16[8,2,64,128]{3,2,1,0:T(8,128)(2,1)S(1)}, bf16[8,2,64,128]{3,2,1,0:T(8,128)(2,1)S(1)}, u32[]{:S(2)}, u32[]{:S(2)}) collective-permute-start(bf16[8,2,64,128]{3,2,1,0:T(8,128)(2,1)S(1)} %get-tuple-element.61), channel_id=1, source_target_pairs={{2,0},{4,2},{6,4},{7,6},{5,7},{3,5},{1,3},{0,1},{10,8},{12,10},{14... | collective-permute-start | bytes 786440 | tf_op jit(solution)/shard_map/ppermute | solution.py:457
  9.1 43.7 %copy-start.10 = (bf16[2,320,256]{2,1,0:T(8,128)(2,1)}, bf16[2,320,256]{2,1,0:T(8,128)(2,1)S(1)}, u32[]{:S(2)}) copy-start(bf16[2,320,256]{2,1,0:T(8,128)(2,1)S(1)} %get-tuple-element.83.refs_0_) | copy-start | bytes 983044
  9.1 24.2 %collective-permute-start.4 = (bf16[2,320,256]{2,1,0:T(8,128)(2,1)S(1)}, bf16[2,320,256]{2,1,0:T(8,128)(2,1)}, u32[]{:S(2)}, u32[]{:S(2)}) collective-permute-start(bf16[2,320,256]{2,1,0:T(8,128)(2,1)S(1)} %get-tuple-element.67), channel_id=1, source_target_pairs={{0,2},{2,0},{4,6},{6,4},{1,3},{3,1},{5,7},{7,5},{8,10},{10,8},{12,... | collective-permute-start | bytes 983048 | tf_op jit(solution)/shard_map/ppermute | solution.py:471
  11.2 22.2 %collective-permute-start.5 = (bf16[2,320,256]{2,1,0:T(8,128)(2,1)S(1)}, bf16[2,320,256]{2,1,0:T(8,128)(2,1)}, u32[]{:S(2)}, u32[]{:S(2)}) collective-permute-start(bf16[2,320,256]{2,1,0:T(8,128)(2,1)S(1)} %get-tuple-element.68), channel_id=1, source_target_pairs={{0,4},{2,6},{4,0},{6,2},{1,5},{3,7},{5,1},{7,3},{8,12},{10,14},{12... | collective-permute-start | bytes 983048 | tf_op jit(solution)/shard_map/ppermute | solution.py:471
  23.2 5.9 %collective-permute-start.2 = (bf16[4,2,64,128]{3,2,1,0:T(8,128)(2,1)S(1)}, bf16[4,2,64,128]{3,2,1,0:T(8,128)(2,1)S(1)}, u32[]{:S(2)}, u32[]{:S(2)}) collective-permute-start(bf16[4,2,64,128]{3,2,1,0:T(8,128)(2,1)S(1)} %pad_maximum_fusion), channel_id=1, source_target_pairs={{0,8},{8,16},{16,24},{24,0},{1,9},{9,17},{17,25},{25,1},{2,10},{10... | collective-permute-start | bytes 393224 | tf_op jit(solution)/shard_map/ppermute | solution.py:464
  24.8 5.8 %collective-permute-start.3 = (bf16[4,2,64,128]{3,2,1,0:T(8,128)(2,1)S(1)}, bf16[4,2,64,128]{3,2,1,0:T(8,128)(2,1)S(1)}, u32[]{:S(2)}, u32[]{:S(2)}) collective-permute-start(bf16[4,2,64,128]{3,2,1,0:T(8,128)(2,1)S(1)} %pad_maximum_fusion.1), channel_id=1, source_target_pairs={{8,0},{16,8},{24,16},{0,24},{9,1},{17,9},{25,17},{1,25},{10,2},{18... | collective-permute-start | bytes 393224 | tf_op jit(solution)/shard_map/ppermute | solution.py:465
  33.4 6.5 %collective-permute-start.6 = (bf16[8,2,64,128]{3,2,1,0:T(8,128)(2,1)S(1)}, bf16[8,2,64,128]{3,2,1,0:T(8,128)(2,1)S(1)}, u32[]{:S(2)}, u32[]{:S(2)}) collective-permute-start(bf16[8,2,64,128]{3,2,1,0:T(8,128)(2,1)S(1)} %get-tuple-element.69), channel_id=1, source_target_pairs={{0,2},{2,4},{4,6},{6,7},{7,5},{5,3},{3,1},{1,0},{8,10},{10,12},{12... | collective-permute-start | bytes 786440 | tf_op jit(solution)/shard_map/ppermute | solution.py:457
  34.4 6.4 %collective-permute-start.7 = (bf16[8,2,64,128]{3,2,1,0:T(8,128)(2,1)S(1)}, bf16[8,2,64,128]{3,2,1,0:T(8,128)(2,1)S(1)}, u32[]{:S(2)}, u32[]{:S(2)}) collective-permute-start(bf16[8,2,64,128]{3,2,1,0:T(8,128)(2,1)S(1)} %get-tuple-element.70), channel_id=1, source_target_pairs={{2,0},{4,2},{6,4},{7,6},{5,7},{3,5},{1,3},{0,1},{10,8},{12,10},{14... | collective-permute-start | bytes 786440 | tf_op jit(solution)/shard_map/ppermute | solution.py:457
  40.8 5.9 %collective-permute-start.8 = (bf16[4,2,64,128]{3,2,1,0:T(8,128)(2,1)S(1)}, bf16[4,2,64,128]{3,2,1,0:T(8,128)(2,1)S(1)}, u32[]{:S(2)}, u32[]{:S(2)}) collective-permute-start(bf16[4,2,64,128]{3,2,1,0:T(8,128)(2,1)S(1)} %pad_maximum_fusion.2), channel_id=1, source_target_pairs={{0,8},{8,16},{16,24},{24,0},{1,9},{9,17},{17,25},{25,1},{2,10},{10... | collective-permute-start | bytes 393224 | tf_op jit(solution)/shard_map/ppermute | solution.py:464
  42.4 5.2 %collective-permute-start.9 = (bf16[4,2,64,128]{3,2,1,0:T(8,128)(2,1)S(1)}, bf16[4,2,64,128]{3,2,1,0:T(8,128)(2,1)S(1)}, u32[]{:S(2)}, u32[]{:S(2)}) collective-permute-start(bf16[4,2,64,128]{3,2,1,0:T(8,128)(2,1)S(1)} %pad_maximum_fusion.3), channel_id=1, source_target_pairs={{8,0},{16,8},{24,16},{0,24},{9,1},{17,9},{25,17},{1,25},{10,2},{18... | collective-permute-start | bytes 393224 | tf_op jit(solution)/shard_map/ppermute | solution.py:465
  43.9 12.0 %collective-permute-start.12 = (bf16[2,320,256]{2,1,0:T(8,128)(2,1)S(1)}, bf16[2,320,256]{2,1,0:T(8,128)(2,1)}, u32[]{:S(2)}, u32[]{:S(2)}) collective-permute-start(bf16[2,320,256]{2,1,0:T(8,128)(2,1)S(1)} %get-tuple-element.79), channel_id=1, source_target_pairs={{0,6},{2,4},{4,2},{6,0},{1,7},{3,5},{5,3},{7,1},{8,14},{10,12},{12... | collective-permute-start | bytes 983048 | tf_op jit(solution)/shard_map/ppermute | solution.py:471
  50.3 6.5 %collective-permute-start.10 = (bf16[8,2,64,128]{3,2,1,0:T(8,128)(2,1)S(1)}, bf16[8,2,64,128]{3,2,1,0:T(8,128)(2,1)S(1)}, u32[]{:S(2)}, u32[]{:S(2)}) collective-permute-start(bf16[8,2,64,128]{3,2,1,0:T(8,128)(2,1)S(1)} %get-tuple-element.77), channel_id=1, source_target_pairs={{0,2},{2,4},{4,6},{6,7},{7,5},{5,3},{3,1},{1,0},{8,10},{10,12},{12... | collective-permute-start | bytes 786440 | tf_op jit(solution)/shard_map/ppermute | solution.py:457
  52.8 6.4 %collective-permute-start.11 = (bf16[8,2,64,128]{3,2,1,0:T(8,128)(2,1)S(1)}, bf16[8,2,64,128]{3,2,1,0:T(8,128)(2,1)S(1)}, u32[]{:S(2)}, u32[]{:S(2)}) collective-permute-start(bf16[8,2,64,128]{3,2,1,0:T(8,128)(2,1)S(1)} %get-tuple-element.78), channel_id=1, source_target_pairs={{2,0},{4,2},{6,4},{7,6},{5,7},{3,5},{1,3},{0,1},{10,8},{12,10},{14... | collective-permute-start | bytes 786440 | tf_op jit(solution)/shard_map/ppermute | solution.py:457
  52.8 10.5 %collective-permute-start.15 = (bf16[2,320,256]{2,1,0:T(8,128)(2,1)S(1)}, bf16[2,320,256]{2,1,0:T(8,128)(2,1)S(1)}, u32[]{:S(2)}, u32[]{:S(2)}) collective-permute-start(bf16[2,320,256]{2,1,0:T(8,128)(2,1)S(1)} %get-tuple-element.83.refs_0_), channel_id=1, source_target_pairs={{0,1},{1,0},{2,3},{3,2},{4,5},{5,4},{6,7},{7,6},{8,9},{9,8},{10,11... | collective-permute-start | bytes 983048 | tf_op jit(solution)/shard_map/ppermute | solution.py:536
  52.8 19.5 %collective-permute-start.16 = (bf16[2,320,256]{2,1,0:T(8,128)(2,1)}, bf16[2,320,256]{2,1,0:T(8,128)(2,1)}, u32[]{:S(2)}, u32[]{:S(2)}) collective-permute-start(bf16[2,320,256]{2,1,0:T(8,128)(2,1)} %collective-permute-done.4.refs_1_), channel_id=1, source_target_pairs={{0,1},{1,0},{2,3},{3,2},{4,5},{5,4},{6,7},{7,6},{8,9},{9,8},{10,11... | collective-permute-start | bytes 983048 | tf_op jit(solution)/shard_map/ppermute | solution.py:536
  55.8 16.5 %collective-permute-start.17 = (bf16[2,320,256]{2,1,0:T(8,128)(2,1)}, bf16[2,320,256]{2,1,0:T(8,128)(2,1)}, u32[]{:S(2)}, u32[]{:S(2)}) collective-permute-start(bf16[2,320,256]{2,1,0:T(8,128)(2,1)} %collective-permute-done.5.refs_2_), channel_id=1, source_target_pairs={{0,1},{1,0},{2,3},{3,2},{4,5},{5,4},{6,7},{7,6},{8,9},{9,8},{10,11... | collective-permute-start | bytes 983048 | tf_op jit(solution)/shard_map/ppermute | solution.py:536
  60.6 11.8 %collective-permute-start.18 = (bf16[2,320,256]{2,1,0:T(8,128)(2,1)}, bf16[2,320,256]{2,1,0:T(8,128)(2,1)}, u32[]{:S(2)}, u32[]{:S(2)}) collective-permute-start(bf16[2,320,256]{2,1,0:T(8,128)(2,1)} %collective-permute-done.12.refs_3_), channel_id=1, source_target_pairs={{0,1},{1,0},{2,3},{3,2},{4,5},{5,4},{6,7},{7,6},{8,9},{9,8},{10,11... | collective-permute-start | bytes 983048 | tf_op jit(solution)/shard_map/ppermute | solution.py:536
  61.3 11.1 %collective-permute-start.13 = (bf16[4,2,64,128]{3,2,1,0:T(8,128)(2,1)}, bf16[4,2,64,128]{3,2,1,0:T(8,128)(2,1)S(1)}, u32[]{:S(2)}, u32[]{:S(2)}) collective-permute-start(bf16[4,2,64,128]{3,2,1,0:T(8,128)(2,1)} %pad_maximum_fusion.4), channel_id=1, source_target_pairs={{0,8},{8,16},{16,24},{24,0},{1,9},{9,17},{17,25},{25,1},{2,10},{10... | collective-permute-start | bytes 393224 | tf_op jit(solution)/shard_map/ppermute | solution.py:464
  64.0 8.3 %collective-permute-start.14 = (bf16[4,2,64,128]{3,2,1,0:T(8,128)(2,1)}, bf16[4,2,64,128]{3,2,1,0:T(8,128)(2,1)}, u32[]{:S(2)}, u32[]{:S(2)}) collective-permute-start(bf16[4,2,64,128]{3,2,1,0:T(8,128)(2,1)} %pad_maximum_fusion.5), channel_id=1, source_target_pairs={{8,0},{16,8},{24,16},{0,24},{9,1},{17,9},{25,17},{1,25},{10,2},{18... | collective-permute-start | bytes 393224 | tf_op jit(solution)/shard_map/ppermute | solution.py:465
  78.1 14.0 %collective-permute-start.19 = (bf16[8,2,64,128]{3,2,1,0:T(8,128)(2,1)S(1)}, bf16[8,2,64,128]{3,2,1,0:T(8,128)(2,1)S(1)}, u32[]{:S(2)}, u32[]{:S(2)}) collective-permute-start(bf16[8,2,64,128]{3,2,1,0:T(8,128)(2,1)S(1)} %get-tuple-element.89), channel_id=1, source_target_pairs={{0,2},{2,4},{4,6},{6,7},{7,5},{5,3},{3,1},{1,0},{8,10},{10,12},{12... | collective-permute-start | bytes 786440 | tf_op jit(solution)/shard_map/ppermute | solution.py:457
  86.4 6.4 %collective-permute-start.20 = (bf16[8,2,64,128]{3,2,1,0:T(8,128)(2,1)S(1)}, bf16[8,2,64,128]{3,2,1,0:T(8,128)(2,1)S(1)}, u32[]{:S(2)}, u32[]{:S(2)}) collective-permute-start(bf16[8,2,64,128]{3,2,1,0:T(8,128)(2,1)S(1)} %get-tuple-element.90), channel_id=1, source_target_pairs={{2,0},{4,2},{6,4},{7,6},{5,7},{3,5},{1,3},{0,1},{10,8},{12,10},{14... | collective-permute-start | bytes 786440 | tf_op jit(solution)/shard_map/ppermute | solution.py:457
  92.9 5.6 %collective-permute-start.21 = (bf16[3,2,64,128]{3,2,1,0:T(8,128)(2,1)S(1)}, bf16[3,2,64,128]{3,2,1,0:T(8,128)(2,1)S(1)}, u32[]{:S(2)}, u32[]{:S(2)}) collective-permute-start(bf16[3,2,64,128]{3,2,1,0:T(8,128)(2,1)S(1)} %pad_maximum_fusion.6), channel_id=1, source_target_pairs={{0,8},{8,16},{16,24},{24,0},{1,9},{9,17},{17,25},{25,1},{2,10},{10... | collective-permute-start | bytes 294920 | tf_op jit(solution)/shard_map/ppermute | solution.py:464
  93.0 6.0 %collective-permute-start.22 = (bf16[3,2,64,128]{3,2,1,0:T(8,128)(2,1)S(1)}, bf16[3,2,64,128]{3,2,1,0:T(8,128)(2,1)S(1)}, u32[]{:S(2)}, u32[]{:S(2)}) collective-permute-start(bf16[3,2,64,128]{3,2,1,0:T(8,128)(2,1)S(1)} %pad_maximum_fusion.7), channel_id=1, source_target_pairs={{8,0},{16,8},{24,16},{0,24},{9,1},{17,9},{25,17},{1,25},{10,2},{18... | collective-permute-start | bytes 294920 | tf_op jit(solution)/shard_map/ppermute | solution.py:465
  (16 other events, 99.5 us)
where the time goes:
time: 104 us
  Pallas kernels  44.7 us (43%)
  starting transfers between devices  32.9 us (32%)
  waiting for transfers between devices  16.1 us (15%)
  local copies, waits for them, and re-layouts  8.3 us (8%)
  other arithmetic  1.52 us (1%)
    pallas_call x12, Pallas kernels, call(): pl.pallas_call(kernel, in_specs=[SMEM] * len(scalars) + [VMEM] * len(oper...  33.3 us
    ppermute x4, starting transfers between devices, swap_sides(): lax.ppermute(one, ('lateral', 'depth'), onward)  14.9 us
    unnamed x35, local copies, waits for them, and re-layouts  8.12 us
    ppermute x4, waiting for transfers between devices, swap_sides(): lax.ppermute(one, ('lateral', 'depth'), onward)  8.03 us
    ppermute x4, starting transfers between devices, swap_ends(): lax.ppermute(first, 'track', [((i + 1) % count, i) for i in range(count)])  7.54 us
    pallas_call x1, Pallas kernels, sort_fine(): pl.pallas_call(fine_sort_kernel, grid=(columns // batch // 2,), in_specs=...  6.06 us
    ppermute x3, starting transfers between devices, send_coarse(): return lax.ppermute(piece, 'lateral', [(i, i ^ step) for i in range(count)])  5.39 us
    ppermute x4, starting transfers between devices, swap_ends(): lax.ppermute(last, 'track', [(i, (i + 1) % count) for i in range(count)])  4.46 us
  transfers between devices with their start and end apart: 23, of which 12 were waited for; matrix products, arithmetic and copies ran while one was open for 2% of the time, Pallas kernels for 31%

commit v1 on v0

--- a/solution.py
+++ b/solution.py
@@ -56,7 +56,7 @@
     lax.fori_loop(0, count, column, 0)
 
 
-def coarse_sort_kernel(where_ref, cols_ref, mass_ref, smoother_ref, blocks_ref, *refs):
+def coarse_sort_kernel(cols_ref, mass_ref, smoother_ref, blocks_ref, *refs):
     pieces, (slots, scratch) = refs[:-2], refs[-2:]
     groups = blocks_ref.shape[2] // HALF
     each = groups // len(pieces)
@@ -67,14 +67,14 @@
         scratch[...] = values
         for step, piece in enumerate(pieces):
             for part in range(each):
-                y = lax.bitwise_xor(where_ref[1], step) * each + part
+                y = lax.bitwise_xor(lax.axis_index("lateral"), step) * each + part
                 taken = scratch[pl.ds(y, HALF, stride=groups), :]
                 piece[part, first : first + HALF, span] = taken.astype(BF16)
 
     listed_at(cols_ref, slots, pl.program_id(0), groups)
     for step in range(STEPS):
         for side in range(2):
-            code = 3 * step + side + 1 - where_ref[0]
+            code = 3 * step + side + 1 - lax.axis_index("depth")
             values = blocks_ref[0, slots[0, code]]
             for group in range(1, groups):
                 values = jnp.where(kind == group, blocks_ref[0, slots[group, code]], values)
@@ -109,13 +109,13 @@
         compiler_params=pltpu.CompilerParams(vmem_limit_bytes=LIMIT),
         name="sort_fine",
     )(
-        cols.reshape(columns * layers, 27),
+        in_hbm(cols.reshape(columns * layers, 27)),
         in_hbm(mass.reshape(columns, layers, 64)),
         in_hbm(paired.reshape(columns, 27, layers * HALF, LANES)),
     )
 
 
-def sort_coarse(where, blocks, cols, mass, smoother, count):
+def sort_coarse(blocks, cols, mass, smoother, count):
     size_x, size_y = blocks.shape[:2]
     paired = blocks.reshape(size_x, size_y, 27, HALF, LANES).transpose(0, 2, 3, 1, 4)
     smoothers = smoother.reshape(size_x, size_y, HALF, LANES).transpose(0, 2, 1, 3)
@@ -127,7 +127,6 @@
         grid=(size_x,),
         in_specs=[
             SMEM,
-            SMEM,
             pl.BlockSpec((1, size_y, 64), lambda i: (i, 0, 0)),
             pl.BlockSpec((1, size_y * HALF, LANES), lambda i: (i, 0, 0)),
             pl.BlockSpec((1, 27, size_y * HALF, LANES), lambda i: (i, 0, 0, 0)),
@@ -138,8 +137,7 @@
         compiler_params=pltpu.CompilerParams(vmem_limit_bytes=LIMIT),
         name="sort_coarse",
     )(
-        where,
-        cols.reshape(size_x * size_y, 27),
+        in_hbm(cols.reshape(size_x * size_y, 27)),
         in_hbm(mass.reshape(size_x, size_y, 64)),
         in_hbm(smoothers.reshape(size_x, size_y * HALF, LANES)),
         in_hbm(paired.reshape(size_x, 27, size_y * HALF, LANES)),
@@ -175,10 +173,23 @@
         return total[(*place, parity, pl.ds(z, HALF, stride=2), slice(None))]
 
 
-class Coarse(Fine):
+class Coarse:
+    def __init__(self, ops_ref, size_y):
+        self.ops_ref, self.size_y = ops_ref, size_y
+
     def kind(self):
         return lax.broadcasted_iota(jnp.int32, (2 * HALF, LANES), 0) // HALF
 
+    def step(self, x, y, step):
+        count, each = self.ops_ref.shape[1], self.ops_ref.shape[2] // self.size_y
+        x = jnp.asarray(x, jnp.int32)
+        group = lax.bitwise_xor(x // each, lax.axis_index("lateral"))
+        span = slice(step * HALF, (step + 1) * HALF)
+        rows = [
+            self.ops_ref[lax.bitwise_xor(lax.axis_index("depth"), z), group, x % each * self.size_y + y, span, :] for z in range(2)
+        ]
+        return jnp.concatenate(rows, axis=0)
+
     def smoother(self, x, y):
         return self.step(x, y, STEPS)[:, :LANES]
 
@@ -189,16 +200,8 @@
         return total[(*place, parity, pl.ds(z * HALF, HALF), slice(None))]
 
 
-def join_coarse(where_ref, pieces, ops_ref, size_y):
-    count = len(pieces) // 2
-    each = pieces[0].shape[0] // size_y
-    for index, piece in enumerate(pieces):
-        layer = lax.bitwise_xor(where_ref[0], index // count)
-        group = lax.bitwise_xor(where_ref[1], index % count)
-        for part in range(piece.shape[0]):
-            for step in range(STEPS + 1):
-                rows = pl.ds(pl.multiple_of(step * 2 * HALF + layer * HALF, HALF), HALF)
-                ops_ref[group * each * size_y + part, rows, :] = piece[part, step * HALF : (step + 1) * HALF, :]
+def rows_of(grid, ops_ref, size_y):
+    return Coarse(ops_ref, size_y) if grid is Coarse else Fine(ops_ref, size_y)
 
 
 def both_layers(cells):
@@ -242,7 +245,7 @@
 
 def inner_kernel(cells_ref, ops_ref, total_ref, *, grid):
     size_x, size_y = cells_ref.shape[:2]
-    rows = grid(ops_ref, size_y)
+    rows = rows_of(grid, ops_ref, size_y)
     total_ref[...] = jnp.zeros_like(total_ref)
 
     def column(x, shifts):
@@ -256,9 +259,9 @@
     over_columns(size_x, column)
 
 
-def beside_kernel(where_ref, one_ref, two_ref, ops_ref, given_ref, total_ref, *, grid):
+def beside_kernel(one_ref, two_ref, ops_ref, given_ref, total_ref, *, grid):
     size_x, size_y = total_ref.shape[:2]
-    rows = grid(ops_ref, size_y)
+    rows = rows_of(grid, ops_ref, size_y)
     total_ref[...] = given_ref[...]
 
     def side(ref, y, step):
@@ -268,28 +271,28 @@
         over_columns(size_x, column)
 
     for odd, low_ref, high_ref in ((0, one_ref, two_ref), (1, two_ref, one_ref)):
-        pl.when((where_ref[0] == odd) & (where_ref[1] > 0))(functools.partial(side, low_ref, 0, 0))
-        pl.when((where_ref[0] == odd) & (where_ref[1] < where_ref[4] - 1))(functools.partial(side, high_ref, size_y - 1, 2))
-
-
-def give_faces(where_ref, cells, one_ref, two_ref, x):
-    even = where_ref[0] % 2 == 0
+        pl.when((lax.axis_index("depth") == odd) & (lax.axis_index("lateral") > 0))(functools.partial(side, low_ref, 0, 0))
+        pl.when((lax.axis_index("depth") == odd) & (lax.axis_index("lateral") < lax.axis_size("lateral") - 1))(functools.partial(side, high_ref, size_y - 1, 2))
+
+
+def give_faces(cells, one_ref, two_ref, x):
+    even = lax.axis_index("depth") % 2 == 0
     for z in range(2):
         low, high = (cells[0][z], cells[-1][z]) if isinstance(cells, list) else (cells[0, z], cells[cells.shape[0] - 1, z])
         one_ref[x, z] = jnp.where(even, high, low)
         two_ref[x, z] = jnp.where(even, low, high)
 
 
-def round_kernel(where_ref, start_ref, round_ref, one_ref, two_ref):
+def round_kernel(start_ref, round_ref, one_ref, two_ref):
     for x in range(start_ref.shape[0]):
         cells = [[start_ref[x, y, z].astype(BF16) for z in range(2)] for y in range(start_ref.shape[1])]
         for y, column in enumerate(cells):
             for z in range(2):
                 round_ref[x, y, z] = column[z]
-        give_faces(where_ref, cells, one_ref, two_ref, x)
-
-
-def round_start(where, start):
+        give_faces(cells, one_ref, two_ref, x)
+
+
+def round_start(start):
     size_x, size_y, layers, width, loads = start.shape
     batch = size_x // 4
     side = pl.BlockSpec((batch, layers, width, loads), lambda i: (i, 0, 0, 0))
@@ -298,30 +301,30 @@
     return pl.pallas_call(
         round_kernel,
         grid=(4,),
-        in_specs=[SMEM, whole],
+        in_specs=[whole],
         out_specs=[whole, side, side],
         out_shape=[jax.ShapeDtypeStruct(start.shape, BF16), face, face],
         compiler_params=pltpu.CompilerParams(vmem_limit_bytes=LIMIT),
         name="round_start",
-    )(where, in_hbm(start))
-
-
-def add_ends(where_ref, before_ref, after_ref, rows, total):
+    )(in_hbm(start))
+
+
+def add_ends(before_ref, after_ref, rows, total):
     size_x, size_y = total.shape[:2]
     for near in range(-1, size_y + 1):
         ys = [y for y in range(size_y) if abs(near - y) <= 1]
         place = near + 1
         if near in (-1, size_y):
-            odd = where_ref[0] % 2
+            odd = lax.axis_index("depth") % 2
             place = odd * (size_y + 1) if near < 0 else (1 - odd) * (size_y + 1)
         inside = True
         if near < 0:
-            inside = where_ref[1] > 0
+            inside = lax.axis_index("lateral") > 0
         if near == size_y:
-            inside = where_ref[1] < where_ref[4] - 1
+            inside = lax.axis_index("lateral") < lax.axis_size("lateral") - 1
         before, after = before_ref[place], after_ref[place]
-        before = jnp.where((where_ref[2] > 0) & inside, before, jnp.zeros_like(before))
-        after = jnp.where((where_ref[2] < where_ref[3] - 1) & inside, after, jnp.zeros_like(after))
+        before = jnp.where((lax.axis_index("track") > 0) & inside, before, jnp.zeros_like(before))
+        after = jnp.where((lax.axis_index("track") < lax.axis_size("track") - 1) & inside, after, jnp.zeros_like(after))
         add_from(total, rows, before, [(0, y, near - y + 1) for y in ys])
         add_from(total, rows, after, [(size_x - 1, y, 6 + near - y + 1) for y in ys])
 
@@ -338,13 +341,13 @@
 
 
 def smooth_kernel(
-    where_ref, before_ref, after_ref, ops_ref, smoother_ref, given_ref, rhs_ref, old_ref, new_ref, round_ref, one_ref, two_ref,
+    before_ref, after_ref, ops_ref, smoother_ref, given_ref, rhs_ref, old_ref, new_ref, round_ref, one_ref, two_ref,
     total, scratch,
 ):
     size_x, size_y = total.shape[:2]
     rows = Fine(ops_ref, size_y)
     total[...] = given_ref[...]
-    add_ends(where_ref, before_ref, after_ref, rows, total)
+    add_ends(before_ref, after_ref, rows, total)
 
     def body(x, y):
         applied = natural(rows, total, (x, y), scratch.at[0, y])
@@ -356,20 +359,27 @@
             new_ref[x, y, z] = value
             round_ref[x, y, z] = value.astype(BF16)
 
-    per_column(size_x, size_y, body, lambda x: give_faces(where_ref, round_ref.at[x], one_ref, two_ref, x))
+    per_column(size_x, size_y, body, lambda x: give_faces(round_ref.at[x], one_ref, two_ref, x))
 
 
 def restrict_kernel(
-    where_ref, group_ref, before_ref, after_ref, ops_ref, transfer_ref, given_ref, rhs_ref, *refs
+    group_ref, before_ref, after_ref, ops_ref, transfer_ref, given_ref, rhs_ref, *refs, layers_at, groups_at
 ):
-    pieces = refs[:-8]
-    coarse_ref, first_ref, round_ref, one_ref, two_ref, coarse_ops_ref, total, scratch = refs[-8:]
+    pieces = refs[:-9]
+    coarse_ref, first_ref, round_ref, one_ref, two_ref, coarse_ops_ref, total, scratch, arrived = refs[-9:]
+    copies, filled = [], {}
+    for index, (layer, group, piece) in enumerate(zip(layers_at, groups_at, pieces)):
+        begin = filled.get((layer, group), 0)
+        filled[layer, group] = begin + piece.shape[0]
+        target = coarse_ops_ref.at[layer, group, pl.ds(begin, piece.shape[0])]
+        copies.append(pltpu.make_async_copy(piece, target, arrived.at[index]))
+        copies[-1].start()
     size_x, size_y = total.shape[:2]
     coarse_y = coarse_ref.shape[1]
     rows = Fine(ops_ref, size_y)
     total[...] = given_ref[...]
     coarse_ref[...] = jnp.zeros_like(coarse_ref)
-    add_ends(where_ref, before_ref, after_ref, rows, total)
+    add_ends(before_ref, after_ref, rows, total)
 
     def body(x, y):
         applied = natural(rows, total, (x, y), scratch.at[0, y])
@@ -381,12 +391,13 @@
         right = jnp.concatenate([total[x, y, 0], total[x, y, 1]], axis=1).astype(BF16)
         both = lax.dot_general(left, right, (((0,), (0,)), ((), ())), preferred_element_type=F32)
         for z in range(2):
-            target = group_ref[(x * size_y + y) * 2 + z] - where_ref[2] * size_x
+            target = group_ref[y, z, x] - lax.axis_index("track") * size_x
             own = both[z * LANES : (z + 1) * LANES]
             coarse_ref[target, y // 2, z] += own[:64, :LANES] + own[64:, LANES:]
 
     per_column(size_x, size_y, body)
-    join_coarse(where_ref, pieces, coarse_ops_ref, coarse_y)
+    for copy in copies:
+        copy.wait()
     coarse_rows = Coarse(coarse_ops_ref, coarse_y)
 
     def first(x, y):
@@ -398,18 +409,18 @@
             first_ref[x, y, z] = value
             round_ref[x, y, z] = value.astype(BF16)
 
-    per_column(size_x, coarse_y, first, lambda x: give_faces(where_ref, round_ref.at[x], one_ref, two_ref, x))
+    per_column(size_x, coarse_y, first, lambda x: give_faces(round_ref.at[x], one_ref, two_ref, x))
 
 
 def correct_kernel(
-    where_ref, group_ref, before_ref, after_ref, coarse_ops_ref, given_ref, coarse_ref, first_ref, transfer_ref,
+    group_ref, before_ref, after_ref, coarse_ops_ref, given_ref, coarse_ref, first_ref, transfer_ref,
     iterate_ref, out_ref, total, correction, scratch,
 ):
     size_x, coarse_y = total.shape[:2]
     size_y = out_ref.shape[1]
     coarse_rows = Coarse(coarse_ops_ref, coarse_y)
     total[...] = given_ref[...]
-    add_ends(where_ref, before_ref, after_ref, coarse_rows, total)
+    add_ends(before_ref, after_ref, coarse_rows, total)
 
     def second(x, y):
         applied = natural(coarse_rows, total, (x, y), scratch.at[0, y])
@@ -423,7 +434,7 @@
     rows = Fine(None, size_y)
 
     def added(x, y):
-        sources = [group_ref[(x * size_y + y) * 2 + z] - where_ref[2] * size_x for z in range(2)]
+        sources = [group_ref[y, z, x] - lax.axis_index("track") * size_x for z in range(2)]
         cells = [correction[sources[z], y // 2, z] for z in range(2)]
         left = mask_layers(transfer_ref[x * size_y + y], rows.kind())
         change = smoothed(rows, left, cells, total, (x, 0), scratch.at[0, y])
@@ -437,10 +448,12 @@
 VMEM = pl.BlockSpec(memory_space=pltpu.VMEM)
 
 
-def call(kernel, name, scalars, operands, out_shape, scratch=()):
+def call(kernel, name, scalars, operands, out_shape, scratch=(), outside=()):
+    operands = list(operands) + [in_hbm(array) for array in outside]
+    inside = len(operands) - len(outside)
     return pl.pallas_call(
         kernel,
-        in_specs=[SMEM] * len(scalars) + [VMEM] * len(operands),
+        in_specs=[SMEM] * len(scalars) + [VMEM] * inside + [pl.BlockSpec(memory_space=pltpu.HBM)] * len(outside),
         out_specs=jax.tree.map(lambda _: VMEM, out_shape),
         out_shape=out_shape,
         scratch_shapes=list(scratch),
@@ -469,6 +482,10 @@
 def send_coarse(piece, step):
     count = lax.axis_size("lateral")
     return lax.ppermute(piece, "lateral", [(i, i ^ step) for i in range(count)])
+
+
+def swap_layer(piece):
+    return lax.ppermute(piece, "depth", [(0, 1), (1, 0)])
 
 
 def per_device(
@@ -486,10 +503,8 @@
     coarse_smoother,
 ):
     size_x, size_y, size_z, width, loads = rhs.shape
-    track, lateral, depth = (lax.axis_index(a) for a in ("track", "lateral", "depth"))
     count = lax.axis_size("lateral")
-    where = jnp.stack([depth, lateral, track, jnp.int32(lax.axis_size("track")), jnp.int32(count)]).astype(jnp.int32)
-    groups = aggregate.reshape(-1)
+    groups = in_hbm(aggregate.transpose(1, 2, 0))
     part_x = coarse_blocks.shape[0]
     coarse_y = size_y // 2
 
@@ -506,44 +521,60 @@
         inner = call(functools.partial(inner_kernel, grid=grid), "inner", [], [cells, ops], shape)
         inner, one, two, *others = lax.optimization_barrier((inner, one, two, *others))
         before, after = swap_ends(cells, one, two)
-        beside = call(functools.partial(beside_kernel, grid=grid), "beside", [where], [one, two, ops, inner], shape)
+        beside = call(functools.partial(beside_kernel, grid=grid), "beside", [], [one, two, ops, inner], shape)
         return before, after, beside, *others
 
     face = full((size_x, size_z, width, loads), BF16)
-    rounded, one, two = round_start(where, start)
+    rounded, one, two = round_start(start)
     iterate = start
-    later, one, two = lax.optimization_barrier((where, one, two))
+    coarse_cols, one, two = lax.optimization_barrier((coarse_cols, one, two))
     one, two = swap_sides(one, two)
-    pieces = sort_coarse(later, coarse_blocks, coarse_cols, coarse_mass, coarse_smoother, count)
+    pieces = sort_coarse(coarse_blocks, coarse_cols, coarse_mass, coarse_smoother, count)
     fine_cols, *pieces = lax.optimization_barrier((fine_cols, *pieces))
+    groups_at = list(range(count))
     middle = count // 2 + 1
-    pieces[1:middle] = [send_coarse(pieces[step], step) for step in range(1, middle)]
+    early, late = pieces[:middle], pieces[middle:]
+    late_at = groups_at[middle:]
+    split = pieces[0].shape[0] // 2
+    if split:
+        early += [piece[:split] for piece in late]
+        late = [piece[split:] for piece in late]
+        groups_at = groups_at + late_at
+    early = [send_coarse(piece, groups_at[index]) if index else piece for index, piece in enumerate(early)]
     fine_ops = sort_fine(fine_blocks, fine_cols, fine_mass)
     fine_total = [pltpu.VMEM(sums(field), F32)] + scratch
     for sweep in range(SWEEPS):
         last = sweep == SWEEPS - 1
-        before, after, beside, *held = outer(rounded, fine_ops, Fine, one, two, *(pieces[middle:] if last else ()))
         if last:
-            pieces[middle:] = [send_coarse(piece, middle + index) for index, piece in enumerate(held)]
+            before, after, beside, *held = outer(rounded, fine_ops, Fine, one, two, *late, *early_other)
+            late, early_other = held[: len(late)], held[len(late) :]
+            late = [send_coarse(piece, group) for piece, group in zip(late, late_at)]
+        else:
+            before, after, beside = outer(rounded, fine_ops, Fine, one, two)
         iterate, rounded, one, two = call(
-            smooth_kernel, "smooth", [where], [before, after, fine_ops, smoothers, beside, rhs, iterate],
+            smooth_kernel, "smooth", [], [before, after, fine_ops, smoothers, beside, rhs, iterate],
             [full(field, F32), full(field, BF16), face, face], fine_total,
         )
-        if sweep == 0:
-            one, *pieces[1:middle] = lax.optimization_barrier((one, *pieces[1:middle]))
+        if last:
+            one, *late = lax.optimization_barrier((one, *late))
+        else:
+            one, *early = lax.optimization_barrier((one, *early))
+            early_other = [swap_layer(piece) for piece in early]
         one, two = swap_sides(one, two)
-    before, after, beside, *pieces[middle:] = outer(rounded, fine_ops, Fine, one, two, *pieces[middle:])
-    pieces = pieces + [lax.ppermute(piece, "depth", [(0, 1), (1, 0)]) for piece in pieces]
-    coarse_rows = full((size_x * coarse_y, (STEPS + 1) * 2 * HALF, WIDE), BF16)
+    before, after, beside, *late = outer(rounded, fine_ops, Fine, one, two, *late)
+    pieces = early + late + early_other + [swap_layer(piece) for piece in late]
+    layers_at = [0] * len(groups_at) + [1] * len(groups_at)
+    coarse_rows = full((2, count, part_x * coarse_y, (STEPS + 1) * HALF, WIDE), BF16)
     coarse_res, first, rounded, one, two, coarse_ops = call(
-        restrict_kernel, "restrict", [where, groups], [before, after, fine_ops, transfers, beside, rhs, *pieces],
+        functools.partial(restrict_kernel, layers_at=layers_at, groups_at=groups_at * 2),
+        "restrict", [groups], [before, after, fine_ops, transfers, beside, rhs],
         [full(coarse_field, F32), full(coarse_field, F32), full(coarse_field, BF16), face, face, coarse_rows],
-        fine_total,
+        fine_total + [pltpu.SemaphoreType.DMA((len(pieces),))], pieces,
     )
     one, two = swap_sides(one, two)
     before, after, beside = outer(rounded, coarse_ops, Coarse, one, two)
     return call(
-        correct_kernel, "correct", [where, groups],
+        correct_kernel, "correct", [groups],
         [before, after, coarse_ops, beside, coarse_res, first, transfers, iterate],
         full(field, F32),
         [pltpu.VMEM(sums(coarse_field), F32), pltpu.VMEM(coarse_field, BF16)] + scratch,

time: 104 us -> 95.6 us (0.919)
  waiting for transfers between devices: 16.1 us -> 25.3 us
  local copies, waits for them, and re-layouts: 8.3 us -> 0.84 us
  starting transfers between devices: 32.9 us -> 28 us
  Pallas kernels: 44.7 us -> 40.5 us
  other arithmetic: 1.52 us -> 0.14 us
    ppermute x4, starting transfers between devices: 14.9 us -> 6.87 us  [swap_sides(): lax.ppermute(one, ('lateral', 'depth'), onward)]
    unnamed x35 -> x28, local copies, waits for them, and re-layouts: 8.12 us -> 0.73 us
    pallas_call x14, Pallas kernels: 38.6 us -> 34.5 us  [the longest x12 29.3 us: call(): pl.pallas_call(kernel, in_specs=[SMEM] * len(scalars) + [VMEM] * inside +...]
    ppermute x4, waiting for transfers between devices: 1.32 us -> 5.32 us  [swap_ends(): lax.ppermute(last, 'track', [(i, (i + 1) % count) for i in range(count)])]
    ppermute x4, waiting for transfers between devices: 3.9 us -> 6.73 us  [swap_sides(): lax.ppermute(two, ('lateral', 'depth'), back)]
    ppermute x3 -> x4, starting transfers between devices: 5.39 us -> 7.81 us  [send_coarse(): return lax.ppermute(piece, 'lateral', [(i, i ^ step) for i in range(count)])]
    ppermute x3 -> x4, waiting for transfers between devices: 0.01 us -> 1.93 us  [send_coarse(): return lax.ppermute(piece, 'lateral', [(i, i ^ step) for i in range(count)])]
    ppermute x4, waiting for transfers between devices: 2.82 us -> 4.14 us  [swap_ends(): lax.ppermute(first, 'track', [((i + 1) % count, i) for i in range(count)])]
  transfers between devices with their start and end apart: 23 -> 25, of which waited for: 12 -> 14; matrix products, arithmetic and copies ran while one was open for 2% -> 0% of each run, Pallas kernels for 31% -> 30%
where the time goes in v1:
time: 95.6 us; the launch traced here: 95.4 us
  Pallas kernels  40.5 us (42%)
  starting transfers between devices  28 us (29%)
  waiting for transfers between devices  25.3 us (26%)
    pallas_call x12, Pallas kernels, call(): pl.pallas_call(kernel, in_specs=[SMEM] * len(scalars) + [VMEM] * inside +...  29.3 us
    ppermute x4, starting transfers between devices, send_coarse(): return lax.ppermute(piece, 'lateral', [(i, i ^ step) for i in range(count)])  7.81 us
    ppermute x4, starting transfers between devices, swap_sides(): lax.ppermute(one, ('lateral', 'depth'), onward)  6.87 us
    ppermute x4, waiting for transfers between devices, swap_sides(): lax.ppermute(one, ('lateral', 'depth'), onward)  6.84 us
    ppermute x4, waiting for transfers between devices, swap_sides(): lax.ppermute(two, ('lateral', 'depth'), back)  6.73 us
    ppermute x4, starting transfers between devices, swap_ends(): lax.ppermute(first, 'track', [((i + 1) % count, i) for i in range(count)])  6.67 us
    pallas_call x1, Pallas kernels, sort_fine(): pl.pallas_call(fine_sort_kernel, grid=(columns // batch // 2,), in_specs=...  6.06 us
    ppermute x4, starting transfers between devices, swap_ends(): lax.ppermute(last, 'track', [(i, (i + 1) % count) for i in range(count)])  5.48 us
  transfers between devices with their start and end apart: 25, of which 14 were waited for; matrix products, arithmetic and copies ran while one was open for 0% of the time, Pallas kernels for 30%

profile of v1, /device:TPU:0, one launch (start us, length us, event | category | flops | bytes accessed | tf_op | source)
XLA Modules:
  0.0 95.4 jit_solution(8747974510547872029)
XLA Ops:
  0.0 2.1 %round_start.1 = (bf16[8,2,2,64,128]{4,3,2,1,0:T(8,128)(2,1)S(1)}, bf16[8,2,64,128]{3,2,1,0:T(8,128)(2,1)S(1)}, bf16[8,2,64,128]{3,2,1,0:T(8,128)(2,1)S(1)}) custom-call(f32[8,2,2,64,128]{4,3,2,1,0:T(8,128)} %old_ref.1), custom_call_target="tpu_custom_call" | custom-call | tf_op jit(solution)/shard_map/round_start/pallas_call | solution.py:301
  2.1 3.0 %collective-permute-start = (bf16[8,2,64,128]{3,2,1,0:T(8,128)(2,1)S(1)}, bf16[8,2,64,128]{3,2,1,0:T(8,128)(2,1)S(1)}, u32[]{:S(2)}, u32[]{:S(2)}) collective-permute-start(bf16[8,2,64,128]{3,2,1,0:T(8,128)(2,1)S(1)} %get-tuple-element.68), channel_id=1, source_target_pairs={{0,2},{2,4},{4,6},{6,7},{7,5},{5,3},{3,1},{1,0},{8,10},{10,12},{12... | collective-permute-start | bytes 786440 | tf_op jit(solution)/shard_map/ppermute | solution.py:470
  5.1 3.1 %sort_coarse.1 = (bf16[2,320,256]{2,1,0:T(8,128)(2,1)S(1)}, bf16[2,320,256]{2,1,0:T(8,128)(2,1)S(1)}, bf16[2,320,256]{2,1,0:T(8,128)(2,1)S(1)}, bf16[2,320,256]{2,1,0:T(8,128)(2,1)S(1)}) custom-call(s32[8,27]{1,0:T(8,128)} %bitcast.57, bf16[2,4,64]{2,1,0:T(4,128)(2,1)} %bitcast.58, bf16[2,128,128]{2,1,0:T(8,128)(2,1)} %bitcast.52, ...), custom_call_target="tpu_custom_call" | custom-call | tf_op jit(solution)/shard_map/sort_coarse/pallas_call | solution.py:125
  8.3 4.1 %collective-permute-start.6 = (bf16[1,320,256]{2,1,0:T(8,128)(2,1)S(1)}, bf16[1,320,256]{2,1,0:T(8,128)(2,1)S(1)}, u32[]{:S(2)}, u32[]{:S(2)}) collective-permute-start(bf16[1,320,256]{2,1,0:T(8,128)(2,1)S(1)} %get-tuple-element.120), channel_id=1, source_target_pairs={{0,6},{2,4},{4,2},{6,0},{1,7},{3,5},{5,3},{7,1},{8,14},{10,12},{12... | collective-permute-start | bytes 491528 | tf_op jit(solution)/shard_map/ppermute | solution.py:484
  13.0 6.1 %sort_fine.1.ops_ref = bf16[16,640,256]{2,1,0:T(8,128)(2,1)S(1)} custom-call(s32[32,27]{1,0:T(8,128)} %bitcast.53, bf16[16,2,64]{2,1,0:T(2,128)(2,1)} %bitcast.54, bf16[16,27,64,128]{3,2,1,0:T(8,128)(2,1)} %bitcast.50), custom_call_target="tpu_custom_call" | custom-call | tf_op jit(solution)/shard_map/sort_fine/pallas_call | solution.py:98
  19.1 2.5 %inner.4.given_ref = f32[8,2,2,64,128]{4,3,2,1,0:T(8,128)S(1)} custom-call(bf16[8,2,2,64,128]{4,3,2,1,0:T(8,128)(2,1)S(1)} %get-tuple-element.59.cells_ref, bf16[16,640,256]{2,1,0:T(8,128)(2,1)S(1)} %sort_fine.1.ops_ref), custom_call_target="tpu_custom_call" | custom-call | tf_op jit(solution)/shard_map/inner/pallas_call | solution.py:454
  26.3 1.7 %collective-permute-done.2.before_ref = bf16[4,2,64,128]{3,2,1,0:T(8,128)(2,1)S(1)} collective-permute-done((bf16[4,2,64,128]{3,2,1,0:T(8,128)(2,1)S(1)}, bf16[4,2,64,128]{3,2,1,0:T(8,128)(2,1)S(1)}, u32[]{:S(2)}, u32[]{:S(2)}) %collective-permute-start.2) | collective-permute-done | bytes 131104 | tf_op jit(solution)/shard_map/ppermute | solution.py:477
  29.5 2.2 %smooth.2 = (f32[8,2,2,64,128]{4,3,2,1,0:T(8,128)S(1)}, bf16[8,2,2,64,128]{4,3,2,1,0:T(8,128)(2,1)S(1)}, bf16[8,2,64,128]{3,2,1,0:T(8,128)(2,1)S(1)}, bf16[8,2,64,128]{3,2,1,0:T(8,128)(2,1)S(1)}) custom-call(bf16[4,2,64,128]{3,2,1,0:T(8,128)(2,1)S(1)} %collective-permute-done.2.before_ref, bf16[4,2,64,128]{3,2,1,0:T(8,128)(2,1)S(1)} %collective-permute-done.3.after_ref, ...), custom_call_target="tpu_custom_call" | custom-call | tf_op jit(solution)/shard_map/smooth/pallas_call | solution.py:454
  31.8 1.9 %collective-permute-done.5.refs_2_ = bf16[2,320,256]{2,1,0:T(8,128)(2,1)S(1)} collective-permute-done((bf16[2,320,256]{2,1,0:T(8,128)(2,1)S(1)}, bf16[2,320,256]{2,1,0:T(8,128)(2,1)S(1)}, u32[]{:S(2)}, u32[]{:S(2)}) %collective-permute-start.5) | collective-permute-done | bytes 327712 | tf_op jit(solution)/shard_map/ppermute | solution.py:484
  35.2 2.5 %inner.5.given_ref = f32[8,2,2,64,128]{4,3,2,1,0:T(8,128)S(1)} custom-call(bf16[8,2,2,64,128]{4,3,2,1,0:T(8,128)(2,1)S(1)} %get-tuple-element.73.cells_ref, bf16[16,640,256]{2,1,0:T(8,128)(2,1)S(1)} %sort_fine.1.ops_ref), custom_call_target="tpu_custom_call" | custom-call | tf_op jit(solution)/shard_map/inner/pallas_call | solution.py:454
  37.7 2.9 %collective-permute-done.7.one_ref = bf16[8,2,64,128]{3,2,1,0:T(8,128)(2,1)S(1)} collective-permute-done((bf16[8,2,64,128]{3,2,1,0:T(8,128)(2,1)S(1)}, bf16[8,2,64,128]{3,2,1,0:T(8,128)(2,1)S(1)}, u32[]{:S(2)}, u32[]{:S(2)}) %collective-permute-start.7) | collective-permute-done | bytes 262176 | tf_op jit(solution)/shard_map/ppermute | solution.py:470
  40.6 2.4 %collective-permute-done.8.two_ref = bf16[8,2,64,128]{3,2,1,0:T(8,128)(2,1)S(1)} collective-permute-done((bf16[8,2,64,128]{3,2,1,0:T(8,128)(2,1)S(1)}, bf16[8,2,64,128]{3,2,1,0:T(8,128)(2,1)S(1)}, u32[]{:S(2)}, u32[]{:S(2)}) %collective-permute-start.8) | collective-permute-done | bytes 262176 | tf_op jit(solution)/shard_map/ppermute | solution.py:470
  44.7 3.1 %collective-permute-start.15 = (bf16[1,320,256]{2,1,0:T(8,128)(2,1)S(1)}, bf16[1,320,256]{2,1,0:T(8,128)(2,1)S(1)}, u32[]{:S(2)}, u32[]{:S(2)}) collective-permute-start(bf16[1,320,256]{2,1,0:T(8,128)(2,1)S(1)} %get-tuple-element.91), channel_id=1, source_target_pairs={{0,6},{2,4},{4,2},{6,0},{1,7},{3,5},{5,3},{7,1},{8,14},{10,12},{12... | collective-permute-start | bytes 491528 | tf_op jit(solution)/shard_map/ppermute | solution.py:484
  50.8 1.9 %collective-permute-done.14.after_ref = bf16[4,2,64,128]{3,2,1,0:T(8,128)(2,1)S(1)} collective-permute-done((bf16[4,2,64,128]{3,2,1,0:T(8,128)(2,1)S(1)}, bf16[4,2,64,128]{3,2,1,0:T(8,128)(2,1)S(1)}, u32[]{:S(2)}, u32[]{:S(2)}) %collective-permute-start.14) | collective-permute-done | bytes 131104 | tf_op jit(solution)/shard_map/ppermute | solution.py:478
  52.8 2.2 %smooth.3 = (f32[8,2,2,64,128]{4,3,2,1,0:T(8,128)S(1)}, bf16[8,2,2,64,128]{4,3,2,1,0:T(8,128)(2,1)S(1)}, bf16[8,2,64,128]{3,2,1,0:T(8,128)(2,1)S(1)}, bf16[8,2,64,128]{3,2,1,0:T(8,128)(2,1)S(1)}) custom-call(bf16[4,2,64,128]{3,2,1,0:T(8,128)(2,1)S(1)} %collective-permute-done.13.before_ref, bf16[4,2,64,128]{3,2,1,0:T(8,128)(2,1)S(1)} %collective-permute-done.14.after_ref, ...), custom_call_target="tpu_custom_call" | custom-call | tf_op jit(solution)/shard_map/smooth/pallas_call | solution.py:454
  55.1 2.0 %collective-permute-start.16 = (bf16[8,2,64,128]{3,2,1,0:T(8,128)(2,1)S(1)}, bf16[8,2,64,128]{3,2,1,0:T(8,128)(2,1)S(1)}, u32[]{:S(2)}, u32[]{:S(2)}) collective-permute-start(bf16[8,2,64,128]{3,2,1,0:T(8,128)(2,1)S(1)} %get-tuple-element.92), channel_id=1, source_target_pairs={{0,2},{2,4},{4,6},{6,7},{7,5},{5,3},{3,1},{1,0},{8,10},{10,12},{12... | collective-permute-start | bytes 786440 | tf_op jit(solution)/shard_map/ppermute | solution.py:470
  57.0 2.5 %inner.6.given_ref = f32[8,2,2,64,128]{4,3,2,1,0:T(8,128)S(1)} custom-call(bf16[8,2,2,64,128]{4,3,2,1,0:T(8,128)(2,1)S(1)} %get-tuple-element.89.cells_ref, bf16[16,640,256]{2,1,0:T(8,128)(2,1)S(1)} %sort_fine.1.ops_ref), custom_call_target="tpu_custom_call" | custom-call | tf_op jit(solution)/shard_map/inner/pallas_call | solution.py:454
  59.6 3.5 %collective-permute-done.17.two_ref = bf16[8,2,64,128]{3,2,1,0:T(8,128)(2,1)S(1)} collective-permute-done((bf16[8,2,64,128]{3,2,1,0:T(8,128)(2,1)S(1)}, bf16[8,2,64,128]{3,2,1,0:T(8,128)(2,1)S(1)}, u32[]{:S(2)}, u32[]{:S(2)}) %collective-permute-start.17) | collective-permute-done | bytes 262176 | tf_op jit(solution)/shard_map/ppermute | solution.py:470
  64.0 2.1 %collective-permute-start.19 = (bf16[4,2,64,128]{3,2,1,0:T(8,128)(2,1)S(1)}, bf16[4,2,64,128]{3,2,1,0:T(8,128)(2,1)S(1)}, u32[]{:S(2)}, u32[]{:S(2)}) collective-permute-start(bf16[4,2,64,128]{3,2,1,0:T(8,128)(2,1)S(1)} %pad_maximum_fusion.5), channel_id=1, source_target_pairs={{8,0},{16,8},{24,16},{0,24},{9,1},{17,9},{25,17},{1,25},{10,2},{18... | collective-permute-start | bytes 393224 | tf_op jit(solution)/shard_map/ppermute | solution.py:478
  67.7 2.6 %collective-permute-done.18.before_ref = bf16[4,2,64,128]{3,2,1,0:T(8,128)(2,1)S(1)} collective-permute-done((bf16[4,2,64,128]{3,2,1,0:T(8,128)(2,1)S(1)}, bf16[4,2,64,128]{3,2,1,0:T(8,128)(2,1)S(1)}, u32[]{:S(2)}, u32[]{:S(2)}) %collective-permute-start.18) | collective-permute-done | bytes 131104 | tf_op jit(solution)/shard_map/ppermute | solution.py:477
  71.1 4.9 %restrict.1 = (f32[8,1,2,64,128]{4,3,2,1,0:T(8,128)S(1)}, f32[8,1,2,64,128]{4,3,2,1,0:T(8,128)S(1)}, bf16[8,1,2,64,128]{4,3,2,1,0:T(8,128)(2,1)S(1)}, bf16[8,2,6...) custom-call(s32[2,2,8]{2,1,0:T(2,128)} %bitcast.55, ...), custom_call_target="tpu_custom_call" | custom-call | tf_op jit(solution)/shard_map/restrict/pallas_call | solution.py:454
  76.0 1.8 %collective-permute-start.21 = (bf16[8,2,64,128]{3,2,1,0:T(8,128)(2,1)S(1)}, bf16[8,2,64,128]{3,2,1,0:T(8,128)(2,1)S(1)}, u32[]{:S(2)}, u32[]{:S(2)}) collective-permute-start(bf16[8,2,64,128]{3,2,1,0:T(8,128)(2,1)S(1)} %get-tuple-element.105), channel_id=1, source_target_pairs={{0,2},{2,4},{4,6},{6,7},{7,5},{5,3},{3,1},{1,0},{8,10},{10,12},{12... | collective-permute-start | bytes 786440 | tf_op jit(solution)/shard_map/ppermute | solution.py:470
  79.4 4.0 %collective-permute-done.21.one_ref = bf16[8,2,64,128]{3,2,1,0:T(8,128)(2,1)S(1)} collective-permute-done((bf16[8,2,64,128]{3,2,1,0:T(8,128)(2,1)S(1)}, bf16[8,2,64,128]{3,2,1,0:T(8,128)(2,1)S(1)}, u32[]{:S(2)}, u32[]{:S(2)}) %collective-permute-start.21) | collective-permute-done | bytes 262176 | tf_op jit(solution)/shard_map/ppermute | solution.py:470
  90.3 5.0 %correct.1 = f32[8,2,2,64,128]{4,3,2,1,0:T(8,128)} custom-call(s32[2,2,8]{2,1,0:T(2,128)} %bitcast.56, bf16[3,2,64,128]{3,2,1,0:T(8,128)(2,1)S(1)} %collective-permute-done.23.before_ref, bf16[3,2,64,128]{3,2,1,0:T(8,128)(2,1)S(1)} %collective-permute-done.24.after_ref, bf16[2,4,2,320,256]{4,3,2,1,0:T(8,128)(2,1)S(1)} %get-tuple-element.104.ops_ref.coarse_ops_ref, ...), custom_call_target="tpu_custom_call" | custom-call | tf_op jit(solution)/shard_map/correct/pallas_call | solution.py:454
  (89 shorter events, 24.9 us)
Async XLA Ops:
  2.1 19.5 %collective-permute-start = (bf16[8,2,64,128]{3,2,1,0:T(8,128)(2,1)S(1)}, bf16[8,2,64,128]{3,2,1,0:T(8,128)(2,1)S(1)}, u32[]{:S(2)}, u32[]{:S(2)}) collective-permute-start(bf16[8,2,64,128]{3,2,1,0:T(8,128)(2,1)S(1)} %get-tuple-element.68), channel_id=1, source_target_pairs={{0,2},{2,4},{4,6},{6,7},{7,5},{5,3},{3,1},{1,0},{8,10},{10,12},{12... | collective-permute-start | bytes 786440 | tf_op jit(solution)/shard_map/ppermute | solution.py:470
  5.1 16.5 %collective-permute-start.1 = (bf16[8,2,64,128]{3,2,1,0:T(8,128)(2,1)S(1)}, bf16[8,2,64,128]{3,2,1,0:T(8,128)(2,1)S(1)}, u32[]{:S(2)}, u32[]{:S(2)}) collective-permute-start(bf16[8,2,64,128]{3,2,1,0:T(8,128)(2,1)S(1)} %get-tuple-element.69), channel_id=1, source_target_pairs={{2,0},{4,2},{6,4},{7,6},{5,7},{3,5},{1,3},{0,1},{10,8},{12,10},{14... | collective-permute-start | bytes 786440 | tf_op jit(solution)/shard_map/ppermute | solution.py:470
  8.3 23.4 %collective-permute-start.6 = (bf16[1,320,256]{2,1,0:T(8,128)(2,1)S(1)}, bf16[1,320,256]{2,1,0:T(8,128)(2,1)S(1)}, u32[]{:S(2)}, u32[]{:S(2)}) collective-permute-start(bf16[1,320,256]{2,1,0:T(8,128)(2,1)S(1)} %get-tuple-element.120), channel_id=1, source_target_pairs={{0,6},{2,4},{4,2},{6,0},{1,7},{3,5},{5,3},{7,1},{8,14},{10,12},{12... | collective-permute-start | bytes 491528 | tf_op jit(solution)/shard_map/ppermute | solution.py:484
  12.4 19.4 %collective-permute-start.4 = (bf16[2,320,256]{2,1,0:T(8,128)(2,1)S(1)}, bf16[2,320,256]{2,1,0:T(8,128)(2,1)S(1)}, u32[]{:S(2)}, u32[]{:S(2)}) collective-permute-start(bf16[2,320,256]{2,1,0:T(8,128)(2,1)S(1)} %get-tuple-element.76), channel_id=1, source_target_pairs={{0,2},{2,0},{4,6},{6,4},{1,3},{3,1},{5,7},{7,5},{8,10},{10,8},{12,... | collective-permute-start | bytes 983048 | tf_op jit(solution)/shard_map/ppermute | solution.py:484
  12.4 21.3 %collective-permute-start.5 = (bf16[2,320,256]{2,1,0:T(8,128)(2,1)S(1)}, bf16[2,320,256]{2,1,0:T(8,128)(2,1)S(1)}, u32[]{:S(2)}, u32[]{:S(2)}) collective-permute-start(bf16[2,320,256]{2,1,0:T(8,128)(2,1)S(1)} %get-tuple-element.77), channel_id=1, source_target_pairs={{0,4},{2,6},{4,0},{6,2},{1,5},{3,7},{5,1},{7,3},{8,12},{10,14},{12... | collective-permute-start | bytes 983048 | tf_op jit(solution)/shard_map/ppermute | solution.py:484
  21.7 6.3 %collective-permute-start.2 = (bf16[4,2,64,128]{3,2,1,0:T(8,128)(2,1)S(1)}, bf16[4,2,64,128]{3,2,1,0:T(8,128)(2,1)S(1)}, u32[]{:S(2)}, u32[]{:S(2)}) collective-permute-start(bf16[4,2,64,128]{3,2,1,0:T(8,128)(2,1)S(1)} %pad_maximum_fusion), channel_id=1, source_target_pairs={{0,8},{8,16},{16,24},{24,0},{1,9},{9,17},{17,25},{25,1},{2,10},{10... | collective-permute-start | bytes 393224 | tf_op jit(solution)/shard_map/ppermute | solution.py:477
  23.3 6.2 %collective-permute-start.3 = (bf16[4,2,64,128]{3,2,1,0:T(8,128)(2,1)S(1)}, bf16[4,2,64,128]{3,2,1,0:T(8,128)(2,1)S(1)}, u32[]{:S(2)}, u32[]{:S(2)}) collective-permute-start(bf16[4,2,64,128]{3,2,1,0:T(8,128)(2,1)S(1)} %pad_maximum_fusion.1), channel_id=1, source_target_pairs={{8,0},{16,8},{24,16},{0,24},{9,1},{17,9},{25,17},{1,25},{10,2},{18... | collective-permute-start | bytes 393224 | tf_op jit(solution)/shard_map/ppermute | solution.py:478
  33.7 9.3 %collective-permute-start.9 = (bf16[2,320,256]{2,1,0:T(8,128)(2,1)S(1)}, bf16[2,320,256]{2,1,0:T(8,128)(2,1)S(1)}, u32[]{:S(2)}, u32[]{:S(2)}) collective-permute-start(bf16[2,320,256]{2,1,0:T(8,128)(2,1)S(1)} %get-tuple-element.81.refs_0_), channel_id=1, source_target_pairs={{0,1},{1,0},{2,3},{3,2},{4,5},{5,4},{6,7},{7,6},{8,9},{9,8},{10,11... | collective-permute-start | bytes 983048 | tf_op jit(solution)/shard_map/ppermute | solution.py:488
  34.2 8.8 %collective-permute-start.10 = (bf16[2,320,256]{2,1,0:T(8,128)(2,1)S(1)}, bf16[2,320,256]{2,1,0:T(8,128)(2,1)S(1)}, u32[]{:S(2)}, u32[]{:S(2)}) collective-permute-start(bf16[2,320,256]{2,1,0:T(8,128)(2,1)S(1)} %collective-permute-done.4.refs_1_), channel_id=1, source_target_pairs={{0,1},{1,0},{2,3},{3,2},{4,5},{5,4},{6,7},{7,6},{8,9},{9,8},{10,11... | collective-permute-start | bytes 983048 | tf_op jit(solution)/shard_map/ppermute | solution.py:488
  34.3 8.7 %collective-permute-start.11 = (bf16[2,320,256]{2,1,0:T(8,128)(2,1)S(1)}, bf16[2,320,256]{2,1,0:T(8,128)(2,1)S(1)}, u32[]{:S(2)}, u32[]{:S(2)}) collective-permute-start(bf16[2,320,256]{2,1,0:T(8,128)(2,1)S(1)} %collective-permute-done.5.refs_2_), channel_id=1, source_target_pairs={{0,1},{1,0},{2,3},{3,2},{4,5},{5,4},{6,7},{7,6},{8,9},{9,8},{10,11... | collective-permute-start | bytes 983048 | tf_op jit(solution)/shard_map/ppermute | solution.py:488
  34.7 5.9 %collective-permute-start.7 = (bf16[8,2,64,128]{3,2,1,0:T(8,128)(2,1)S(1)}, bf16[8,2,64,128]{3,2,1,0:T(8,128)(2,1)S(1)}, u32[]{:S(2)}, u32[]{:S(2)}) collective-permute-start(bf16[8,2,64,128]{3,2,1,0:T(8,128)(2,1)S(1)} %get-tuple-element.79), channel_id=1, source_target_pairs={{0,2},{2,4},{4,6},{6,7},{7,5},{5,3},{3,1},{1,0},{8,10},{10,12},{12... | collective-permute-start | bytes 786440 | tf_op jit(solution)/shard_map/ppermute | solution.py:470
  35.1 7.9 %collective-permute-start.8 = (bf16[8,2,64,128]{3,2,1,0:T(8,128)(2,1)S(1)}, bf16[8,2,64,128]{3,2,1,0:T(8,128)(2,1)S(1)}, u32[]{:S(2)}, u32[]{:S(2)}) collective-permute-start(bf16[8,2,64,128]{3,2,1,0:T(8,128)(2,1)S(1)} %get-tuple-element.80), channel_id=1, source_target_pairs={{2,0},{4,2},{6,4},{7,6},{5,7},{3,5},{1,3},{0,1},{10,8},{12,10},{14... | collective-permute-start | bytes 786440 | tf_op jit(solution)/shard_map/ppermute | solution.py:470
  43.1 7.7 %collective-permute-start.13 = (bf16[4,2,64,128]{3,2,1,0:T(8,128)(2,1)S(1)}, bf16[4,2,64,128]{3,2,1,0:T(8,128)(2,1)S(1)}, u32[]{:S(2)}, u32[]{:S(2)}) collective-permute-start(bf16[4,2,64,128]{3,2,1,0:T(8,128)(2,1)S(1)} %pad_maximum_fusion.2), channel_id=1, source_target_pairs={{0,8},{8,16},{16,24},{24,0},{1,9},{9,17},{17,25},{25,1},{2,10},{10... | collective-permute-start | bytes 393224 | tf_op jit(solution)/shard_map/ppermute | solution.py:477
  44.7 10.4 %collective-permute-start.15 = (bf16[1,320,256]{2,1,0:T(8,128)(2,1)S(1)}, bf16[1,320,256]{2,1,0:T(8,128)(2,1)S(1)}, u32[]{:S(2)}, u32[]{:S(2)}) collective-permute-start(bf16[1,320,256]{2,1,0:T(8,128)(2,1)S(1)} %get-tuple-element.91), channel_id=1, source_target_pairs={{0,6},{2,4},{4,2},{6,0},{1,7},{3,5},{5,3},{7,1},{8,14},{10,12},{12... | collective-permute-start | bytes 491528 | tf_op jit(solution)/shard_map/ppermute | solution.py:484
  47.8 5.0 %collective-permute-start.14 = (bf16[4,2,64,128]{3,2,1,0:T(8,128)(2,1)S(1)}, bf16[4,2,64,128]{3,2,1,0:T(8,128)(2,1)S(1)}, u32[]{:S(2)}, u32[]{:S(2)}) collective-permute-start(bf16[4,2,64,128]{3,2,1,0:T(8,128)(2,1)S(1)} %pad_maximum_fusion.3), channel_id=1, source_target_pairs={{8,0},{16,8},{24,16},{0,24},{9,1},{17,9},{25,17},{1,25},{10,2},{18... | collective-permute-start | bytes 393224 | tf_op jit(solution)/shard_map/ppermute | solution.py:478
  55.0 8.0 %collective-permute-start.17 = (bf16[8,2,64,128]{3,2,1,0:T(8,128)(2,1)S(1)}, bf16[8,2,64,128]{3,2,1,0:T(8,128)(2,1)S(1)}, u32[]{:S(2)}, u32[]{:S(2)}) collective-permute-start(bf16[8,2,64,128]{3,2,1,0:T(8,128)(2,1)S(1)} %get-tuple-element.93), channel_id=1, source_target_pairs={{2,0},{4,2},{6,4},{7,6},{5,7},{3,5},{1,3},{0,1},{10,8},{12,10},{14... | collective-permute-start | bytes 786440 | tf_op jit(solution)/shard_map/ppermute | solution.py:470
  55.1 8.0 %collective-permute-start.16 = (bf16[8,2,64,128]{3,2,1,0:T(8,128)(2,1)S(1)}, bf16[8,2,64,128]{3,2,1,0:T(8,128)(2,1)S(1)}, u32[]{:S(2)}, u32[]{:S(2)}) collective-permute-start(bf16[8,2,64,128]{3,2,1,0:T(8,128)(2,1)S(1)} %get-tuple-element.92), channel_id=1, source_target_pairs={{0,2},{2,4},{4,6},{6,7},{7,5},{5,3},{3,1},{1,0},{8,10},{10,12},{12... | collective-permute-start | bytes 786440 | tf_op jit(solution)/shard_map/ppermute | solution.py:470
  63.1 7.2 %collective-permute-start.18 = (bf16[4,2,64,128]{3,2,1,0:T(8,128)(2,1)S(1)}, bf16[4,2,64,128]{3,2,1,0:T(8,128)(2,1)S(1)}, u32[]{:S(2)}, u32[]{:S(2)}) collective-permute-start(bf16[4,2,64,128]{3,2,1,0:T(8,128)(2,1)S(1)} %pad_maximum_fusion.4), channel_id=1, source_target_pairs={{0,8},{8,16},{16,24},{24,0},{1,9},{9,17},{17,25},{25,1},{2,10},{10... | collective-permute-start | bytes 393224 | tf_op jit(solution)/shard_map/ppermute | solution.py:477
  64.0 6.4 %collective-permute-start.20 = (bf16[1,320,256]{2,1,0:T(8,128)(2,1)S(1)}, bf16[1,320,256]{2,1,0:T(8,128)(2,1)S(1)}, u32[]{:S(2)}, u32[]{:S(2)}) collective-permute-start(bf16[1,320,256]{2,1,0:T(8,128)(2,1)S(1)} %collective-permute-done.15.refs_4_), channel_id=1, source_target_pairs={{0,1},{1,0},{2,3},{3,2},{4,5},{5,4},{6,7},{7,6},{8,9},{9,8},{10,11... | collective-permute-start | bytes 491528 | tf_op jit(solution)/shard_map/ppermute | solution.py:488
  64.0 6.4 %collective-permute-start.19 = (bf16[4,2,64,128]{3,2,1,0:T(8,128)(2,1)S(1)}, bf16[4,2,64,128]{3,2,1,0:T(8,128)(2,1)S(1)}, u32[]{:S(2)}, u32[]{:S(2)}) collective-permute-start(bf16[4,2,64,128]{3,2,1,0:T(8,128)(2,1)S(1)} %pad_maximum_fusion.5), channel_id=1, source_target_pairs={{8,0},{16,8},{24,16},{0,24},{9,1},{17,9},{25,17},{1,25},{10,2},{18... | collective-permute-start | bytes 393224 | tf_op jit(solution)/shard_map/ppermute | solution.py:478
  76.0 7.4 %collective-permute-start.21 = (bf16[8,2,64,128]{3,2,1,0:T(8,128)(2,1)S(1)}, bf16[8,2,64,128]{3,2,1,0:T(8,128)(2,1)S(1)}, u32[]{:S(2)}, u32[]{:S(2)}) collective-permute-start(bf16[8,2,64,128]{3,2,1,0:T(8,128)(2,1)S(1)} %get-tuple-element.105), channel_id=1, source_target_pairs={{0,2},{2,4},{4,6},{6,7},{7,5},{5,3},{3,1},{1,0},{8,10},{10,12},{12... | collective-permute-start | bytes 786440 | tf_op jit(solution)/shard_map/ppermute | solution.py:470
  77.8 6.4 %collective-permute-start.22 = (bf16[8,2,64,128]{3,2,1,0:T(8,128)(2,1)S(1)}, bf16[8,2,64,128]{3,2,1,0:T(8,128)(2,1)S(1)}, u32[]{:S(2)}, u32[]{:S(2)}) collective-permute-start(bf16[8,2,64,128]{3,2,1,0:T(8,128)(2,1)S(1)} %get-tuple-element.106), channel_id=1, source_target_pairs={{2,0},{4,2},{6,4},{7,6},{5,7},{3,5},{1,3},{0,1},{10,8},{12,10},{14... | collective-permute-start | bytes 786440 | tf_op jit(solution)/shard_map/ppermute | solution.py:470
  84.2 5.6 %collective-permute-start.23 = (bf16[3,2,64,128]{3,2,1,0:T(8,128)(2,1)S(1)}, bf16[3,2,64,128]{3,2,1,0:T(8,128)(2,1)S(1)}, u32[]{:S(2)}, u32[]{:S(2)}) collective-permute-start(bf16[3,2,64,128]{3,2,1,0:T(8,128)(2,1)S(1)} %pad_maximum_fusion.6), channel_id=1, source_target_pairs={{0,8},{8,16},{16,24},{24,0},{1,9},{9,17},{17,25},{25,1},{2,10},{10... | collective-permute-start | bytes 294920 | tf_op jit(solution)/shard_map/ppermute | solution.py:477
  85.7 4.7 %collective-permute-start.24 = (bf16[3,2,64,128]{3,2,1,0:T(8,128)(2,1)S(1)}, bf16[3,2,64,128]{3,2,1,0:T(8,128)(2,1)S(1)}, u32[]{:S(2)}, u32[]{:S(2)}) collective-permute-start(bf16[3,2,64,128]{3,2,1,0:T(8,128)(2,1)S(1)} %pad_maximum_fusion.7), channel_id=1, source_target_pairs={{8,0},{16,8},{24,16},{0,24},{9,1},{17,9},{25,17},{1,25},{10,2},{18... | collective-permute-start | bytes 294920 | tf_op jit(solution)/shard_map/ppermute | solution.py:478
  (15 other events, 182.4 us)

commit v2 on v1

v2 whole, which is shorter than its diff:
```python
import functools

import jax
import jax.numpy as jnp
from jax import lax
from jax.experimental import pallas as pl
from jax.experimental.pallas import tpu as pltpu
from jax.sharding import PartitionSpec as P

SWEEPS = 2
DAMPING = 0.8
HALF = 32
LANES = 128
WIDE = 256
STEPS = 9
BF16 = jnp.bfloat16
F32 = jnp.float32
LIMIT = 8 * 1024 * 1024


def listed_at(cols_ref, slots, index, groups):
    for group in range(groups):
        codes = [cols_ref[index * groups + group, slot] for slot in range(27)]
        for slot, code in enumerate(codes):
            slots[group, code] = slot


def diagonal(mass, rows, groups):
    row = lax.broadcasted_iota(jnp.int32, (rows, LANES), 0)
    lane = lax.broadcasted_iota(jnp.int32, (rows, LANES), 1)
    spread = jnp.zeros((rows, LANES), F32)
    for group in range(groups):
        spread = jnp.where(row % groups == group, mass[group : group + 1], spread)
    return jnp.where(lane % 64 == 2 * (row // groups) + lane // 64, spread, 0.0)


def fine_sort_kernel(cols_ref, mass_ref, blocks_ref, out_ref, slots, held, arrived):
    second = lax.broadcasted_iota(jnp.int32, (2 * HALF, LANES), 0) % 2 == 1
    columns, parts = out_ref.shape[0], arrived.shape[0]
    each = columns // parts
    copies = [
        pltpu.make_async_copy(blocks_ref.at[pl.ds(part * each, each)], held.at[pl.ds(part * each, each)], arrived.at[part])
        for part in range(parts)
    ]
    for copy in copies:
        copy.start()
    for index in range(columns):
        listed_at(cols_ref, slots.at[index], index, 2)
    for index in range(columns):
        if index % each == 0:
            copies[index // each].wait()
        for step in range(STEPS):
            for side in range(2):
                upper = held[index, slots[index, 0, 3 * step + side + 1]]
                lower = held[index, slots[index, 1, 3 * step + side]]
                span = slice(side * LANES, (side + 1) * LANES)
                out_ref[index, step * 2 * HALF : (step + 1) * 2 * HALF, span] = jnp.where(second, lower, upper)
        mass = mass_ref[index].astype(F32)
        mass = diagonal(jnp.concatenate([mass, mass], axis=1), 2 * HALF, 2)
        for side in range(2):
            span = slice(side * LANES, (side + 1) * LANES)
            out_ref[index, STEPS * 2 * HALF :, span] = jnp.where(second == (side == 1), mass, 0.0).astype(BF16)


def coarse_sort_kernel(cols_ref, mass_ref, smoother_ref, blocks_ref, out_ref, slots, scratch):
    groups = blocks_ref.shape[2] // HALF
    rows = groups * HALF
    kind = lax.broadcasted_iota(jnp.int32, (rows, LANES), 0) % groups

    def hand_out(values, first, span):
        scratch[...] = values
        for y in range(groups):
            out_ref[y, first : first + HALF, span] = scratch[pl.ds(y, HALF, stride=groups), :].astype(BF16)

    listed_at(cols_ref, slots, pl.program_id(0), groups)
    for step in range(STEPS):
        for side in range(2):
            code = 3 * step + side + 1 - lax.axis_index("depth")
            values = blocks_ref[0, slots[0, code]]
            for group in range(1, groups):
                values = jnp.where(kind == group, blocks_ref[0, slots[group, code]], values)
            hand_out(values.astype(F32), step * HALF, slice(side * LANES, (side + 1) * LANES))
    hand_out(smoother_ref[0].astype(F32), STEPS * HALF, slice(0, LANES))
    mass = mass_ref[0].astype(F32)
    mass = diagonal(jnp.concatenate([mass, mass], axis=1), rows, groups)
    hand_out(mass, STEPS * HALF, slice(LANES, WIDE))


def in_hbm(array):
    return pltpu.with_memory_space_constraint(array, pltpu.HBM)


def sort_fine(blocks, cols, mass):
    size_x, size_y, layers = blocks.shape[:3]
    columns = size_x * size_y
    paired = blocks.reshape(size_x, size_y, layers, 27, HALF, LANES).transpose(0, 1, 3, 4, 2, 5)
    rows = (STEPS + 1) * 2 * HALF
    shape = (columns, 27, layers * HALF, LANES)
    return pl.pallas_call(
        fine_sort_kernel,
        in_specs=[SMEM, VMEM, pl.BlockSpec(memory_space=pltpu.HBM)],
        out_specs=VMEM,
        out_shape=jax.ShapeDtypeStruct((columns, rows, WIDE), BF16),
        scratch_shapes=[
            pltpu.SMEM((columns, 2, 27), jnp.int32), pltpu.VMEM(shape, BF16), pltpu.SemaphoreType.DMA((columns // 2,)),
        ],
        compiler_params=pltpu.CompilerParams(vmem_limit_bytes=2 * LIMIT),
        name="sort_fine",
    )(in_hbm(cols.reshape(columns * layers, 27)), in_hbm(mass.reshape(columns, layers, 64)), in_hbm(paired.reshape(shape)))


def sort_coarse(blocks, cols, mass, smoother):
    size_x, size_y = blocks.shape[:2]
    paired = blocks.reshape(size_x, size_y, 27, HALF, LANES).transpose(0, 2, 3, 1, 4)
    smoothers = smoother.reshape(size_x, size_y, HALF, LANES).transpose(0, 2, 1, 3)
    rows = (STEPS + 1) * HALF
    return pl.pallas_call(
        coarse_sort_kernel,
        grid=(size_x,),
        in_specs=[
            SMEM,
            pl.BlockSpec((1, size_y, 64), lambda i: (i, 0, 0)),
            pl.BlockSpec((1, size_y * HALF, LANES), lambda i: (i, 0, 0)),
            pl.BlockSpec((1, 27, size_y * HALF, LANES), lambda i: (i, 0, 0, 0)),
        ],
        out_specs=pl.BlockSpec((size_y, rows, WIDE), lambda i: (i, 0, 0)),
        out_shape=jax.ShapeDtypeStruct((size_x * size_y, rows, WIDE), BF16),
        scratch_shapes=[pltpu.SMEM((size_y, 27), jnp.int32), pltpu.VMEM((size_y * HALF, LANES), F32)],
        compiler_params=pltpu.CompilerParams(vmem_limit_bytes=LIMIT),
        name="sort_coarse",
    )(
        in_hbm(cols.reshape(size_x * size_y, 27)),
        in_hbm(mass.reshape(size_x, size_y, 64)),
        in_hbm(smoothers.reshape(size_x, size_y * HALF, LANES)),
        in_hbm(paired.reshape(size_x, 27, size_y * HALF, LANES)),
    )


def two_sided(block):
    none = jnp.zeros_like(block)
    return jnp.concatenate(
        [jnp.concatenate([block, none], axis=1), jnp.concatenate([none, block], axis=1)], axis=0
    )


def mask_layers(block, kind):
    none = jnp.zeros_like(block)
    return jnp.concatenate([jnp.where(kind == 0, block, none), jnp.where(kind == 1, block, none)], axis=1)


class Fine:
    def __init__(self, ops_ref, size_y):
        self.ops_ref, self.size_y = ops_ref, size_y

    def kind(self):
        return lax.broadcasted_iota(jnp.int32, (2 * HALF, LANES), 0) % 2

    def step(self, x, y, step):
        return self.ops_ref[x * self.size_y + y, step * 2 * HALF : (step + 1) * 2 * HALF, :]

    def mass(self, x, y):
        return self.step(x, y, STEPS)

    def half(self, total, place, z, parity):
        return total[(*place, parity, pl.ds(z, HALF, stride=2), slice(None))]


class Coarse:
    def __init__(self, own_ref, other_ref, size_y):
        self.own_ref, self.other_ref, self.size_y = own_ref, other_ref, size_y

    def kind(self):
        row = lax.broadcasted_iota(jnp.int32, (2 * HALF, LANES), 0)
        return lax.bitwise_xor(row // HALF, lax.axis_index("depth"))

    def step(self, x, y, step):
        place, span = x * self.size_y + y, slice(step * HALF, (step + 1) * HALF)
        return jnp.concatenate([self.own_ref[place, span, :], self.other_ref[place, span, :]], axis=0)

    def smoother(self, x, y):
        return self.step(x, y, STEPS)[:, :LANES]

    def mass(self, x, y):
        return mask_layers(self.step(x, y, STEPS)[:, LANES:], self.kind())

    def half(self, total, place, z, parity):
        first = pl.multiple_of(lax.bitwise_xor(jnp.int32(z), lax.axis_index("depth")) * HALF, HALF)
        return total[(*place, parity, pl.ds(first, HALF), slice(None))]


def both_layers(cells):
    return jnp.concatenate([two_sided(cells[0]), two_sided(cells[1])], axis=0)


def tip(ref, end):
    return ref.at[end * (ref.shape[0] - 1)]


def add_from(total_ref, rows, cells, targets, slot=lambda x: x):
    left = [rows.step(*target) for target in targets]
    given = jnp.dot(jnp.concatenate(left, axis=0), both_layers(cells), preferred_element_type=F32)
    parts = [given[index * 2 * HALF : (index + 1) * 2 * HALF] for index in range(len(left))]
    for (x, y, _), part in zip(targets, parts):
        for parity in range(2):
            total_ref[slot(x), y, parity] += part[:, parity * LANES : (parity + 1) * LANES]


def natural(rows, total, places, scratches):
    for place, scratch in zip(places, scratches):
        for z in range(2):
            for parity in range(2):
                scratch[z, pl.ds(parity, HALF, stride=2), :] = rows.half(total, place, z, parity)
    return [[scratch[z] for z in range(2)] for scratch in scratches]


def smoothed(rows, lefts, columns, total, places, scratches):
    given = [
        jnp.dot(left, both_layers([cell.astype(BF16) for cell in cells]), preferred_element_type=F32)
        for left, cells in zip(lefts, columns)
    ]
    for part, place in zip(given, places):
        for parity in range(2):
            total[(*place, parity)] = part[:, parity * LANES : (parity + 1) * LANES]
    return natural(rows, total, places, scratches)


def over_columns(size_x, column):
    if size_x == 1:
        column(0, (0,))
        return
    column(0, (-1, 0))
    for x in range(1, size_x - 1):
        column(x, (-1, 0, 1))
    column(size_x - 1, (0, 1))


def inner_kernel(cells_ref, ends_ref, *refs, grid):
    *ops, total_ref = refs
    size_x, size_y = cells_ref.shape[:2]
    rows = grid(*ops, size_y)
    total_ref[...] = jnp.zeros_like(total_ref)

    def column(x, shifts):
        row = tip(ends_ref, min(x, 1)) if x in (0, size_x - 1) else cells_ref.at[x]
        sums = {}
        for near in range(size_y):
            targets = [(shift, y) for shift in shifts for y in range(size_y) if abs(near - y) <= 1]
            left = [rows.step(x - shift, y, (shift + 1) * 3 + near - y + 1) for shift, y in targets]
            left.append(rows.mass(x, near))
            given = jnp.dot(jnp.concatenate(left, axis=0), both_layers(row[near]), preferred_element_type=F32)
            for index, target in enumerate(targets + [(0, near)]):
                part = given[index * 2 * HALF : (index + 1) * 2 * HALF]
                sums[target] = sums[target] + part if target in sums else part
        for (shift, y), part in sums.items():
            for parity in range(2):
                total_ref[x - shift, y, parity] += part[:, parity * LANES : (parity + 1) * LANES]

    over_columns(size_x, column)


def inside_track(cells, low):
    at = lax.axis_index("lateral")
    inside = at > 0 if low else at < lax.axis_size("lateral") - 1
    return jnp.where(inside, cells, jnp.zeros_like(cells))


def add_sides(one_ref, two_ref, rows, total):
    size_x, size_y = total.shape[:2]

    def both(low_ref, high_ref):
        def column(x, shifts):
            for cells, y, step in (
                (inside_track(low_ref[x], True), 0, 0),
                (inside_track(high_ref[x], False), size_y - 1, 2),
            ):
                add_from(total, rows, cells, [(x - shift, y, (shift + 1) * 3 + step) for shift in shifts])

        over_columns(size_x, column)

    odd = lax.axis_index("depth") % 2
    pl.when(odd == 0)(lambda: both(one_ref, two_ref))
    pl.when(odd == 1)(lambda: both(two_ref, one_ref))


def give_faces(low, high, one_ref, two_ref, x):
    even = lax.axis_index("depth") % 2 == 0
    for z in range(2):
        one_ref[x, z] = jnp.where(even, high[z], low[z])
        two_ref[x, z] = jnp.where(even, low[z], high[z])


def give_all_faces(cells_ref, ends_ref, one_ref, two_ref):
    size_x, size_y = cells_ref.shape[:2]

    for x in range(1, size_x - 1):
        give_faces(cells_ref.at[x, 0], cells_ref.at[x, size_y - 1], one_ref, two_ref, x)
    for end in range(2):
        ends = tip(ends_ref, end)
        give_faces(ends.at[0], ends.at[size_y - 1], one_ref, two_ref, end * (size_x - 1))


def round_kernel(start_ref, round_ref, one_ref, two_ref):
    for x in range(start_ref.shape[0]):
        cells = [[start_ref[x, y, z].astype(BF16) for z in range(2)] for y in range(start_ref.shape[1])]
        for y, column in enumerate(cells):
            for z in range(2):
                round_ref[x, y, z] = column[z]
        give_faces(cells[0], cells[-1], one_ref, two_ref, x)


def round_start(start):
    size_x, size_y, layers, width, loads = start.shape
    batch = size_x // 4
    side = pl.BlockSpec((batch, layers, width, loads), lambda i: (i, 0, 0, 0))
    whole = pl.BlockSpec((batch, size_y, layers, width, loads), lambda i: (i, 0, 0, 0, 0))
    face = jax.ShapeDtypeStruct((size_x, layers, width, loads), BF16)
    return pl.pallas_call(
        round_kernel,
        grid=(4,),
        in_specs=[whole],
        out_specs=[whole, side, side],
        out_shape=[jax.ShapeDtypeStruct(start.shape, BF16), face, face],
        compiler_params=pltpu.CompilerParams(vmem_limit_bytes=LIMIT),
        name="round_start",
    )(in_hbm(start))


def add_ends(given_refs, rows, total, size_x):
    size_y = total.shape[1]
    odd = lax.axis_index("depth") % 2
    at, count = lax.axis_index("track"), lax.axis_size("track")
    for near in range(-1, size_y + 1):
        ys = [y for y in range(size_y) if abs(near - y) <= 1]
        corner = near in (-1, size_y)
        place = (odd if near < 0 else 1 - odd) if corner else near
        for end, inside in ((0, at > 0), (1, at < count - 1)):
            cells = given_refs[2 * corner + end][place]
            cells = jnp.where(inside, cells, jnp.zeros_like(cells))
            if corner:
                cells = inside_track(cells, near < 0)
            targets = [(end * (size_x - 1), y, 6 * end + near - y + 1) for y in ys]
            add_from(total, rows, cells, targets, slot=lambda x, end=end: end)


def add_coarse_ends(before_ref, after_ref, rows, total):
    size_x, size_y = total.shape[:2]
    at = lax.axis_index(("track", "lateral"))
    count = lax.axis_size(("track", "lateral"))
    for near in range(size_y):
        ys = [y for y in range(size_y) if abs(near - y) <= 1]
        for end, ref, inside in ((0, before_ref, at > 0), (1, after_ref, at < count - 1)):
            cells = ref[near]
            cells = jnp.where(inside, cells, jnp.zeros_like(cells))
            add_from(total, rows, cells, [(end * (size_x - 1), y, 6 * end + near - y + 1) for y in ys])


def over_inside(size_x, body):
    for x in range(1, size_x - 1):
        body(x)


def smooth_columns(rows, total, places, smoothers, rhs, old, scratch):
    first = [scratch.at[index, 0] for index in range(len(places))]
    second = [scratch.at[index, 1] for index in range(len(places))]
    applied = natural(rows, total, places, first)
    residuals = [[ref[z] - part[z] for z in range(2)] for ref, part in zip(rhs, applied)]
    lefts = [mask_layers(smoother, rows.kind()) for smoother in smoothers]
    changes = smoothed(rows, lefts, residuals, total, places, second)
    return [[ref[z] + DAMPING * part[z] for z in range(2)] for ref, part in zip(old, changes)]


def keep_ends(total, end_total_ref):
    for end in range(2):
        end_total_ref[end] = tip(total, end)[...]


def smooth_inside_kernel(
    one_ref, two_ref, ops_ref, smoother_ref, given_ref, rhs_ref, old_ref, end_total_ref, new_ref, round_ref, total, scratch
):
    size_x, size_y = total.shape[:2]
    rows = Fine(ops_ref, size_y)
    total[...] = given_ref[...]
    add_sides(one_ref, two_ref, rows, total)
    keep_ends(total, end_total_ref)

    def body(x):
        ys = range(size_y)
        values = smooth_columns(
            rows, total, [(x, y) for y in ys], [smoother_ref[x * size_y + y] for y in ys],
            [rhs_ref.at[x, y] for y in ys], [old_ref.at[x, y] for y in ys], scratch,
        )
        for y in ys:
            for z in range(2):
                new_ref[x, y, z] = values[y][z]
                round_ref[x, y, z] = values[y][z].astype(BF16)

    over_inside(size_x, body)


def smooth_ends_kernel(
    before_ref, after_ref, corner_before_ref, corner_after_ref, ops_ref, smoother_ref, given_ref, rhs_ref, old_ref, cells_ref,
    new_ref, round_ref, one_ref, two_ref, total, scratch,
):
    size_x, size_y = cells_ref.shape[:2]
    rows = Fine(ops_ref, size_y)
    total[...] = given_ref[...]
    add_ends([before_ref, after_ref, corner_before_ref, corner_after_ref], rows, total, size_x)

    places = [(end, y) for end in range(2) for y in range(size_y)]
    row = lambda end: end * (size_x - 1)
    values = smooth_columns(
        rows, total, places, [smoother_ref[row(end) * size_y + y] for end, y in places],
        [rhs_ref.at[row(end), y] for end, y in places], [tip(old_ref, end).at[y] for end, y in places], scratch,
    )
    for (end, y), value in zip(places, values):
        for z in range(2):
            new_ref[end, y, z] = value[z]
            round_ref[end, y, z] = value[z].astype(BF16)
    give_all_faces(cells_ref, round_ref, one_ref, two_ref)


def restrict_columns(rows, total, places, transfers, rhs, group_ref, xs, coarse_ref, scratch):
    size_x = coarse_ref.shape[0]
    first = [scratch.at[index, 0] for index in range(len(places))]
    applied = natural(rows, total, places, first)
    for index, place in enumerate(places):
        for z in range(2):
            scratch[index, 1, z] = rhs[index][z] - applied[index][z]
    for index, place in enumerate(places):
        for z in range(2):
            for parity in range(2):
                taken = scratch[index, 1, z, pl.ds(parity, HALF, stride=2), :]
                total[(*place, parity, pl.ds(z, HALF, stride=2), slice(None))] = taken
    given = []
    for place, transfer in zip(places, transfers):
        left = mask_layers(transfer, rows.kind())
        right = jnp.concatenate([total[(*place, 0)], total[(*place, 1)]], axis=1).astype(BF16)
        given.append(lax.dot_general(left, right, (((0,), (0,)), ((), ())), preferred_element_type=F32))
    for (_, y), x, both in zip(places, xs, given):
        for z in range(2):
            target = group_ref[y, z, x] - lax.axis_index("track") * size_x
            own = both[z * LANES : (z + 1) * LANES]
            coarse_ref[target, y // 2, z] += own[:64, :LANES] + own[64:, LANES:]


def restrict_inside_kernel(
    group_ref, one_ref, two_ref, ops_ref, transfer_ref, given_ref, rhs_ref, end_total_ref, coarse_ref, total, scratch
):
    size_x, size_y = total.shape[:2]
    rows = Fine(ops_ref, size_y)
    total[...] = given_ref[...]
    coarse_ref[...] = jnp.zeros_like(coarse_ref)
    add_sides(one_ref, two_ref, rows, total)
    keep_ends(total, end_total_ref)

    def body(x):
        ys = range(size_y)
        restrict_columns(
            rows, total, [(x, y) for y in ys], [transfer_ref[x * size_y + y] for y in ys],
            [rhs_ref.at[x, y] for y in ys], group_ref, [x] * size_y, coarse_ref, scratch,
        )

    over_inside(size_x, body)


def restrict_ends_kernel(
    group_ref, before_ref, after_ref, corner_before_ref, corner_after_ref, ops_ref, transfer_ref, given_ref, rhs_ref,
    part_ref, *refs
):
    pieces, (coarse_ref, total, scratch) = refs[:-3], refs[-3:]
    size_x, size_y = rhs_ref.shape[:2]
    rows = Fine(ops_ref, size_y)
    total[...] = given_ref[...]
    coarse_ref[...] = part_ref[...]
    add_ends([before_ref, after_ref, corner_before_ref, corner_after_ref], rows, total, size_x)

    places = [(end, y) for end in range(2) for y in range(size_y)]
    xs = [end * (size_x - 1) for end, _ in places]
    restrict_columns(
        rows, total, places, [transfer_ref[x * size_y + y] for x, (_, y) in zip(xs, places)],
        [rhs_ref.at[x, y] for x, (_, y) in zip(xs, places)], group_ref, xs, coarse_ref, scratch,
    )
    for step, piece in enumerate(pieces):
        first = lax.bitwise_xor(lax.axis_index("lateral"), step) * piece.shape[0]
        for x in range(piece.shape[0]):
            piece[x] = coarse_ref[first + x].astype(BF16)


def placed(pieces):
    found = []
    for step, piece in enumerate(pieces):
        first = lax.bitwise_xor(lax.axis_index("lateral"), step) * piece.shape[1]
        found += [(x, first + y, piece.at[x, y]) for x in range(piece.shape[0]) for y in range(piece.shape[1])]
    return found


def first_kernel(own_ref, other_ref, *refs):
    pieces, (coarse_ref, first_ref, round_ref, total, scratch) = refs[:-5], refs[-5:]
    rows = Coarse(own_ref, other_ref, coarse_ref.shape[1])
    columns = placed(pieces)
    cells = [[piece[z] for z in range(2)] for _, _, piece in columns]
    lefts = [mask_layers(rows.smoother(x, y), rows.kind()) for x, y, _ in columns]
    places = [(index,) for index in range(len(columns))]
    changes = smoothed(rows, lefts, cells, total, places, [scratch.at[index] for index in range(len(columns))])
    for (x, y, _), cell, change in zip(columns, cells, changes):
        for z in range(2):
            value = DAMPING * change[z]
            coarse_ref[x, y, z] = cell[z]
            first_ref[x, y, z] = value
            round_ref[x, y, z] = value.astype(BF16)


def second_kernel(before_ref, after_ref, own_ref, other_ref, given_ref, coarse_ref, first_ref, *refs):
    pieces, (total, scratch) = refs[:-2], refs[-2:]
    rows = Coarse(own_ref, other_ref, total.shape[1])
    total[...] = given_ref[...]
    add_coarse_ends(before_ref, after_ref, rows, total)
    columns = placed(pieces)
    values = smooth_columns(
        rows, total, [(x, y) for x, y, _ in columns], [rows.smoother(x, y) for x, y, _ in columns],
        [[coarse_ref[x, y, z].astype(F32) for z in range(2)] for x, y, _ in columns],
        [first_ref.at[x, y] for x, y, _ in columns], scratch,
    )
    for (_, _, piece), value in zip(columns, values):
        for z in range(2):
            piece[z] = value[z].astype(BF16)


def prolong_kernel(group_ref, transfer_ref, iterate_ref, ends_ref, *refs):
    pieces, (out_ref, correction, total, scratch, made, sent) = refs[:-6], refs[-6:]
    size_x, size_y = out_ref.shape[:2]
    for step, piece in enumerate(pieces):
        first = lax.bitwise_xor(lax.axis_index("lateral"), step) * piece.shape[0]
        for x in range(piece.shape[0]):
            correction[first + x] = piece[x]
    rows = Fine(None, size_y)

    def send(x):
        return pltpu.make_async_copy(made.at[x], out_ref.at[x], sent.at[x])

    def added(x, iterate):
        ys = range(size_y)
        source = lambda y, z: group_ref[y, z, x] - lax.axis_index("track") * size_x
        cells = [[correction[source(y, z), y // 2, z] for z in range(2)] for y in ys]
        lefts = [mask_layers(transfer_ref[x * size_y + y], rows.kind()) for y in ys]
        changes = smoothed(rows, lefts, cells, total, [(y,) for y in ys], [scratch.at[y, 0] for y in ys])
        for y in ys:
            for z in range(2):
                made[x, y, z] = iterate[y, z] + changes[y][z]
        send(x).start()

    for end in range(2):
        added(end * (size_x - 1), tip(ends_ref, end))
    over_inside(size_x, lambda x: added(x, iterate_ref.at[x]))
    for x in range(size_x):
        send(x).wait()


SMEM = pl.BlockSpec(memory_space=pltpu.SMEM)
VMEM = pl.BlockSpec(memory_space=pltpu.VMEM)


def call(kernel, name, scalars, operands, out_shape, scratch=(), out_space=pltpu.VMEM):
    return pl.pallas_call(
        kernel,
        in_specs=[SMEM] * len(scalars) + [VMEM] * len(operands),
        out_specs=jax.tree.map(lambda _: pl.BlockSpec(memory_space=out_space), out_shape),
        out_shape=out_shape,
        scratch_shapes=list(scratch),
        compiler_params=pltpu.CompilerParams(vmem_limit_bytes=LIMIT),
        name=name,
    )(*scalars, *operands)


def swap_sides(one, two):
    lateral, depth = lax.axis_size("lateral"), lax.axis_size("depth")
    ring = [i * depth for i in range(lateral)] + [i * depth + 1 for i in reversed(range(lateral))]
    onward = list(zip(ring, ring[1:] + ring[:1]))
    back = [(b, a) for a, b in onward]
    return lax.ppermute(one, ("lateral", "depth"), onward), lax.ppermute(two, ("lateral", "depth"), back)


def swap_ends(last, first):
    count = lax.axis_size("track")
    before = lax.ppermute(last, "track", [(i, (i + 1) % count) for i in range(count)])
    after = lax.ppermute(first, "track", [((i + 1) % count, i) for i in range(count)])
    return before, after


def swap_corners(one, two):
    return swap_ends(jnp.concatenate([one[-1:], two[-1:]], axis=0), jnp.concatenate([one[:1], two[:1]], axis=0))


def swap_pieces(pieces):
    count = len(pieces)
    moved = [lax.ppermute(pieces[step], "lateral", [(i, i ^ step) for i in range(count)]) for step in range(count - 1, 0, -1)]
    return [pieces[0]] + moved[::-1]


def swap_coarse_ends(cells):
    axes = ("track", "lateral")
    count = lax.axis_size(axes)
    before = lax.ppermute(cells[-1], axes, [(i, (i + 1) % count) for i in range(count)])
    after = lax.ppermute(cells[0], axes, [((i + 1) % count, i) for i in range(count)])
    return before, after


def per_device(
    rhs,
    start,
    fine_blocks,
    fine_cols,
    fine_mass,
    fine_smoother,
    transfer,
    aggregate,
    coarse_blocks,
    coarse_cols,
    coarse_mass,
    coarse_smoother,
):
    size_x, size_y, size_z, width, loads = rhs.shape
    count = lax.axis_size("lateral")
    groups = in_hbm(aggregate.transpose(1, 2, 0))
    part_x, all_y = coarse_blocks.shape[:2]
    coarse_y = size_y // 2

    paired = lambda a: a.reshape(size_x, size_y, size_z, HALF, LANES).transpose(0, 1, 3, 2, 4).reshape(-1, 2 * HALF, LANES)
    smoothers, transfers = paired(fine_smoother), paired(transfer)
    field = (size_x, size_y, size_z, width, loads)
    coarse_field = (size_x, coarse_y, size_z, width, loads)
    solve_field = (part_x, all_y, size_z, width, loads)
    sums = lambda shape: shape[:2] + (2, 2 * HALF, LANES)
    full = jax.ShapeDtypeStruct
    two_ends = lambda shape: (2,) + shape[1:]
    scratch = pltpu.VMEM((2 * size_y, 2, 2, width, loads), F32)
    whole, ends = pltpu.VMEM(sums(field), F32), pltpu.VMEM(two_ends(sums(field)), F32)
    face = full((size_x, size_z, width, loads), BF16)

    def inner_of(cells, tips, ops, grid):
        shape = full(sums(cells.shape), F32)
        return call(functools.partial(inner_kernel, grid=grid), "inner", [], [cells, tips, *ops], shape)

    rounded, one, two = round_start(start)
    tips, old, old_tips = rounded, start, start
    fine_cols, one, two = lax.optimization_barrier((fine_cols, one, two))
    one, two = swap_sides(one, two)
    fine_ops = sort_fine(fine_blocks, fine_cols, fine_mass)
    for sweep in range(SWEEPS + 1):
        inner = inner_of(rounded, tips, [fine_ops], Fine)
        inner, tips = lax.optimization_barrier((inner, tips))
        near = swap_ends(tips[-1], tips[0])
        if sweep == 1:
            coarse_cols, inner = lax.optimization_barrier((coarse_cols, inner))
            own_ops = sort_coarse(coarse_blocks, coarse_cols, coarse_mass, coarse_smoother)
            inner, one, two, own_ops = lax.optimization_barrier((inner, one, two, own_ops))
            other_ops = lax.ppermute(own_ops, "depth", [(0, 1), (1, 0)])
        else:
            inner, one, two = lax.optimization_barrier((inner, one, two))
        around = [*near, *swap_corners(one, two)]
        if sweep == SWEEPS:
            break
        end_total, new, rounded = call(
            smooth_inside_kernel, "smooth_inside", [], [one, two, fine_ops, smoothers, inner, rhs, old],
            [full(two_ends(sums(field)), F32), full(field, F32), full(field, BF16)], [whole, scratch],
        )
        new_tips, tips, one, two = call(
            smooth_ends_kernel, "smooth_ends", [], [*around, fine_ops, smoothers, end_total, rhs, old_tips, rounded],
            [full(two_ends(field), F32), full(two_ends(field), BF16), face, face], [ends, scratch],
        )
        old, old_tips = new, new_tips
        one, two = swap_sides(one, two)
    end_total, coarse_part = call(
        restrict_inside_kernel, "restrict_inside", [groups], [one, two, fine_ops, transfers, inner, rhs],
        [full(two_ends(sums(field)), F32), full(coarse_field, F32)], [whole, scratch],
    )
    piece = full((part_x,) + coarse_field[1:], BF16)
    pieces = call(
        restrict_ends_kernel, "restrict_ends", [groups],
        [*around, fine_ops, transfers, end_total, rhs, coarse_part], [piece] * count,
        [pltpu.VMEM(coarse_field, F32), ends, scratch],
    )
    line = pltpu.VMEM((part_x * all_y, 2, 2, width, loads), F32)
    coarse_ops = [own_ops, other_ops]
    coarse_res, first, rounded = call(
        first_kernel, "first", [], coarse_ops + swap_pieces(pieces),
        [full(solve_field, BF16), full(solve_field, F32), full(solve_field, BF16)],
        [
            pltpu.VMEM((part_x * all_y, 2, 2 * HALF, LANES), F32),
            pltpu.VMEM((part_x * all_y, 2, width, loads), F32),
        ],
    )
    before, after = swap_coarse_ends(rounded)
    inner = inner_of(rounded, rounded, coarse_ops, Coarse)
    pieces = call(
        second_kernel, "second", [], [before, after, *coarse_ops, inner, coarse_res, first], [piece] * count,
        [pltpu.VMEM(sums(solve_field), F32), line],
    )
    return call(
        prolong_kernel, "prolong", [groups], [transfers, old, old_tips] + swap_pieces(pieces), full(field, F32),
        [
            pltpu.VMEM(coarse_field, BF16), pltpu.VMEM((size_y, 2, 2 * HALF, LANES), F32), scratch,
            pltpu.VMEM(field, F32), pltpu.SemaphoreType.DMA((size_x,)),
        ],
        out_space=pltpu.HBM,
    )


def solution(mesh):
    in_specs = (
        P("track", "lateral", None, None, "depth"),
        P("track", "lateral", None, None, "depth"),
        P("track", "lateral", None, None, None),
        P("track", "lateral", None, None),
        P("track", "lateral", None, None),
        P("track", "lateral", None, None),
        P("track", "lateral", None, None),
        P("track", "lateral", None),
        P(("track", "lateral"), None, "depth", None, None),
        P(("track", "lateral"), None, "depth", None),
        P(("track", "lateral"), None, "depth", None),
        P(("track", "lateral"), None, "depth", None),
    )
    out_specs = P("track", "lateral", None, None, "depth")
    return jax.shard_map(
        per_device, mesh=mesh, in_specs=in_specs, out_specs=out_specs, check_vma=False
    )
```

time: 95.6 us -> 84.4 us (0.88)
  Pallas kernels: 40.5 us -> 23.5 us
  starting transfers between devices: 28 us -> 34 us
    pallas_call x13 -> x14, Pallas kernels: 35.4 us -> 18.4 us  [the longest x13 14 us: call(): pl.pallas_call(kernel, in_specs=[SMEM] * len(scalars) + [VMEM] * len(oper...]
    ppermute x9, waiting for transfers between devices: 2.31 us -> 16.9 us  [the longest x6 9.15 us: swap_pieces(): lax.ppermute(pieces[step], 'lateral', [(i, i ^ step) for i in range(count)])]
    ppermute x4 -> x3, waiting for transfers between devices: 6.73 us -> 1.23 us  [swap_sides(): lax.ppermute(two, ('lateral', 'depth'), back)]
    ppermute x4 -> x3, waiting for transfers between devices: 6.84 us -> 1.69 us  [swap_sides(): lax.ppermute(one, ('lateral', 'depth'), onward)]
    ppermute x4 -> x6, starting transfers between devices: 6.67 us -> 9.75 us  [swap_ends(): lax.ppermute(first, 'track', [((i + 1) % count, i) for i in range(count)])]
    ppermute x9, starting transfers between devices: 8.83 us -> 11 us  [the longest x6 8.89 us: swap_pieces(): lax.ppermute(pieces[step], 'lateral', [(i, i ^ step) for i in range(count)])]
    ppermute x4 -> x6, waiting for transfers between devices: 4.14 us -> 2.49 us  [swap_ends(): lax.ppermute(first, 'track', [((i + 1) % count, i) for i in range(count)])]
    ppermute x4 -> x6, waiting for transfers between devices: 5.32 us -> 3.69 us  [swap_ends(): lax.ppermute(last, 'track', [(i, (i + 1) % count) for i in range(count)])]
  transfers between devices with their start and end apart: 25 -> 27, of which waited for: 14 -> 16; matrix products, arithmetic and copies ran while one was open for 0% -> 0% of each run, Pallas kernels for 30% -> 21%
where the time goes in v2:
time: 84.4 us; the launch traced here: 84.1 us
  starting transfers between devices  34 us (40%)
  waiting for transfers between devices  26 us (31%)
  Pallas kernels  23.5 us (28%)
    pallas_call x13, Pallas kernels, call(): pl.pallas_call(kernel, in_specs=[SMEM] * len(scalars) + [VMEM] * len(oper...  14 us
    ppermute x6, starting transfers between devices, swap_ends(): lax.ppermute(first, 'track', [((i + 1) % count, i) for i in range(count)])  9.75 us
    ppermute x6, waiting for transfers between devices, swap_pieces(): lax.ppermute(pieces[step], 'lateral', [(i, i ^ step) for i in range(count)])  9.15 us
    ppermute x6, starting transfers between devices, swap_pieces(): lax.ppermute(pieces[step], 'lateral', [(i, i ^ step) for i in range(count)])  8.89 us
    ppermute x3, starting transfers between devices, swap_sides(): lax.ppermute(one, ('lateral', 'depth'), onward)  6.75 us
    ppermute x6, starting transfers between devices, swap_ends(): lax.ppermute(last, 'track', [(i, (i + 1) % count) for i in range(count)])  6.49 us
    pallas_call x1, Pallas kernels, sort_fine(): pl.pallas_call(fine_sort_kernel, in_specs=[SMEM, VMEM, pl.BlockSpec(memor...  4.38 us
    ppermute x1, waiting for transfers between devices, swap_coarse_ends(): lax.ppermute(cells[-1], axes, [(i, (i + 1) % count) for i in range(count)])  4.08 us
  transfers between devices with their start and end apart: 27, of which 16 were waited for; matrix products, arithmetic and copies ran while one was open for 0% of the time, Pallas kernels for 21%

profile of v2, /device:TPU:0, one launch (start us, length us, event | category | flops | bytes accessed | tf_op | source)
XLA Modules:
  0.0 84.1 jit_solution(15172784358260085662)
XLA Ops:
  0.0 2.1 %round_start.1 = (bf16[8,2,2,64,128]{4,3,2,1,0:T(8,128)(2,1)S(1)}, bf16[8,2,64,128]{3,2,1,0:T(8,128)(2,1)S(1)}, bf16[8,2,64,128]{3,2,1,0:T(8,128)(2,1)S(1)}) custom-call(f32[8,2,2,64,128]{4,3,2,1,0:T(8,128)} %old_ref.3), custom_call_target="tpu_custom_call" | custom-call | tf_op jit(solution)/shard_map/round_start/pallas_call | solution.py:317
  2.1 3.0 %collective-permute-start = (bf16[8,2,64,128]{3,2,1,0:T(8,128)(2,1)S(1)}, bf16[8,2,64,128]{3,2,1,0:T(8,128)(2,1)S(1)}, u32[]{:S(2)}, u32[]{:S(2)}) collective-permute-start(bf16[8,2,64,128]{3,2,1,0:T(8,128)(2,1)S(1)} %get-tuple-element.61), channel_id=1, source_target_pairs={{0,2},{2,4},{4,6},{6,7},{7,5},{5,3},{3,1},{1,0},{8,10},{10,12},{12... | collective-permute-start | bytes 786440 | tf_op jit(solution)/shard_map/ppermute | solution.py:580
  5.1 4.4 %sort_fine.1.refs_0_.ops_ref = bf16[16,640,256]{2,1,0:T(8,128)(2,1)S(1)} custom-call(s32[32,27]{1,0:T(8,128)} %bitcast.59, bf16[16,2,64]{2,1,0:T(2,128)(2,1)} %bitcast.60, bf16[16,27,64,128]{3,2,1,0:T(8,128)(2,1)} %bitcast.53), custom_call_target="tpu_custom_call" | custom-call | tf_op jit(solution)/shard_map/sort_fine/pallas_call | solution.py:99
  10.6 2.5 %collective-permute-start.3 = (bf16[2,2,64,128]{3,2,1,0:T(8,128)(2,1)S(1)}, bf16[2,2,64,128]{3,2,1,0:T(8,128)(2,1)S(1)}, u32[]{:S(2)}, u32[]{:S(2)}) collective-permute-start(bf16[2,2,64,128]{3,2,1,0:T(8,128)(2,1)S(1)} %get-tuple-element.107), channel_id=1, source_target_pairs={{8,0},{16,8},{24,16},{0,24},{9,1},{17,9},{25,17},{1,25},{10,2},{18... | collective-permute-start | bytes 196616 | tf_op jit(solution)/shard_map/ppermute | solution.py:586
  13.2 2.0 %collective-permute-start.4 = (bf16[2,2,64,128]{3,2,1,0:T(8,128)(2,1)S(1)}, bf16[2,2,64,128]{3,2,1,0:T(8,128)(2,1)S(1)}, u32[]{:S(2)}, u32[]{:S(2)}) collective-permute-start(bf16[2,2,64,128]{3,2,1,0:T(8,128)(2,1)S(1)} %pad_maximum_fusion), channel_id=1, source_target_pairs={{0,8},{8,16},{16,24},{24,0},{1,9},{9,17},{17,25},{25,1},{2,10},{10... | collective-permute-start | bytes 196616 | tf_op jit(solution)/shard_map/ppermute | solution.py:585
  20.4 1.8 %collective-permute-start.6 = (bf16[8,2,64,128]{3,2,1,0:T(8,128)(2,1)S(1)}, bf16[8,2,64,128]{3,2,1,0:T(8,128)(2,1)S(1)}, u32[]{:S(2)}, u32[]{:S(2)}) collective-permute-start(bf16[8,2,64,128]{3,2,1,0:T(8,128)(2,1)S(1)} %get-tuple-element.72), channel_id=1, source_target_pairs={{0,2},{2,4},{4,6},{6,7},{7,5},{5,3},{3,1},{1,0},{8,10},{10,12},{12... | collective-permute-start | bytes 786440 | tf_op jit(solution)/shard_map/ppermute | solution.py:580
  23.3 2.1 %collective-permute-start.9 = (bf16[2,2,64,128]{3,2,1,0:T(8,128)(2,1)S(1)}, bf16[2,2,64,128]{3,2,1,0:T(8,128)(2,1)S(1)}, u32[]{:S(2)}, u32[]{:S(2)}) collective-permute-start(bf16[2,2,64,128]{3,2,1,0:T(8,128)(2,1)S(1)} %get-tuple-element.125), channel_id=1, source_target_pairs={{8,0},{16,8},{24,16},{0,24},{9,1},{17,9},{25,17},{1,25},{10,2},{18... | collective-permute-start | bytes 196616 | tf_op jit(solution)/shard_map/ppermute | solution.py:586
  25.5 3.0 %sort_coarse.1.own_ref.refs_0_ = bf16[8,320,256]{2,1,0:T(8,128)(2,1)S(1)} custom-call(s32[8,27]{1,0:T(8,128)} %bitcast.61, bf16[2,4,64]{2,1,0:T(4,128)(2,1)} %bitcast.62, bf16[2,128,128]{2,1,0:T(8,128)(2,1)} %bitcast.55, bf16[2,27,128,128]{3,2,1,0:T(8,128)(2,1)} %bitcast.54), custom_call_target="tpu_custom_call" | custom-call | tf_op jit(solution)/shard_map/sort_coarse/pallas_call | solution.py:117
  28.7 2.4 %collective-permute-start.10 = (bf16[2,2,64,128]{3,2,1,0:T(8,128)(2,1)S(1)}, bf16[2,2,64,128]{3,2,1,0:T(8,128)(2,1)S(1)}, u32[]{:S(2)}, u32[]{:S(2)}) collective-permute-start(bf16[2,2,64,128]{3,2,1,0:T(8,128)(2,1)S(1)} %pad_maximum_fusion.2), channel_id=1, source_target_pairs={{0,8},{8,16},{16,24},{24,0},{1,9},{9,17},{17,25},{25,1},{2,10},{10... | collective-permute-start | bytes 196616 | tf_op jit(solution)/shard_map/ppermute | solution.py:585
  36.2 1.9 %collective-permute-start.15 = (bf16[8,2,64,128]{3,2,1,0:T(8,128)(2,1)S(1)}, bf16[8,2,64,128]{3,2,1,0:T(8,128)(2,1)S(1)}, u32[]{:S(2)}, u32[]{:S(2)}) collective-permute-start(bf16[8,2,64,128]{3,2,1,0:T(8,128)(2,1)S(1)} %get-tuple-element.89), channel_id=1, source_target_pairs={{0,2},{2,4},{4,6},{6,7},{7,5},{5,3},{3,1},{1,0},{8,10},{10,12},{12... | collective-permute-start | bytes 786440 | tf_op jit(solution)/shard_map/ppermute | solution.py:580
  39.2 2.5 %collective-permute-start.14 = (bf16[2,2,64,128]{3,2,1,0:T(8,128)(2,1)S(1)}, bf16[2,2,64,128]{3,2,1,0:T(8,128)(2,1)S(1)}, u32[]{:S(2)}, u32[]{:S(2)}) collective-permute-start(bf16[2,2,64,128]{3,2,1,0:T(8,128)(2,1)S(1)} %get-tuple-element.123), channel_id=1, source_target_pairs={{8,0},{16,8},{24,16},{0,24},{9,1},{17,9},{25,17},{1,25},{10,2},{18... | collective-permute-start | bytes 196616 | tf_op jit(solution)/shard_map/ppermute | solution.py:586
  41.7 1.7 %collective-permute-done.15.one_ref = bf16[8,2,64,128]{3,2,1,0:T(8,128)(2,1)S(1)} collective-permute-done((bf16[8,2,64,128]{3,2,1,0:T(8,128)(2,1)S(1)}, bf16[8,2,64,128]{3,2,1,0:T(8,128)(2,1)S(1)}, u32[]{:S(2)}, u32[]{:S(2)}) %collective-permute-start.15) | collective-permute-done | bytes 262176 | tf_op jit(solution)/shard_map/ppermute | solution.py:580
  44.5 2.1 %collective-permute-start.17 = (bf16[2,2,64,128]{3,2,1,0:T(8,128)(2,1)S(1)}, bf16[2,2,64,128]{3,2,1,0:T(8,128)(2,1)S(1)}, u32[]{:S(2)}, u32[]{:S(2)}) collective-permute-start(bf16[2,2,64,128]{3,2,1,0:T(8,128)(2,1)S(1)} %pad_maximum_fusion.4), channel_id=1, source_target_pairs={{0,8},{8,16},{16,24},{24,0},{1,9},{9,17},{17,25},{25,1},{2,10},{10... | collective-permute-start | bytes 196616 | tf_op jit(solution)/shard_map/ppermute | solution.py:585
  47.5 2.1 %restrict_inside.1 = (f32[2,2,2,64,128]{4,3,2,1,0:T(8,128)S(1)}, f32[8,1,2,64,128]{4,3,2,1,0:T(8,128)S(1)}) custom-call(s32[2,2,8]{2,1,0:T(2,128)} %bitcast.56, bf16[8,2,64,128]{3,2,1,0:T(8,128)(2,1)S(1)} %collective-permute-done.15.one_ref, bf16[8,2,64,128]{3,2,1,0:T(8,128)(2,1)S(1)} %collective-permute-done.16.two_ref, ...), custom_call_target="tpu_custom_call" | custom-call | tf_op jit(solution)/shard_map/restrict_inside/pallas_call | solution.py:564
  52.3 1.6 %collective-permute-start.19 = (bf16[2,1,2,64,128]{4,3,2,1,0:T(8,128)(2,1)S(1)}, bf16[2,1,2,64,128]{4,3,2,1,0:T(8,128)(2,1)S(1)}, u32[]{:S(2)}, u32[]{:S(2)}) collective-permute-start(bf16[2,1,2,64,128]{4,3,2,1,0:T(8,128)(2,1)S(1)} %get-tuple-element.97), channel_id=1, source_target_pairs={{0,2},{2,0},{4,6},{6,4},{1,3},{3,1},{5,7},{7,5},{8,10},{10,8},{12,... | collective-permute-start | bytes 196616 | tf_op jit(solution)/shard_map/ppermute | solution.py:596
  53.9 2.7 %collective-permute-start.20 = (bf16[2,1,2,64,128]{4,3,2,1,0:T(8,128)(2,1)S(1)}, bf16[2,1,2,64,128]{4,3,2,1,0:T(8,128)(2,1)S(1)}, u32[]{:S(2)}, u32[]{:S(2)}) collective-permute-start(bf16[2,1,2,64,128]{4,3,2,1,0:T(8,128)(2,1)S(1)} %get-tuple-element.98), channel_id=1, source_target_pairs={{0,4},{2,6},{4,0},{6,2},{1,5},{3,7},{5,1},{7,3},{8,12},{10,14},{12... | collective-permute-start | bytes 196616 | tf_op jit(solution)/shard_map/ppermute | solution.py:596
  57.1 3.4 %collective-permute-done.20.refs_2_ = bf16[2,1,2,64,128]{4,3,2,1,0:T(8,128)(2,1)S(1)} collective-permute-done((bf16[2,1,2,64,128]{4,3,2,1,0:T(8,128)(2,1)S(1)}, bf16[2,1,2,64,128]{4,3,2,1,0:T(8,128)(2,1)S(1)}, u32[]{:S(2)}, u32[]{:S(2)}) %collective-permute-start.20) | collective-permute-done | bytes 65568 | tf_op jit(solution)/shard_map/ppermute | solution.py:596
  60.5 2.4 %collective-permute-done.21.refs_3_ = bf16[2,1,2,64,128]{4,3,2,1,0:T(8,128)(2,1)S(1)} collective-permute-done((bf16[2,1,2,64,128]{4,3,2,1,0:T(8,128)(2,1)S(1)}, bf16[2,1,2,64,128]{4,3,2,1,0:T(8,128)(2,1)S(1)}, u32[]{:S(2)}, u32[]{:S(2)}) %collective-permute-start.21) | collective-permute-done | bytes 65568 | tf_op jit(solution)/shard_map/ppermute | solution.py:596
  63.4 1.6 %collective-permute-start.23 = (bf16[4,2,64,128]{3,2,1,0:T(8,128)(2,1)S(1)}, bf16[4,2,64,128]{3,2,1,0:T(8,128)(2,1)S(1)}, u32[]{:S(2)}, u32[]{:S(2)}) collective-permute-start(bf16[4,2,64,128]{3,2,1,0:T(8,128)(2,1)S(1)} %get-tuple-element.109), channel_id=1, source_target_pairs={{2,0},{4,2},{6,4},{8,6},{10,8},{12,10},{14,12},{16,14},{18,16},{20... | collective-permute-start | bytes 393224 | tf_op jit(solution)/shard_map/ppermute | solution.py:604
  66.0 3.6 %collective-permute-done.23.after_ref = bf16[4,2,64,128]{3,2,1,0:T(8,128)(2,1)S(1)} collective-permute-done((bf16[4,2,64,128]{3,2,1,0:T(8,128)(2,1)S(1)}, bf16[4,2,64,128]{3,2,1,0:T(8,128)(2,1)S(1)}, u32[]{:S(2)}, u32[]{:S(2)}) %collective-permute-start.23) | collective-permute-done | bytes 131104 | tf_op jit(solution)/shard_map/ppermute | solution.py:604
  69.7 4.1 %collective-permute-done.22.before_ref = bf16[4,2,64,128]{3,2,1,0:T(8,128)(2,1)S(1)} collective-permute-done((bf16[4,2,64,128]{3,2,1,0:T(8,128)(2,1)S(1)}, bf16[4,2,64,128]{3,2,1,0:T(8,128)(2,1)S(1)}, u32[]{:S(2)}, u32[]{:S(2)}) %collective-permute-start.22) | collective-permute-done | bytes 131104 | tf_op jit(solution)/shard_map/ppermute | solution.py:603
  74.7 4.3 %collective-permute-start.26 = (bf16[2,1,2,64,128]{4,3,2,1,0:T(8,128)(2,1)S(1)}, bf16[2,1,2,64,128]{4,3,2,1,0:T(8,128)(2,1)S(1)}, u32[]{:S(2)}, u32[]{:S(2)}) collective-permute-start(bf16[2,1,2,64,128]{4,3,2,1,0:T(8,128)(2,1)S(1)} %get-tuple-element.106), channel_id=1, source_target_pairs={{0,6},{2,4},{4,2},{6,0},{1,7},{3,5},{5,3},{7,1},{8,14},{10,12},{12... | collective-permute-start | bytes 196616 | tf_op jit(solution)/shard_map/ppermute | solution.py:596
  79.8 2.1 %collective-permute-done.26.refs_3_ = bf16[2,1,2,64,128]{4,3,2,1,0:T(8,128)(2,1)S(1)} collective-permute-done((bf16[2,1,2,64,128]{4,3,2,1,0:T(8,128)(2,1)S(1)}, bf16[2,1,2,64,128]{4,3,2,1,0:T(8,128)(2,1)S(1)}, u32[]{:S(2)}, u32[]{:S(2)}) %collective-permute-start.26) | collective-permute-done | bytes 65568 | tf_op jit(solution)/shard_map/ppermute | solution.py:596
  81.9 2.0 %prolong.1 = f32[8,2,2,64,128]{4,3,2,1,0:T(8,128)} custom-call(s32[2,2,8]{2,1,0:T(2,128)} %bitcast.58, bf16[16,64,128]{2,1,0:T(8,128)(2,1)S(1)} %bitcast.52, f32[8,2,2,64,128]{4,3,2,1,0:T(8,128)S(1)} %get-tuple-element.79.iterate_ref, f32[2,2,2,64,128]{4,3,2,1,0:T(8,128)S(1)} %get-tuple-element.84.ends_ref, ...), custom_call_target="tpu_custom_call" | custom-call | tf_op jit(solution)/shard_map/prolong/pallas_call | solution.py:564
  (69 shorter events, 22.1 us)
Async XLA Ops:
  2.1 11.1 %collective-permute-start = (bf16[8,2,64,128]{3,2,1,0:T(8,128)(2,1)S(1)}, bf16[8,2,64,128]{3,2,1,0:T(8,128)(2,1)S(1)}, u32[]{:S(2)}, u32[]{:S(2)}) collective-permute-start(bf16[8,2,64,128]{3,2,1,0:T(8,128)(2,1)S(1)} %get-tuple-element.61), channel_id=1, source_target_pairs={{0,2},{2,4},{4,6},{6,7},{7,5},{5,3},{3,1},{1,0},{8,10},{10,12},{12... | collective-permute-start | bytes 786440 | tf_op jit(solution)/shard_map/ppermute | solution.py:580
  5.1 8.0 %collective-permute-start.1 = (bf16[8,2,64,128]{3,2,1,0:T(8,128)(2,1)S(1)}, bf16[8,2,64,128]{3,2,1,0:T(8,128)(2,1)S(1)}, u32[]{:S(2)}, u32[]{:S(2)}) collective-permute-start(bf16[8,2,64,128]{3,2,1,0:T(8,128)(2,1)S(1)} %get-tuple-element.62), channel_id=1, source_target_pairs={{2,0},{4,2},{6,4},{7,6},{5,7},{3,5},{1,3},{0,1},{10,8},{12,10},{14... | collective-permute-start | bytes 786440 | tf_op jit(solution)/shard_map/ppermute | solution.py:580
  10.6 6.8 %collective-permute-start.3 = (bf16[2,2,64,128]{3,2,1,0:T(8,128)(2,1)S(1)}, bf16[2,2,64,128]{3,2,1,0:T(8,128)(2,1)S(1)}, u32[]{:S(2)}, u32[]{:S(2)}) collective-permute-start(bf16[2,2,64,128]{3,2,1,0:T(8,128)(2,1)S(1)} %get-tuple-element.107), channel_id=1, source_target_pairs={{8,0},{16,8},{24,16},{0,24},{9,1},{17,9},{25,17},{1,25},{10,2},{18... | collective-permute-start | bytes 196616 | tf_op jit(solution)/shard_map/ppermute | solution.py:586
  13.1 5.8 %collective-permute-start.2 = (bf16[2,2,64,128]{3,2,1,0:T(8,128)(2,1)S(1)}, bf16[2,2,64,128]{3,2,1,0:T(8,128)(2,1)S(1)}, u32[]{:S(2)}, u32[]{:S(2)}) collective-permute-start(bf16[2,2,64,128]{3,2,1,0:T(8,128)(2,1)S(1)} %get-tuple-element.108), channel_id=1, source_target_pairs={{0,8},{8,16},{16,24},{24,0},{1,9},{9,17},{17,25},{25,1},{2,10},{10... | collective-permute-start | bytes 196616 | tf_op jit(solution)/shard_map/ppermute | solution.py:585
  13.2 6.5 %collective-permute-start.4 = (bf16[2,2,64,128]{3,2,1,0:T(8,128)(2,1)S(1)}, bf16[2,2,64,128]{3,2,1,0:T(8,128)(2,1)S(1)}, u32[]{:S(2)}, u32[]{:S(2)}) collective-permute-start(bf16[2,2,64,128]{3,2,1,0:T(8,128)(2,1)S(1)} %pad_maximum_fusion), channel_id=1, source_target_pairs={{0,8},{8,16},{16,24},{24,0},{1,9},{9,17},{17,25},{25,1},{2,10},{10... | collective-permute-start | bytes 196616 | tf_op jit(solution)/shard_map/ppermute | solution.py:585
  20.4 8.1 %collective-permute-start.6 = (bf16[8,2,64,128]{3,2,1,0:T(8,128)(2,1)S(1)}, bf16[8,2,64,128]{3,2,1,0:T(8,128)(2,1)S(1)}, u32[]{:S(2)}, u32[]{:S(2)}) collective-permute-start(bf16[8,2,64,128]{3,2,1,0:T(8,128)(2,1)S(1)} %get-tuple-element.72), channel_id=1, source_target_pairs={{0,2},{2,4},{4,6},{6,7},{7,5},{5,3},{3,1},{1,0},{8,10},{10,12},{12... | collective-permute-start | bytes 786440 | tf_op jit(solution)/shard_map/ppermute | solution.py:580
  22.2 6.4 %collective-permute-start.7 = (bf16[8,2,64,128]{3,2,1,0:T(8,128)(2,1)S(1)}, bf16[8,2,64,128]{3,2,1,0:T(8,128)(2,1)S(1)}, u32[]{:S(2)}, u32[]{:S(2)}) collective-permute-start(bf16[8,2,64,128]{3,2,1,0:T(8,128)(2,1)S(1)} %get-tuple-element.73), channel_id=1, source_target_pairs={{2,0},{4,2},{6,4},{7,6},{5,7},{3,5},{1,3},{0,1},{10,8},{12,10},{14... | collective-permute-start | bytes 786440 | tf_op jit(solution)/shard_map/ppermute | solution.py:580
  23.3 9.6 %collective-permute-start.9 = (bf16[2,2,64,128]{3,2,1,0:T(8,128)(2,1)S(1)}, bf16[2,2,64,128]{3,2,1,0:T(8,128)(2,1)S(1)}, u32[]{:S(2)}, u32[]{:S(2)}) collective-permute-start(bf16[2,2,64,128]{3,2,1,0:T(8,128)(2,1)S(1)} %get-tuple-element.125), channel_id=1, source_target_pairs={{8,0},{16,8},{24,16},{0,24},{9,1},{17,9},{25,17},{1,25},{10,2},{18... | collective-permute-start | bytes 196616 | tf_op jit(solution)/shard_map/ppermute | solution.py:586
  25.5 7.5 %collective-permute-start.8 = (bf16[2,2,64,128]{3,2,1,0:T(8,128)(2,1)S(1)}, bf16[2,2,64,128]{3,2,1,0:T(8,128)(2,1)S(1)}, u32[]{:S(2)}, u32[]{:S(2)}) collective-permute-start(bf16[2,2,64,128]{3,2,1,0:T(8,128)(2,1)S(1)} %get-tuple-element.126), channel_id=1, source_target_pairs={{0,8},{8,16},{16,24},{24,0},{1,9},{9,17},{17,25},{25,1},{2,10},{10... | collective-permute-start | bytes 196616 | tf_op jit(solution)/shard_map/ppermute | solution.py:585
  28.6 34.3 %collective-permute-start.12 = (bf16[8,320,256]{2,1,0:T(8,128)(2,1)S(1)}, bf16[8,320,256]{2,1,0:T(8,128)(2,1)S(1)}, u32[]{:S(2)}, u32[]{:S(2)}) collective-permute-start(bf16[8,320,256]{2,1,0:T(8,128)(2,1)S(1)} %sort_coarse.1.own_ref.refs_0_), channel_id=1, source_target_pairs={{0,1},{1,0},{2,3},{3,2},{4,5},{5,4},{6,7},{7,6},{8,9},{9,8},{10,11... | collective-permute-start | bytes 3932168 | tf_op jit(solution)/shard_map/ppermute | solution.py:657
  28.7 5.6 %collective-permute-start.10 = (bf16[2,2,64,128]{3,2,1,0:T(8,128)(2,1)S(1)}, bf16[2,2,64,128]{3,2,1,0:T(8,128)(2,1)S(1)}, u32[]{:S(2)}, u32[]{:S(2)}) collective-permute-start(bf16[2,2,64,128]{3,2,1,0:T(8,128)(2,1)S(1)} %pad_maximum_fusion.2), channel_id=1, source_target_pairs={{0,8},{8,16},{16,24},{24,0},{1,9},{9,17},{17,25},{25,1},{2,10},{10... | collective-permute-start | bytes 196616 | tf_op jit(solution)/shard_map/ppermute | solution.py:585
  31.1 4.5 %collective-permute-start.11 = (bf16[2,2,64,128]{3,2,1,0:T(8,128)(2,1)S(1)}, bf16[2,2,64,128]{3,2,1,0:T(8,128)(2,1)S(1)}, u32[]{:S(2)}, u32[]{:S(2)}) collective-permute-start(bf16[2,2,64,128]{3,2,1,0:T(8,128)(2,1)S(1)} %pad_maximum_fusion.3), channel_id=1, source_target_pairs={{8,0},{16,8},{24,16},{0,24},{9,1},{17,9},{25,17},{1,25},{10,2},{18... | collective-permute-start | bytes 196616 | tf_op jit(solution)/shard_map/ppermute | solution.py:586
  36.2 7.1 %collective-permute-start.15 = (bf16[8,2,64,128]{3,2,1,0:T(8,128)(2,1)S(1)}, bf16[8,2,64,128]{3,2,1,0:T(8,128)(2,1)S(1)}, u32[]{:S(2)}, u32[]{:S(2)}) collective-permute-start(bf16[8,2,64,128]{3,2,1,0:T(8,128)(2,1)S(1)} %get-tuple-element.89), channel_id=1, source_target_pairs={{0,2},{2,4},{4,6},{6,7},{7,5},{5,3},{3,1},{1,0},{8,10},{10,12},{12... | collective-permute-start | bytes 786440 | tf_op jit(solution)/shard_map/ppermute | solution.py:580
  38.1 6.4 %collective-permute-start.16 = (bf16[8,2,64,128]{3,2,1,0:T(8,128)(2,1)S(1)}, bf16[8,2,64,128]{3,2,1,0:T(8,128)(2,1)S(1)}, u32[]{:S(2)}, u32[]{:S(2)}) collective-permute-start(bf16[8,2,64,128]{3,2,1,0:T(8,128)(2,1)S(1)} %get-tuple-element.90), channel_id=1, source_target_pairs={{2,0},{4,2},{6,4},{7,6},{5,7},{3,5},{1,3},{0,1},{10,8},{12,10},{14... | collective-permute-start | bytes 786440 | tf_op jit(solution)/shard_map/ppermute | solution.py:580
  39.2 10.5 %collective-permute-start.14 = (bf16[2,2,64,128]{3,2,1,0:T(8,128)(2,1)S(1)}, bf16[2,2,64,128]{3,2,1,0:T(8,128)(2,1)S(1)}, u32[]{:S(2)}, u32[]{:S(2)}) collective-permute-start(bf16[2,2,64,128]{3,2,1,0:T(8,128)(2,1)S(1)} %get-tuple-element.123), channel_id=1, source_target_pairs={{8,0},{16,8},{24,16},{0,24},{9,1},{17,9},{25,17},{1,25},{10,2},{18... | collective-permute-start | bytes 196616 | tf_op jit(solution)/shard_map/ppermute | solution.py:586
  41.7 8.0 %collective-permute-start.13 = (bf16[2,2,64,128]{3,2,1,0:T(8,128)(2,1)S(1)}, bf16[2,2,64,128]{3,2,1,0:T(8,128)(2,1)S(1)}, u32[]{:S(2)}, u32[]{:S(2)}) collective-permute-start(bf16[2,2,64,128]{3,2,1,0:T(8,128)(2,1)S(1)} %get-tuple-element.124), channel_id=1, source_target_pairs={{0,8},{8,16},{16,24},{24,0},{1,9},{9,17},{17,25},{25,1},{2,10},{10... | collective-permute-start | bytes 196616 | tf_op jit(solution)/shard_map/ppermute | solution.py:585
  44.5 5.2 %collective-permute-start.17 = (bf16[2,2,64,128]{3,2,1,0:T(8,128)(2,1)S(1)}, bf16[2,2,64,128]{3,2,1,0:T(8,128)(2,1)S(1)}, u32[]{:S(2)}, u32[]{:S(2)}) collective-permute-start(bf16[2,2,64,128]{3,2,1,0:T(8,128)(2,1)S(1)} %pad_maximum_fusion.4), channel_id=1, source_target_pairs={{0,8},{8,16},{16,24},{24,0},{1,9},{9,17},{17,25},{25,1},{2,10},{10... | collective-permute-start | bytes 196616 | tf_op jit(solution)/shard_map/ppermute | solution.py:585
  52.3 4.9 %collective-permute-start.19 = (bf16[2,1,2,64,128]{4,3,2,1,0:T(8,128)(2,1)S(1)}, bf16[2,1,2,64,128]{4,3,2,1,0:T(8,128)(2,1)S(1)}, u32[]{:S(2)}, u32[]{:S(2)}) collective-permute-start(bf16[2,1,2,64,128]{4,3,2,1,0:T(8,128)(2,1)S(1)} %get-tuple-element.97), channel_id=1, source_target_pairs={{0,2},{2,0},{4,6},{6,4},{1,3},{3,1},{5,7},{7,5},{8,10},{10,8},{12,... | collective-permute-start | bytes 196616 | tf_op jit(solution)/shard_map/ppermute | solution.py:596
  53.9 6.6 %collective-permute-start.20 = (bf16[2,1,2,64,128]{4,3,2,1,0:T(8,128)(2,1)S(1)}, bf16[2,1,2,64,128]{4,3,2,1,0:T(8,128)(2,1)S(1)}, u32[]{:S(2)}, u32[]{:S(2)}) collective-permute-start(bf16[2,1,2,64,128]{4,3,2,1,0:T(8,128)(2,1)S(1)} %get-tuple-element.98), channel_id=1, source_target_pairs={{0,4},{2,6},{4,0},{6,2},{1,5},{3,7},{5,1},{7,3},{8,12},{10,14},{12... | collective-permute-start | bytes 196616 | tf_op jit(solution)/shard_map/ppermute | solution.py:596
  56.7 6.3 %collective-permute-start.21 = (bf16[2,1,2,64,128]{4,3,2,1,0:T(8,128)(2,1)S(1)}, bf16[2,1,2,64,128]{4,3,2,1,0:T(8,128)(2,1)S(1)}, u32[]{:S(2)}, u32[]{:S(2)}) collective-permute-start(bf16[2,1,2,64,128]{4,3,2,1,0:T(8,128)(2,1)S(1)} %get-tuple-element.99), channel_id=1, source_target_pairs={{0,6},{2,4},{4,2},{6,0},{1,7},{3,5},{5,3},{7,1},{8,14},{10,12},{12... | collective-permute-start | bytes 196616 | tf_op jit(solution)/shard_map/ppermute | solution.py:596
  63.4 6.3 %collective-permute-start.23 = (bf16[4,2,64,128]{3,2,1,0:T(8,128)(2,1)S(1)}, bf16[4,2,64,128]{3,2,1,0:T(8,128)(2,1)S(1)}, u32[]{:S(2)}, u32[]{:S(2)}) collective-permute-start(bf16[4,2,64,128]{3,2,1,0:T(8,128)(2,1)S(1)} %get-tuple-element.109), channel_id=1, source_target_pairs={{2,0},{4,2},{6,4},{8,6},{10,8},{12,10},{14,12},{16,14},{18,16},{20... | collective-permute-start | bytes 393224 | tf_op jit(solution)/shard_map/ppermute | solution.py:604
  65.0 8.7 %collective-permute-start.22 = (bf16[4,2,64,128]{3,2,1,0:T(8,128)(2,1)S(1)}, bf16[4,2,64,128]{3,2,1,0:T(8,128)(2,1)S(1)}, u32[]{:S(2)}, u32[]{:S(2)}) collective-permute-start(bf16[4,2,64,128]{3,2,1,0:T(8,128)(2,1)S(1)} %get-tuple-element.110), channel_id=1, source_target_pairs={{0,2},{2,4},{4,6},{6,8},{8,10},{10,12},{12,14},{14,16},{16,18},{18... | collective-permute-start | bytes 393224 | tf_op jit(solution)/shard_map/ppermute | solution.py:603
  74.6 5.2 %collective-permute-start.25 = (bf16[2,1,2,64,128]{4,3,2,1,0:T(8,128)(2,1)S(1)}, bf16[2,1,2,64,128]{4,3,2,1,0:T(8,128)(2,1)S(1)}, u32[]{:S(2)}, u32[]{:S(2)}) collective-permute-start(bf16[2,1,2,64,128]{4,3,2,1,0:T(8,128)(2,1)S(1)} %get-tuple-element.105), channel_id=1, source_target_pairs={{0,4},{2,6},{4,0},{6,2},{1,5},{3,7},{5,1},{7,3},{8,12},{10,14},{12... | collective-permute-start | bytes 196616 | tf_op jit(solution)/shard_map/ppermute | solution.py:596
  74.7 7.3 %collective-permute-start.26 = (bf16[2,1,2,64,128]{4,3,2,1,0:T(8,128)(2,1)S(1)}, bf16[2,1,2,64,128]{4,3,2,1,0:T(8,128)(2,1)S(1)}, u32[]{:S(2)}, u32[]{:S(2)}) collective-permute-start(bf16[2,1,2,64,128]{4,3,2,1,0:T(8,128)(2,1)S(1)} %get-tuple-element.106), channel_id=1, source_target_pairs={{0,6},{2,4},{4,2},{6,0},{1,7},{3,5},{5,3},{7,1},{8,14},{10,12},{12... | collective-permute-start | bytes 196616 | tf_op jit(solution)/shard_map/ppermute | solution.py:596
  (7 other events, 42.8 us)

commit v3 on v2

--- a/solution.py
+++ b/solution.py
@@ -342,14 +342,15 @@
             add_from(total, rows, cells, targets, slot=lambda x, end=end: end)
 
 
-def add_coarse_ends(before_ref, after_ref, rows, total):
+def add_coarse_ends(one_ref, two_ref, rows, total):
     size_x, size_y = total.shape[:2]
+    even = lax.axis_index("depth") % 2 == 0
     at = lax.axis_index(("track", "lateral"))
     count = lax.axis_size(("track", "lateral"))
     for near in range(size_y):
         ys = [y for y in range(size_y) if abs(near - y) <= 1]
-        for end, ref, inside in ((0, before_ref, at > 0), (1, after_ref, at < count - 1)):
-            cells = ref[near]
+        one, two = one_ref[near], two_ref[near]
+        for end, cells, inside in ((0, jnp.where(even, one, two), at > 0), (1, jnp.where(even, two, one), at < count - 1)):
             cells = jnp.where(inside, cells, jnp.zeros_like(cells))
             add_from(total, rows, cells, [(end * (size_x - 1), y, 6 * end + near - y + 1) for y in ys])
 
@@ -495,9 +496,9 @@
 
 
 def first_kernel(own_ref, other_ref, *refs):
-    pieces, (coarse_ref, first_ref, round_ref, total, scratch) = refs[:-5], refs[-5:]
+    pieces, (coarse_ref, first_ref, round_ref, one_ref, two_ref, total, scratch) = refs[:-7], refs[-7:]
     rows = Coarse(own_ref, other_ref, coarse_ref.shape[1])
-    columns = placed(pieces)
+    columns = placed(pieces[::-1])
     cells = [[piece[z] for z in range(2)] for _, _, piece in columns]
     lefts = [mask_layers(rows.smoother(x, y), rows.kind()) for x, y, _ in columns]
     places = [(index,) for index in range(len(columns))]
@@ -508,13 +509,15 @@
             coarse_ref[x, y, z] = cell[z]
             first_ref[x, y, z] = value
             round_ref[x, y, z] = value.astype(BF16)
-
-
-def second_kernel(before_ref, after_ref, own_ref, other_ref, given_ref, coarse_ref, first_ref, *refs):
+    for y in range(one_ref.shape[0]):
+        give_faces(round_ref.at[0, y], round_ref.at[round_ref.shape[0] - 1, y], one_ref, two_ref, y)
+
+
+def second_kernel(one_ref, two_ref, own_ref, other_ref, given_ref, coarse_ref, first_ref, *refs):
     pieces, (total, scratch) = refs[:-2], refs[-2:]
     rows = Coarse(own_ref, other_ref, total.shape[1])
     total[...] = given_ref[...]
-    add_coarse_ends(before_ref, after_ref, rows, total)
+    add_coarse_ends(one_ref, two_ref, rows, total)
     columns = placed(pieces)
     values = smooth_columns(
         rows, total, [(x, y) for x, y, _ in columns], [rows.smoother(x, y) for x, y, _ in columns],
@@ -529,7 +532,7 @@
 def prolong_kernel(group_ref, transfer_ref, iterate_ref, ends_ref, *refs):
     pieces, (out_ref, correction, total, scratch, made, sent) = refs[:-6], refs[-6:]
     size_x, size_y = out_ref.shape[:2]
-    for step, piece in enumerate(pieces):
+    for step, piece in enumerate(pieces[::-1]):
         first = lax.bitwise_xor(lax.axis_index("lateral"), step) * piece.shape[0]
         for x in range(piece.shape[0]):
             correction[first + x] = piece[x]
@@ -572,12 +575,16 @@
     )(*scalars, *operands)
 
 
-def swap_sides(one, two):
-    lateral, depth = lax.axis_size("lateral"), lax.axis_size("depth")
-    ring = [i * depth for i in range(lateral)] + [i * depth + 1 for i in reversed(range(lateral))]
+def swap_round(one, two, axes):
+    count, depth = lax.axis_size(axes), lax.axis_size("depth")
+    ring = [i * depth for i in range(count)] + [i * depth + 1 for i in reversed(range(count))]
     onward = list(zip(ring, ring[1:] + ring[:1]))
     back = [(b, a) for a, b in onward]
-    return lax.ppermute(one, ("lateral", "depth"), onward), lax.ppermute(two, ("lateral", "depth"), back)
+    return lax.ppermute(one, (*axes, "depth"), onward), lax.ppermute(two, (*axes, "depth"), back)
+
+
+def swap_sides(one, two):
+    return swap_round(one, two, ("lateral",))
 
 
 def swap_ends(last, first):
@@ -593,16 +600,8 @@
 
 def swap_pieces(pieces):
     count = len(pieces)
-    moved = [lax.ppermute(pieces[step], "lateral", [(i, i ^ step) for i in range(count)]) for step in range(count - 1, 0, -1)]
-    return [pieces[0]] + moved[::-1]
-
-
-def swap_coarse_ends(cells):
-    axes = ("track", "lateral")
-    count = lax.axis_size(axes)
-    before = lax.ppermute(cells[-1], axes, [(i, (i + 1) % count) for i in range(count)])
-    after = lax.ppermute(cells[0], axes, [((i + 1) % count, i) for i in range(count)])
-    return before, after
+    moved = [lax.ppermute(pieces[step], "lateral", [(i, i ^ step) for i in range(count)]) for step in range(1, count)]
+    return moved[::-1] + [pieces[0]]
 
 
 def per_device(
@@ -682,18 +681,19 @@
     )
     line = pltpu.VMEM((part_x * all_y, 2, 2, width, loads), F32)
     coarse_ops = [own_ops, other_ops]
-    coarse_res, first, rounded = call(
+    row = full(solve_field[1:], BF16)
+    coarse_res, first, rounded, one, two = call(
         first_kernel, "first", [], coarse_ops + swap_pieces(pieces),
-        [full(solve_field, BF16), full(solve_field, F32), full(solve_field, BF16)],
+        [full(solve_field, BF16), full(solve_field, F32), full(solve_field, BF16), row, row],
         [
             pltpu.VMEM((part_x * all_y, 2, 2 * HALF, LANES), F32),
             pltpu.VMEM((part_x * all_y, 2, width, loads), F32),
         ],
     )
-    before, after = swap_coarse_ends(rounded)
+    one, two = swap_round(one, two, ("track", "lateral"))
     inner = inner_of(rounded, rounded, coarse_ops, Coarse)
     pieces = call(
-        second_kernel, "second", [], [before, after, *coarse_ops, inner, coarse_res, first], [piece] * count,
+        second_kernel, "second", [], [one, two, *coarse_ops, inner, coarse_res, first], [piece] * count,
         [pltpu.VMEM(sums(solve_field), F32), line],
     )
     return call(

time: 84.4 us -> 82.4 us (0.976)
  starting transfers between devices: 34 us -> 32.6 us
    ppermute x8, starting transfers between devices: 8.83 us -> 7.32 us  [the longest x4 7.28 us: swap_round(): lax.ppermute(one, (*axes, 'depth'), onward)]
  transfers between devices with their start and end apart: 27 -> 27, of which waited for: 16 -> 15; matrix products, arithmetic and copies ran while one was open for 0% -> 0% of each run, Pallas kernels for 21% -> 21%
where the time goes in v3:
time: 82.4 us; the launch traced here: 82.1 us
  starting transfers between devices  32.6 us (40%)
  waiting for transfers between devices  25.4 us (31%)
  Pallas kernels  23.5 us (29%)
    pallas_call x13, Pallas kernels, call(): pl.pallas_call(kernel, in_specs=[SMEM] * len(scalars) + [VMEM] * len(oper...  14.1 us
    ppermute x6, starting transfers between devices, swap_ends(): lax.ppermute(first, 'track', [((i + 1) % count, i) for i in range(count)])  9.75 us
    ppermute x6, waiting for transfers between devices, swap_pieces(): lax.ppermute(pieces[step], 'lateral', [(i, i ^ step) for i in range(count)])  9.11 us
    ppermute x6, starting transfers between devices, swap_pieces(): lax.ppermute(pieces[step], 'lateral', [(i, i ^ step) for i in range(count)])  8.92 us
    ppermute x4, starting transfers between devices, swap_round(): lax.ppermute(one, (*axes, 'depth'), onward)  7.28 us
    ppermute x6, starting transfers between devices, swap_ends(): lax.ppermute(last, 'track', [(i, (i + 1) % count) for i in range(count)])  6.49 us
    ppermute x4, waiting for transfers between devices, swap_round(): lax.ppermute(two, (*axes, 'depth'), back)  5.78 us
    pallas_call x1, Pallas kernels, sort_fine(): pl.pallas_call(fine_sort_kernel, in_specs=[SMEM, VMEM, pl.BlockSpec(memor...  4.38 us
  transfers between devices with their start and end apart: 27, of which 15 were waited for; matrix products, arithmetic and copies ran while one was open for 0% of the time, Pallas kernels for 21%

profile of v3, /device:TPU:0, one launch (start us, length us, event | category | flops | bytes accessed | tf_op | source)
XLA Modules:
  0.0 82.1 jit_solution(9477283833954747614)
XLA Ops:
  0.0 2.1 %round_start.1 = (bf16[8,2,2,64,128]{4,3,2,1,0:T(8,128)(2,1)S(1)}, bf16[8,2,64,128]{3,2,1,0:T(8,128)(2,1)S(1)}, bf16[8,2,64,128]{3,2,1,0:T(8,128)(2,1)S(1)}) custom-call(f32[8,2,2,64,128]{4,3,2,1,0:T(8,128)} %old_ref.3), custom_call_target="tpu_custom_call" | custom-call | tf_op jit(solution)/shard_map/round_start/pallas_call | solution.py:317
  2.1 3.0 %collective-permute-start = (bf16[8,2,64,128]{3,2,1,0:T(8,128)(2,1)S(1)}, bf16[8,2,64,128]{3,2,1,0:T(8,128)(2,1)S(1)}, u32[]{:S(2)}, u32[]{:S(2)}) collective-permute-start(bf16[8,2,64,128]{3,2,1,0:T(8,128)(2,1)S(1)} %get-tuple-element.63), channel_id=1, source_target_pairs={{0,2},{2,4},{4,6},{6,7},{7,5},{5,3},{3,1},{1,0},{8,10},{10,12},{12... | collective-permute-start | bytes 786440 | tf_op jit(solution)/shard_map/ppermute | solution.py:583
  5.1 4.4 %sort_fine.1.refs_0_.ops_ref = bf16[16,640,256]{2,1,0:T(8,128)(2,1)S(1)} custom-call(s32[32,27]{1,0:T(8,128)} %bitcast.55, bf16[16,2,64]{2,1,0:T(2,128)(2,1)} %bitcast.56, bf16[16,27,64,128]{3,2,1,0:T(8,128)(2,1)} %bitcast.49), custom_call_target="tpu_custom_call" | custom-call | tf_op jit(solution)/shard_map/sort_fine/pallas_call | solution.py:99
  10.6 2.5 %collective-permute-start.3 = (bf16[2,2,64,128]{3,2,1,0:T(8,128)(2,1)S(1)}, bf16[2,2,64,128]{3,2,1,0:T(8,128)(2,1)S(1)}, u32[]{:S(2)}, u32[]{:S(2)}) collective-permute-start(bf16[2,2,64,128]{3,2,1,0:T(8,128)(2,1)S(1)} %get-tuple-element.111), channel_id=1, source_target_pairs={{8,0},{16,8},{24,16},{0,24},{9,1},{17,9},{25,17},{1,25},{10,2},{18... | collective-permute-start | bytes 196616 | tf_op jit(solution)/shard_map/ppermute | solution.py:593
  13.2 2.0 %collective-permute-start.4 = (bf16[2,2,64,128]{3,2,1,0:T(8,128)(2,1)S(1)}, bf16[2,2,64,128]{3,2,1,0:T(8,128)(2,1)S(1)}, u32[]{:S(2)}, u32[]{:S(2)}) collective-permute-start(bf16[2,2,64,128]{3,2,1,0:T(8,128)(2,1)S(1)} %pad_maximum_fusion), channel_id=1, source_target_pairs={{0,8},{8,16},{16,24},{24,0},{1,9},{9,17},{17,25},{25,1},{2,10},{10... | collective-permute-start | bytes 196616 | tf_op jit(solution)/shard_map/ppermute | solution.py:592
  17.5 1.5 %collective-permute-done.2.before_ref = bf16[2,2,64,128]{3,2,1,0:T(8,128)(2,1)S(1)} collective-permute-done((bf16[2,2,64,128]{3,2,1,0:T(8,128)(2,1)S(1)}, bf16[2,2,64,128]{3,2,1,0:T(8,128)(2,1)S(1)}, u32[]{:S(2)}, u32[]{:S(2)}) %collective-permute-start.2) | collective-permute-done | bytes 65568 | tf_op jit(solution)/shard_map/ppermute | solution.py:592
  20.4 1.8 %collective-permute-start.6 = (bf16[8,2,64,128]{3,2,1,0:T(8,128)(2,1)S(1)}, bf16[8,2,64,128]{3,2,1,0:T(8,128)(2,1)S(1)}, u32[]{:S(2)}, u32[]{:S(2)}) collective-permute-start(bf16[8,2,64,128]{3,2,1,0:T(8,128)(2,1)S(1)} %get-tuple-element.74), channel_id=1, source_target_pairs={{0,2},{2,4},{4,6},{6,7},{7,5},{5,3},{3,1},{1,0},{8,10},{10,12},{12... | collective-permute-start | bytes 786440 | tf_op jit(solution)/shard_map/ppermute | solution.py:583
  23.3 2.1 %collective-permute-start.9 = (bf16[2,2,64,128]{3,2,1,0:T(8,128)(2,1)S(1)}, bf16[2,2,64,128]{3,2,1,0:T(8,128)(2,1)S(1)}, u32[]{:S(2)}, u32[]{:S(2)}) collective-permute-start(bf16[2,2,64,128]{3,2,1,0:T(8,128)(2,1)S(1)} %get-tuple-element.127), channel_id=1, source_target_pairs={{8,0},{16,8},{24,16},{0,24},{9,1},{17,9},{25,17},{1,25},{10,2},{18... | collective-permute-start | bytes 196616 | tf_op jit(solution)/shard_map/ppermute | solution.py:593
  25.5 3.0 %sort_coarse.1.own_ref.refs_0_ = bf16[8,320,256]{2,1,0:T(8,128)(2,1)S(1)} custom-call(s32[8,27]{1,0:T(8,128)} %bitcast.57, bf16[2,4,64]{2,1,0:T(4,128)(2,1)} %bitcast.58, bf16[2,128,128]{2,1,0:T(8,128)(2,1)} %bitcast.51, bf16[2,27,128,128]{3,2,1,0:T(8,128)(2,1)} %bitcast.50), custom_call_target="tpu_custom_call" | custom-call | tf_op jit(solution)/shard_map/sort_coarse/pallas_call | solution.py:117
  28.7 2.4 %collective-permute-start.10 = (bf16[2,2,64,128]{3,2,1,0:T(8,128)(2,1)S(1)}, bf16[2,2,64,128]{3,2,1,0:T(8,128)(2,1)S(1)}, u32[]{:S(2)}, u32[]{:S(2)}) collective-permute-start(bf16[2,2,64,128]{3,2,1,0:T(8,128)(2,1)S(1)} %pad_maximum_fusion.2), channel_id=1, source_target_pairs={{0,8},{8,16},{16,24},{24,0},{1,9},{9,17},{17,25},{25,1},{2,10},{10... | collective-permute-start | bytes 196616 | tf_op jit(solution)/shard_map/ppermute | solution.py:592
  36.2 1.9 %collective-permute-start.15 = (bf16[8,2,64,128]{3,2,1,0:T(8,128)(2,1)S(1)}, bf16[8,2,64,128]{3,2,1,0:T(8,128)(2,1)S(1)}, u32[]{:S(2)}, u32[]{:S(2)}) collective-permute-start(bf16[8,2,64,128]{3,2,1,0:T(8,128)(2,1)S(1)} %get-tuple-element.91), channel_id=1, source_target_pairs={{0,2},{2,4},{4,6},{6,7},{7,5},{5,3},{3,1},{1,0},{8,10},{10,12},{12... | collective-permute-start | bytes 786440 | tf_op jit(solution)/shard_map/ppermute | solution.py:583
  39.2 2.5 %collective-permute-start.14 = (bf16[2,2,64,128]{3,2,1,0:T(8,128)(2,1)S(1)}, bf16[2,2,64,128]{3,2,1,0:T(8,128)(2,1)S(1)}, u32[]{:S(2)}, u32[]{:S(2)}) collective-permute-start(bf16[2,2,64,128]{3,2,1,0:T(8,128)(2,1)S(1)} %get-tuple-element.125), channel_id=1, source_target_pairs={{8,0},{16,8},{24,16},{0,24},{9,1},{17,9},{25,17},{1,25},{10,2},{18... | collective-permute-start | bytes 196616 | tf_op jit(solution)/shard_map/ppermute | solution.py:593
  41.7 1.7 %collective-permute-done.15.one_ref = bf16[8,2,64,128]{3,2,1,0:T(8,128)(2,1)S(1)} collective-permute-done((bf16[8,2,64,128]{3,2,1,0:T(8,128)(2,1)S(1)}, bf16[8,2,64,128]{3,2,1,0:T(8,128)(2,1)S(1)}, u32[]{:S(2)}, u32[]{:S(2)}) %collective-permute-start.15) | collective-permute-done | bytes 262176 | tf_op jit(solution)/shard_map/ppermute | solution.py:583
  44.5 2.1 %collective-permute-start.17 = (bf16[2,2,64,128]{3,2,1,0:T(8,128)(2,1)S(1)}, bf16[2,2,64,128]{3,2,1,0:T(8,128)(2,1)S(1)}, u32[]{:S(2)}, u32[]{:S(2)}) collective-permute-start(bf16[2,2,64,128]{3,2,1,0:T(8,128)(2,1)S(1)} %pad_maximum_fusion.4), channel_id=1, source_target_pairs={{0,8},{8,16},{16,24},{24,0},{1,9},{9,17},{17,25},{25,1},{2,10},{10... | collective-permute-start | bytes 196616 | tf_op jit(solution)/shard_map/ppermute | solution.py:592
  47.5 2.1 %restrict_inside.1 = (f32[2,2,2,64,128]{4,3,2,1,0:T(8,128)S(1)}, f32[8,1,2,64,128]{4,3,2,1,0:T(8,128)S(1)}) custom-call(s32[2,2,8]{2,1,0:T(2,128)} %bitcast.52, bf16[8,2,64,128]{3,2,1,0:T(8,128)(2,1)S(1)} %collective-permute-done.15.one_ref, bf16[8,2,64,128]{3,2,1,0:T(8,128)(2,1)S(1)} %collective-permute-done.16.two_ref, ...), custom_call_target="tpu_custom_call" | custom-call | tf_op jit(solution)/shard_map/restrict_inside/pallas_call | solution.py:567
  52.3 3.8 %collective-permute-start.19 = (bf16[2,1,2,64,128]{4,3,2,1,0:T(8,128)(2,1)S(1)}, bf16[2,1,2,64,128]{4,3,2,1,0:T(8,128)(2,1)S(1)}, u32[]{:S(2)}, u32[]{:S(2)}) collective-permute-start(bf16[2,1,2,64,128]{4,3,2,1,0:T(8,128)(2,1)S(1)} %get-tuple-element.98), channel_id=1, source_target_pairs={{0,6},{2,4},{4,2},{6,0},{1,7},{3,5},{5,3},{7,1},{8,14},{10,12},{12... | collective-permute-start | bytes 196616 | tf_op jit(solution)/shard_map/ppermute | solution.py:603
  56.8 1.8 %collective-permute-done.19.refs_0_ = bf16[2,1,2,64,128]{4,3,2,1,0:T(8,128)(2,1)S(1)} collective-permute-done((bf16[2,1,2,64,128]{4,3,2,1,0:T(8,128)(2,1)S(1)}, bf16[2,1,2,64,128]{4,3,2,1,0:T(8,128)(2,1)S(1)}, u32[]{:S(2)}, u32[]{:S(2)}) %collective-permute-start.19) | collective-permute-done | bytes 65568 | tf_op jit(solution)/shard_map/ppermute | solution.py:603
  58.5 2.8 %collective-permute-done.20.refs_1_ = bf16[2,1,2,64,128]{4,3,2,1,0:T(8,128)(2,1)S(1)} collective-permute-done((bf16[2,1,2,64,128]{4,3,2,1,0:T(8,128)(2,1)S(1)}, bf16[2,1,2,64,128]{4,3,2,1,0:T(8,128)(2,1)S(1)}, u32[]{:S(2)}, u32[]{:S(2)}) %collective-permute-start.20) | collective-permute-done | bytes 65568 | tf_op jit(solution)/shard_map/ppermute | solution.py:603
  63.0 2.6 %collective-permute-done.22.one_ref = bf16[4,2,64,128]{3,2,1,0:T(8,128)(2,1)S(1)} collective-permute-done((bf16[4,2,64,128]{3,2,1,0:T(8,128)(2,1)S(1)}, bf16[4,2,64,128]{3,2,1,0:T(8,128)(2,1)S(1)}, u32[]{:S(2)}, u32[]{:S(2)}) %collective-permute-start.22) | collective-permute-done | bytes 131104 | tf_op jit(solution)/shard_map/ppermute | solution.py:583
  65.6 4.5 %collective-permute-done.23.two_ref = bf16[4,2,64,128]{3,2,1,0:T(8,128)(2,1)S(1)} collective-permute-done((bf16[4,2,64,128]{3,2,1,0:T(8,128)(2,1)S(1)}, bf16[4,2,64,128]{3,2,1,0:T(8,128)(2,1)S(1)}, u32[]{:S(2)}, u32[]{:S(2)}) %collective-permute-start.23) | collective-permute-done | bytes 131104 | tf_op jit(solution)/shard_map/ppermute | solution.py:583
  70.9 3.8 %collective-permute-start.24 = (bf16[2,1,2,64,128]{4,3,2,1,0:T(8,128)(2,1)S(1)}, bf16[2,1,2,64,128]{4,3,2,1,0:T(8,128)(2,1)S(1)}, u32[]{:S(2)}, u32[]{:S(2)}) collective-permute-start(bf16[2,1,2,64,128]{4,3,2,1,0:T(8,128)(2,1)S(1)} %get-tuple-element.107), channel_id=1, source_target_pairs={{0,6},{2,4},{4,2},{6,0},{1,7},{3,5},{5,3},{7,1},{8,14},{10,12},{12... | collective-permute-start | bytes 196616 | tf_op jit(solution)/shard_map/ppermute | solution.py:603
  75.3 1.7 %collective-permute-done.24.refs_0_ = bf16[2,1,2,64,128]{4,3,2,1,0:T(8,128)(2,1)S(1)} collective-permute-done((bf16[2,1,2,64,128]{4,3,2,1,0:T(8,128)(2,1)S(1)}, bf16[2,1,2,64,128]{4,3,2,1,0:T(8,128)(2,1)S(1)}, u32[]{:S(2)}, u32[]{:S(2)}) %collective-permute-start.24) | collective-permute-done | bytes 65568 | tf_op jit(solution)/shard_map/ppermute | solution.py:603
  77.0 2.8 %collective-permute-done.25.refs_1_ = bf16[2,1,2,64,128]{4,3,2,1,0:T(8,128)(2,1)S(1)} collective-permute-done((bf16[2,1,2,64,128]{4,3,2,1,0:T(8,128)(2,1)S(1)}, bf16[2,1,2,64,128]{4,3,2,1,0:T(8,128)(2,1)S(1)}, u32[]{:S(2)}, u32[]{:S(2)}) %collective-permute-start.25) | collective-permute-done | bytes 65568 | tf_op jit(solution)/shard_map/ppermute | solution.py:603
  79.9 2.0 %prolong.1 = f32[8,2,2,64,128]{4,3,2,1,0:T(8,128)} custom-call(s32[2,2,8]{2,1,0:T(2,128)} %bitcast.54, bf16[16,64,128]{2,1,0:T(8,128)(2,1)S(1)} %bitcast.48, f32[8,2,2,64,128]{4,3,2,1,0:T(8,128)S(1)} %get-tuple-element.81.iterate_ref, f32[2,2,2,64,128]{4,3,2,1,0:T(8,128)S(1)} %get-tuple-element.86.ends_ref, ...), custom_call_target="tpu_custom_call" | custom-call | tf_op jit(solution)/shard_map/prolong/pallas_call | solution.py:567
  (68 shorter events, 20.6 us)
Async XLA Ops:
  2.1 11.1 %collective-permute-start = (bf16[8,2,64,128]{3,2,1,0:T(8,128)(2,1)S(1)}, bf16[8,2,64,128]{3,2,1,0:T(8,128)(2,1)S(1)}, u32[]{:S(2)}, u32[]{:S(2)}) collective-permute-start(bf16[8,2,64,128]{3,2,1,0:T(8,128)(2,1)S(1)} %get-tuple-element.63), channel_id=1, source_target_pairs={{0,2},{2,4},{4,6},{6,7},{7,5},{5,3},{3,1},{1,0},{8,10},{10,12},{12... | collective-permute-start | bytes 786440 | tf_op jit(solution)/shard_map/ppermute | solution.py:583
  5.1 8.0 %collective-permute-start.1 = (bf16[8,2,64,128]{3,2,1,0:T(8,128)(2,1)S(1)}, bf16[8,2,64,128]{3,2,1,0:T(8,128)(2,1)S(1)}, u32[]{:S(2)}, u32[]{:S(2)}) collective-permute-start(bf16[8,2,64,128]{3,2,1,0:T(8,128)(2,1)S(1)} %get-tuple-element.64), channel_id=1, source_target_pairs={{2,0},{4,2},{6,4},{7,6},{5,7},{3,5},{1,3},{0,1},{10,8},{12,10},{14... | collective-permute-start | bytes 786440 | tf_op jit(solution)/shard_map/ppermute | solution.py:583
  10.6 6.8 %collective-permute-start.3 = (bf16[2,2,64,128]{3,2,1,0:T(8,128)(2,1)S(1)}, bf16[2,2,64,128]{3,2,1,0:T(8,128)(2,1)S(1)}, u32[]{:S(2)}, u32[]{:S(2)}) collective-permute-start(bf16[2,2,64,128]{3,2,1,0:T(8,128)(2,1)S(1)} %get-tuple-element.111), channel_id=1, source_target_pairs={{8,0},{16,8},{24,16},{0,24},{9,1},{17,9},{25,17},{1,25},{10,2},{18... | collective-permute-start | bytes 196616 | tf_op jit(solution)/shard_map/ppermute | solution.py:593
  13.1 5.8 %collective-permute-start.2 = (bf16[2,2,64,128]{3,2,1,0:T(8,128)(2,1)S(1)}, bf16[2,2,64,128]{3,2,1,0:T(8,128)(2,1)S(1)}, u32[]{:S(2)}, u32[]{:S(2)}) collective-permute-start(bf16[2,2,64,128]{3,2,1,0:T(8,128)(2,1)S(1)} %get-tuple-element.112), channel_id=1, source_target_pairs={{0,8},{8,16},{16,24},{24,0},{1,9},{9,17},{17,25},{25,1},{2,10},{10... | collective-permute-start | bytes 196616 | tf_op jit(solution)/shard_map/ppermute | solution.py:592
  13.2 6.5 %collective-permute-start.4 = (bf16[2,2,64,128]{3,2,1,0:T(8,128)(2,1)S(1)}, bf16[2,2,64,128]{3,2,1,0:T(8,128)(2,1)S(1)}, u32[]{:S(2)}, u32[]{:S(2)}) collective-permute-start(bf16[2,2,64,128]{3,2,1,0:T(8,128)(2,1)S(1)} %pad_maximum_fusion), channel_id=1, source_target_pairs={{0,8},{8,16},{16,24},{24,0},{1,9},{9,17},{17,25},{25,1},{2,10},{10... | collective-permute-start | bytes 196616 | tf_op jit(solution)/shard_map/ppermute | solution.py:592
  20.4 8.1 %collective-permute-start.6 = (bf16[8,2,64,128]{3,2,1,0:T(8,128)(2,1)S(1)}, bf16[8,2,64,128]{3,2,1,0:T(8,128)(2,1)S(1)}, u32[]{:S(2)}, u32[]{:S(2)}) collective-permute-start(bf16[8,2,64,128]{3,2,1,0:T(8,128)(2,1)S(1)} %get-tuple-element.74), channel_id=1, source_target_pairs={{0,2},{2,4},{4,6},{6,7},{7,5},{5,3},{3,1},{1,0},{8,10},{10,12},{12... | collective-permute-start | bytes 786440 | tf_op jit(solution)/shard_map/ppermute | solution.py:583
  22.2 6.4 %collective-permute-start.7 = (bf16[8,2,64,128]{3,2,1,0:T(8,128)(2,1)S(1)}, bf16[8,2,64,128]{3,2,1,0:T(8,128)(2,1)S(1)}, u32[]{:S(2)}, u32[]{:S(2)}) collective-permute-start(bf16[8,2,64,128]{3,2,1,0:T(8,128)(2,1)S(1)} %get-tuple-element.75), channel_id=1, source_target_pairs={{2,0},{4,2},{6,4},{7,6},{5,7},{3,5},{1,3},{0,1},{10,8},{12,10},{14... | collective-permute-start | bytes 786440 | tf_op jit(solution)/shard_map/ppermute | solution.py:583
  23.3 9.6 %collective-permute-start.9 = (bf16[2,2,64,128]{3,2,1,0:T(8,128)(2,1)S(1)}, bf16[2,2,64,128]{3,2,1,0:T(8,128)(2,1)S(1)}, u32[]{:S(2)}, u32[]{:S(2)}) collective-permute-start(bf16[2,2,64,128]{3,2,1,0:T(8,128)(2,1)S(1)} %get-tuple-element.127), channel_id=1, source_target_pairs={{8,0},{16,8},{24,16},{0,24},{9,1},{17,9},{25,17},{1,25},{10,2},{18... | collective-permute-start | bytes 196616 | tf_op jit(solution)/shard_map/ppermute | solution.py:593
  25.5 7.5 %collective-permute-start.8 = (bf16[2,2,64,128]{3,2,1,0:T(8,128)(2,1)S(1)}, bf16[2,2,64,128]{3,2,1,0:T(8,128)(2,1)S(1)}, u32[]{:S(2)}, u32[]{:S(2)}) collective-permute-start(bf16[2,2,64,128]{3,2,1,0:T(8,128)(2,1)S(1)} %get-tuple-element.128), channel_id=1, source_target_pairs={{0,8},{8,16},{16,24},{24,0},{1,9},{9,17},{17,25},{25,1},{2,10},{10... | collective-permute-start | bytes 196616 | tf_op jit(solution)/shard_map/ppermute | solution.py:592
  28.6 32.8 %collective-permute-start.12 = (bf16[8,320,256]{2,1,0:T(8,128)(2,1)S(1)}, bf16[8,320,256]{2,1,0:T(8,128)(2,1)S(1)}, u32[]{:S(2)}, u32[]{:S(2)}) collective-permute-start(bf16[8,320,256]{2,1,0:T(8,128)(2,1)S(1)} %sort_coarse.1.own_ref.refs_0_), channel_id=1, source_target_pairs={{0,1},{1,0},{2,3},{3,2},{4,5},{5,4},{6,7},{7,6},{8,9},{9,8},{10,11... | collective-permute-start | bytes 3932168 | tf_op jit(solution)/shard_map/ppermute | solution.py:656
  28.7 5.6 %collective-permute-start.10 = (bf16[2,2,64,128]{3,2,1,0:T(8,128)(2,1)S(1)}, bf16[2,2,64,128]{3,2,1,0:T(8,128)(2,1)S(1)}, u32[]{:S(2)}, u32[]{:S(2)}) collective-permute-start(bf16[2,2,64,128]{3,2,1,0:T(8,128)(2,1)S(1)} %pad_maximum_fusion.2), channel_id=1, source_target_pairs={{0,8},{8,16},{16,24},{24,0},{1,9},{9,17},{17,25},{25,1},{2,10},{10... | collective-permute-start | bytes 196616 | tf_op jit(solution)/shard_map/ppermute | solution.py:592
  31.1 4.5 %collective-permute-start.11 = (bf16[2,2,64,128]{3,2,1,0:T(8,128)(2,1)S(1)}, bf16[2,2,64,128]{3,2,1,0:T(8,128)(2,1)S(1)}, u32[]{:S(2)}, u32[]{:S(2)}) collective-permute-start(bf16[2,2,64,128]{3,2,1,0:T(8,128)(2,1)S(1)} %pad_maximum_fusion.3), channel_id=1, source_target_pairs={{8,0},{16,8},{24,16},{0,24},{9,1},{17,9},{25,17},{1,25},{10,2},{18... | collective-permute-start | bytes 196616 | tf_op jit(solution)/shard_map/ppermute | solution.py:593
  36.2 7.1 %collective-permute-start.15 = (bf16[8,2,64,128]{3,2,1,0:T(8,128)(2,1)S(1)}, bf16[8,2,64,128]{3,2,1,0:T(8,128)(2,1)S(1)}, u32[]{:S(2)}, u32[]{:S(2)}) collective-permute-start(bf16[8,2,64,128]{3,2,1,0:T(8,128)(2,1)S(1)} %get-tuple-element.91), channel_id=1, source_target_pairs={{0,2},{2,4},{4,6},{6,7},{7,5},{5,3},{3,1},{1,0},{8,10},{10,12},{12... | collective-permute-start | bytes 786440 | tf_op jit(solution)/shard_map/ppermute | solution.py:583
  38.1 6.4 %collective-permute-start.16 = (bf16[8,2,64,128]{3,2,1,0:T(8,128)(2,1)S(1)}, bf16[8,2,64,128]{3,2,1,0:T(8,128)(2,1)S(1)}, u32[]{:S(2)}, u32[]{:S(2)}) collective-permute-start(bf16[8,2,64,128]{3,2,1,0:T(8,128)(2,1)S(1)} %get-tuple-element.92), channel_id=1, source_target_pairs={{2,0},{4,2},{6,4},{7,6},{5,7},{3,5},{1,3},{0,1},{10,8},{12,10},{14... | collective-permute-start | bytes 786440 | tf_op jit(solution)/shard_map/ppermute | solution.py:583
  39.2 10.5 %collective-permute-start.14 = (bf16[2,2,64,128]{3,2,1,0:T(8,128)(2,1)S(1)}, bf16[2,2,64,128]{3,2,1,0:T(8,128)(2,1)S(1)}, u32[]{:S(2)}, u32[]{:S(2)}) collective-permute-start(bf16[2,2,64,128]{3,2,1,0:T(8,128)(2,1)S(1)} %get-tuple-element.125), channel_id=1, source_target_pairs={{8,0},{16,8},{24,16},{0,24},{9,1},{17,9},{25,17},{1,25},{10,2},{18... | collective-permute-start | bytes 196616 | tf_op jit(solution)/shard_map/ppermute | solution.py:593
  41.7 8.0 %collective-permute-start.13 = (bf16[2,2,64,128]{3,2,1,0:T(8,128)(2,1)S(1)}, bf16[2,2,64,128]{3,2,1,0:T(8,128)(2,1)S(1)}, u32[]{:S(2)}, u32[]{:S(2)}) collective-permute-start(bf16[2,2,64,128]{3,2,1,0:T(8,128)(2,1)S(1)} %get-tuple-element.126), channel_id=1, source_target_pairs={{0,8},{8,16},{16,24},{24,0},{1,9},{9,17},{17,25},{25,1},{2,10},{10... | collective-permute-start | bytes 196616 | tf_op jit(solution)/shard_map/ppermute | solution.py:592
  44.5 5.2 %collective-permute-start.17 = (bf16[2,2,64,128]{3,2,1,0:T(8,128)(2,1)S(1)}, bf16[2,2,64,128]{3,2,1,0:T(8,128)(2,1)S(1)}, u32[]{:S(2)}, u32[]{:S(2)}) collective-permute-start(bf16[2,2,64,128]{3,2,1,0:T(8,128)(2,1)S(1)} %pad_maximum_fusion.4), channel_id=1, source_target_pairs={{0,8},{8,16},{16,24},{24,0},{1,9},{9,17},{17,25},{25,1},{2,10},{10... | collective-permute-start | bytes 196616 | tf_op jit(solution)/shard_map/ppermute | solution.py:592
  52.3 6.2 %collective-permute-start.19 = (bf16[2,1,2,64,128]{4,3,2,1,0:T(8,128)(2,1)S(1)}, bf16[2,1,2,64,128]{4,3,2,1,0:T(8,128)(2,1)S(1)}, u32[]{:S(2)}, u32[]{:S(2)}) collective-permute-start(bf16[2,1,2,64,128]{4,3,2,1,0:T(8,128)(2,1)S(1)} %get-tuple-element.98), channel_id=1, source_target_pairs={{0,6},{2,4},{4,2},{6,0},{1,7},{3,5},{5,3},{7,1},{8,14},{10,12},{12... | collective-permute-start | bytes 196616 | tf_op jit(solution)/shard_map/ppermute | solution.py:603
  56.1 5.2 %collective-permute-start.20 = (bf16[2,1,2,64,128]{4,3,2,1,0:T(8,128)(2,1)S(1)}, bf16[2,1,2,64,128]{4,3,2,1,0:T(8,128)(2,1)S(1)}, u32[]{:S(2)}, u32[]{:S(2)}) collective-permute-start(bf16[2,1,2,64,128]{4,3,2,1,0:T(8,128)(2,1)S(1)} %get-tuple-element.99), channel_id=1, source_target_pairs={{0,4},{2,6},{4,0},{6,2},{1,5},{3,7},{5,1},{7,3},{8,12},{10,14},{12... | collective-permute-start | bytes 196616 | tf_op jit(solution)/shard_map/ppermute | solution.py:603
  56.1 5.2 %collective-permute-start.21 = (bf16[2,1,2,64,128]{4,3,2,1,0:T(8,128)(2,1)S(1)}, bf16[2,1,2,64,128]{4,3,2,1,0:T(8,128)(2,1)S(1)}, u32[]{:S(2)}, u32[]{:S(2)}) collective-permute-start(bf16[2,1,2,64,128]{4,3,2,1,0:T(8,128)(2,1)S(1)} %get-tuple-element.100), channel_id=1, source_target_pairs={{0,2},{2,0},{4,6},{6,4},{1,3},{3,1},{5,7},{7,5},{8,10},{10,8},{12,... | collective-permute-start | bytes 196616 | tf_op jit(solution)/shard_map/ppermute | solution.py:603
  62.3 7.8 %collective-permute-start.23 = (bf16[4,2,64,128]{3,2,1,0:T(8,128)(2,1)S(1)}, bf16[4,2,64,128]{3,2,1,0:T(8,128)(2,1)S(1)}, u32[]{:S(2)}, u32[]{:S(2)}) collective-permute-start(bf16[4,2,64,128]{3,2,1,0:T(8,128)(2,1)S(1)} %get-tuple-element.103), channel_id=1, source_target_pairs={{2,0},{4,2},{6,4},{8,6},{10,8},{12,10},{14,12},{16,14},{18,16},{20... | collective-permute-start | bytes 393224 | tf_op jit(solution)/shard_map/ppermute | solution.py:583
  70.9 6.1 %collective-permute-start.24 = (bf16[2,1,2,64,128]{4,3,2,1,0:T(8,128)(2,1)S(1)}, bf16[2,1,2,64,128]{4,3,2,1,0:T(8,128)(2,1)S(1)}, u32[]{:S(2)}, u32[]{:S(2)}) collective-permute-start(bf16[2,1,2,64,128]{4,3,2,1,0:T(8,128)(2,1)S(1)} %get-tuple-element.107), channel_id=1, source_target_pairs={{0,6},{2,4},{4,2},{6,0},{1,7},{3,5},{5,3},{7,1},{8,14},{10,12},{12... | collective-permute-start | bytes 196616 | tf_op jit(solution)/shard_map/ppermute | solution.py:603
  74.7 5.2 %collective-permute-start.25 = (bf16[2,1,2,64,128]{4,3,2,1,0:T(8,128)(2,1)S(1)}, bf16[2,1,2,64,128]{4,3,2,1,0:T(8,128)(2,1)S(1)}, u32[]{:S(2)}, u32[]{:S(2)}) collective-permute-start(bf16[2,1,2,64,128]{4,3,2,1,0:T(8,128)(2,1)S(1)} %get-tuple-element.108), channel_id=1, source_target_pairs={{0,4},{2,6},{4,0},{6,2},{1,5},{3,7},{5,1},{7,3},{8,12},{10,14},{12... | collective-permute-start | bytes 196616 | tf_op jit(solution)/shard_map/ppermute | solution.py:603
  74.7 5.2 %collective-permute-start.26 = (bf16[2,1,2,64,128]{4,3,2,1,0:T(8,128)(2,1)S(1)}, bf16[2,1,2,64,128]{4,3,2,1,0:T(8,128)(2,1)S(1)}, u32[]{:S(2)}, u32[]{:S(2)}) collective-permute-start(bf16[2,1,2,64,128]{4,3,2,1,0:T(8,128)(2,1)S(1)} %get-tuple-element.109), channel_id=1, source_target_pairs={{0,2},{2,0},{4,6},{6,4},{1,3},{3,1},{5,7},{7,5},{8,10},{10,8},{12,... | collective-permute-start | bytes 196616 | tf_op jit(solution)/shard_map/ppermute | solution.py:603
  (7 other events, 42.2 us)

commit v4 on v3

--- a/solution.py
+++ b/solution.py
@@ -299,9 +299,14 @@
         give_faces(ends.at[0], ends.at[size_y - 1], one_ref, two_ref, end * (size_x - 1))
 
 
-def round_kernel(start_ref, round_ref, one_ref, two_ref):
-    for x in range(start_ref.shape[0]):
-        cells = [[start_ref[x, y, z].astype(BF16) for z in range(2)] for y in range(start_ref.shape[1])]
+def round_kernel(start_ref, round_ref, one_ref, two_ref, held, arrived):
+    size_x, size_y = start_ref.shape[:2]
+    copies = [pltpu.make_async_copy(start_ref.at[x], held.at[x], arrived.at[x]) for x in range(size_x)]
+    for copy in copies:
+        copy.start()
+    for x, copy in enumerate(copies):
+        copy.wait()
+        cells = [[held[x, y, z].astype(BF16) for z in range(2)] for y in range(size_y)]
         for y, column in enumerate(cells):
             for z in range(2):
                 round_ref[x, y, z] = column[z]
@@ -309,17 +314,14 @@
 
 
 def round_start(start):
-    size_x, size_y, layers, width, loads = start.shape
-    batch = size_x // 4
-    side = pl.BlockSpec((batch, layers, width, loads), lambda i: (i, 0, 0, 0))
-    whole = pl.BlockSpec((batch, size_y, layers, width, loads), lambda i: (i, 0, 0, 0, 0))
+    size_x, _, layers, width, loads = start.shape
     face = jax.ShapeDtypeStruct((size_x, layers, width, loads), BF16)
     return pl.pallas_call(
         round_kernel,
-        grid=(4,),
-        in_specs=[whole],
-        out_specs=[whole, side, side],
+        in_specs=[pl.BlockSpec(memory_space=pltpu.HBM)],
+        out_specs=[VMEM] * 3,
         out_shape=[jax.ShapeDtypeStruct(start.shape, BF16), face, face],
+        scratch_shapes=[pltpu.VMEM(start.shape, F32), pltpu.SemaphoreType.DMA((size_x,))],
         compiler_params=pltpu.CompilerParams(vmem_limit_bytes=LIMIT),
         name="round_start",
     )(in_hbm(start))

time: 82.4 us -> 81.6 us (level)
  transfers between devices with their start and end apart: 27 -> 27, of which waited for: 15 -> 15; matrix products, arithmetic and copies ran while one was open for 0% -> 0% of each run, Pallas kernels for 21% -> 22%
where the time goes in v4:
time: 81.6 us; the launch traced here: 81.3 us
  starting transfers between devices  32.7 us (40%)
  waiting for transfers between devices  25.2 us (31%)
  Pallas kernels  22.8 us (28%)
    pallas_call x13, Pallas kernels, call(): pl.pallas_call(kernel, in_specs=[SMEM] * len(scalars) + [VMEM] * len(oper...  14.1 us
    ppermute x6, starting transfers between devices, swap_ends(): lax.ppermute(first, 'track', [((i + 1) % count, i) for i in range(count)])  9.93 us
    ppermute x6, waiting for transfers between devices, swap_pieces(): lax.ppermute(pieces[step], 'lateral', [(i, i ^ step) for i in range(count)])  9.11 us
    ppermute x6, starting transfers between devices, swap_pieces(): lax.ppermute(pieces[step], 'lateral', [(i, i ^ step) for i in range(count)])  8.92 us
    ppermute x4, starting transfers between devices, swap_round(): lax.ppermute(one, (*axes, 'depth'), onward)  7.28 us
    ppermute x6, starting transfers between devices, swap_ends(): lax.ppermute(last, 'track', [(i, (i + 1) % count) for i in range(count)])  6.49 us
    ppermute x4, waiting for transfers between devices, swap_round(): lax.ppermute(two, (*axes, 'depth'), back)  5.78 us
    pallas_call x1, Pallas kernels, sort_fine(): pl.pallas_call(fine_sort_kernel, in_specs=[SMEM, VMEM, pl.BlockSpec(memor...  4.38 us
  transfers between devices with their start and end apart: 27, of which 15 were waited for; matrix products, arithmetic and copies ran while one was open for 0% of the time, Pallas kernels for 22%

profile of v4, /device:TPU:0, one launch (start us, length us, event | category | flops | bytes accessed | tf_op | source)
XLA Modules:
  0.0 81.3 jit_solution(330342776215052620)
XLA Ops:
  1.4 3.0 %collective-permute-start = (bf16[8,2,64,128]{3,2,1,0:T(8,128)(2,1)S(1)}, bf16[8,2,64,128]{3,2,1,0:T(8,128)(2,1)S(1)}, u32[]{:S(2)}, u32[]{:S(2)}) collective-permute-start(bf16[8,2,64,128]{3,2,1,0:T(8,128)(2,1)S(1)} %get-tuple-element.63), channel_id=1, source_target_pairs={{0,2},{2,4},{4,6},{6,7},{7,5},{5,3},{3,1},{1,0},{8,10},{10,12},{12... | collective-permute-start | bytes 786440 | tf_op jit(solution)/shard_map/ppermute | solution.py:585
  4.4 4.4 %sort_fine.1.refs_0_.ops_ref = bf16[16,640,256]{2,1,0:T(8,128)(2,1)S(1)} custom-call(s32[32,27]{1,0:T(8,128)} %bitcast.55, bf16[16,2,64]{2,1,0:T(2,128)(2,1)} %bitcast.56, bf16[16,27,64,128]{3,2,1,0:T(8,128)(2,1)} %bitcast.49), custom_call_target="tpu_custom_call" | custom-call | tf_op jit(solution)/shard_map/sort_fine/pallas_call | solution.py:99
  9.9 2.5 %collective-permute-start.3 = (bf16[2,2,64,128]{3,2,1,0:T(8,128)(2,1)S(1)}, bf16[2,2,64,128]{3,2,1,0:T(8,128)(2,1)S(1)}, u32[]{:S(2)}, u32[]{:S(2)}) collective-permute-start(bf16[2,2,64,128]{3,2,1,0:T(8,128)(2,1)S(1)} %get-tuple-element.111), channel_id=1, source_target_pairs={{8,0},{16,8},{24,16},{0,24},{9,1},{17,9},{25,17},{1,25},{10,2},{18... | collective-permute-start | bytes 196616 | tf_op jit(solution)/shard_map/ppermute | solution.py:595
  12.5 2.0 %collective-permute-start.4 = (bf16[2,2,64,128]{3,2,1,0:T(8,128)(2,1)S(1)}, bf16[2,2,64,128]{3,2,1,0:T(8,128)(2,1)S(1)}, u32[]{:S(2)}, u32[]{:S(2)}) collective-permute-start(bf16[2,2,64,128]{3,2,1,0:T(8,128)(2,1)S(1)} %pad_maximum_fusion), channel_id=1, source_target_pairs={{0,8},{8,16},{16,24},{24,0},{1,9},{9,17},{17,25},{25,1},{2,10},{10... | collective-permute-start | bytes 196616 | tf_op jit(solution)/shard_map/ppermute | solution.py:594
  16.7 1.5 %collective-permute-done.2.before_ref = bf16[2,2,64,128]{3,2,1,0:T(8,128)(2,1)S(1)} collective-permute-done((bf16[2,2,64,128]{3,2,1,0:T(8,128)(2,1)S(1)}, bf16[2,2,64,128]{3,2,1,0:T(8,128)(2,1)S(1)}, u32[]{:S(2)}, u32[]{:S(2)}) %collective-permute-start.2) | collective-permute-done | bytes 65568 | tf_op jit(solution)/shard_map/ppermute | solution.py:594
  19.6 1.8 %collective-permute-start.6 = (bf16[8,2,64,128]{3,2,1,0:T(8,128)(2,1)S(1)}, bf16[8,2,64,128]{3,2,1,0:T(8,128)(2,1)S(1)}, u32[]{:S(2)}, u32[]{:S(2)}) collective-permute-start(bf16[8,2,64,128]{3,2,1,0:T(8,128)(2,1)S(1)} %get-tuple-element.74), channel_id=1, source_target_pairs={{0,2},{2,4},{4,6},{6,7},{7,5},{5,3},{3,1},{1,0},{8,10},{10,12},{12... | collective-permute-start | bytes 786440 | tf_op jit(solution)/shard_map/ppermute | solution.py:585
  22.6 2.1 %collective-permute-start.9 = (bf16[2,2,64,128]{3,2,1,0:T(8,128)(2,1)S(1)}, bf16[2,2,64,128]{3,2,1,0:T(8,128)(2,1)S(1)}, u32[]{:S(2)}, u32[]{:S(2)}) collective-permute-start(bf16[2,2,64,128]{3,2,1,0:T(8,128)(2,1)S(1)} %get-tuple-element.127), channel_id=1, source_target_pairs={{8,0},{16,8},{24,16},{0,24},{9,1},{17,9},{25,17},{1,25},{10,2},{18... | collective-permute-start | bytes 196616 | tf_op jit(solution)/shard_map/ppermute | solution.py:595
  24.7 3.0 %sort_coarse.1.own_ref.refs_0_ = bf16[8,320,256]{2,1,0:T(8,128)(2,1)S(1)} custom-call(s32[8,27]{1,0:T(8,128)} %bitcast.57, bf16[2,4,64]{2,1,0:T(4,128)(2,1)} %bitcast.58, bf16[2,128,128]{2,1,0:T(8,128)(2,1)} %bitcast.51, bf16[2,27,128,128]{3,2,1,0:T(8,128)(2,1)} %bitcast.50), custom_call_target="tpu_custom_call" | custom-call | tf_op jit(solution)/shard_map/sort_coarse/pallas_call | solution.py:117
  28.0 2.4 %collective-permute-start.10 = (bf16[2,2,64,128]{3,2,1,0:T(8,128)(2,1)S(1)}, bf16[2,2,64,128]{3,2,1,0:T(8,128)(2,1)S(1)}, u32[]{:S(2)}, u32[]{:S(2)}) collective-permute-start(bf16[2,2,64,128]{3,2,1,0:T(8,128)(2,1)S(1)} %pad_maximum_fusion.2), channel_id=1, source_target_pairs={{0,8},{8,16},{16,24},{24,0},{1,9},{9,17},{17,25},{25,1},{2,10},{10... | collective-permute-start | bytes 196616 | tf_op jit(solution)/shard_map/ppermute | solution.py:594
  32.2 1.4 %collective-permute-done.10.corner_before_ref = bf16[2,2,64,128]{3,2,1,0:T(8,128)(2,1)S(1)} collective-permute-done((bf16[2,2,64,128]{3,2,1,0:T(8,128)(2,1)S(1)}, bf16[2,2,64,128]{3,2,1,0:T(8,128)(2,1)S(1)}, u32[]{:S(2)}, u32[]{:S(2)}) %collective-permute-start.10) | collective-permute-done | bytes 65568 | tf_op jit(solution)/shard_map/ppermute | solution.py:594
  35.5 1.9 %collective-permute-start.15 = (bf16[8,2,64,128]{3,2,1,0:T(8,128)(2,1)S(1)}, bf16[8,2,64,128]{3,2,1,0:T(8,128)(2,1)S(1)}, u32[]{:S(2)}, u32[]{:S(2)}) collective-permute-start(bf16[8,2,64,128]{3,2,1,0:T(8,128)(2,1)S(1)} %get-tuple-element.91), channel_id=1, source_target_pairs={{0,2},{2,4},{4,6},{6,7},{7,5},{5,3},{3,1},{1,0},{8,10},{10,12},{12... | collective-permute-start | bytes 786440 | tf_op jit(solution)/shard_map/ppermute | solution.py:585
  38.5 2.7 %collective-permute-start.14 = (bf16[2,2,64,128]{3,2,1,0:T(8,128)(2,1)S(1)}, bf16[2,2,64,128]{3,2,1,0:T(8,128)(2,1)S(1)}, u32[]{:S(2)}, u32[]{:S(2)}) collective-permute-start(bf16[2,2,64,128]{3,2,1,0:T(8,128)(2,1)S(1)} %get-tuple-element.125), channel_id=1, source_target_pairs={{8,0},{16,8},{24,16},{0,24},{9,1},{17,9},{25,17},{1,25},{10,2},{18... | collective-permute-start | bytes 196616 | tf_op jit(solution)/shard_map/ppermute | solution.py:595
  41.1 1.5 %collective-permute-done.15.one_ref = bf16[8,2,64,128]{3,2,1,0:T(8,128)(2,1)S(1)} collective-permute-done((bf16[8,2,64,128]{3,2,1,0:T(8,128)(2,1)S(1)}, bf16[8,2,64,128]{3,2,1,0:T(8,128)(2,1)S(1)}, u32[]{:S(2)}, u32[]{:S(2)}) %collective-permute-start.15) | collective-permute-done | bytes 262176 | tf_op jit(solution)/shard_map/ppermute | solution.py:585
  43.8 2.1 %collective-permute-start.17 = (bf16[2,2,64,128]{3,2,1,0:T(8,128)(2,1)S(1)}, bf16[2,2,64,128]{3,2,1,0:T(8,128)(2,1)S(1)}, u32[]{:S(2)}, u32[]{:S(2)}) collective-permute-start(bf16[2,2,64,128]{3,2,1,0:T(8,128)(2,1)S(1)} %pad_maximum_fusion.4), channel_id=1, source_target_pairs={{0,8},{8,16},{16,24},{24,0},{1,9},{9,17},{17,25},{25,1},{2,10},{10... | collective-permute-start | bytes 196616 | tf_op jit(solution)/shard_map/ppermute | solution.py:594
  46.8 2.1 %restrict_inside.1 = (f32[2,2,2,64,128]{4,3,2,1,0:T(8,128)S(1)}, f32[8,1,2,64,128]{4,3,2,1,0:T(8,128)S(1)}) custom-call(s32[2,2,8]{2,1,0:T(2,128)} %bitcast.52, bf16[8,2,64,128]{3,2,1,0:T(8,128)(2,1)S(1)} %collective-permute-done.15.one_ref, bf16[8,2,64,128]{3,2,1,0:T(8,128)(2,1)S(1)} %collective-permute-done.16.two_ref, ...), custom_call_target="tpu_custom_call" | custom-call | tf_op jit(solution)/shard_map/restrict_inside/pallas_call | solution.py:569
  51.6 3.8 %collective-permute-start.19 = (bf16[2,1,2,64,128]{4,3,2,1,0:T(8,128)(2,1)S(1)}, bf16[2,1,2,64,128]{4,3,2,1,0:T(8,128)(2,1)S(1)}, u32[]{:S(2)}, u32[]{:S(2)}) collective-permute-start(bf16[2,1,2,64,128]{4,3,2,1,0:T(8,128)(2,1)S(1)} %get-tuple-element.98), channel_id=1, source_target_pairs={{0,6},{2,4},{4,2},{6,0},{1,7},{3,5},{5,3},{7,1},{8,14},{10,12},{12... | collective-permute-start | bytes 196616 | tf_op jit(solution)/shard_map/ppermute | solution.py:605
  56.0 1.8 %collective-permute-done.19.refs_0_ = bf16[2,1,2,64,128]{4,3,2,1,0:T(8,128)(2,1)S(1)} collective-permute-done((bf16[2,1,2,64,128]{4,3,2,1,0:T(8,128)(2,1)S(1)}, bf16[2,1,2,64,128]{4,3,2,1,0:T(8,128)(2,1)S(1)}, u32[]{:S(2)}, u32[]{:S(2)}) %collective-permute-start.19) | collective-permute-done | bytes 65568 | tf_op jit(solution)/shard_map/ppermute | solution.py:605
  57.8 2.8 %collective-permute-done.20.refs_1_ = bf16[2,1,2,64,128]{4,3,2,1,0:T(8,128)(2,1)S(1)} collective-permute-done((bf16[2,1,2,64,128]{4,3,2,1,0:T(8,128)(2,1)S(1)}, bf16[2,1,2,64,128]{4,3,2,1,0:T(8,128)(2,1)S(1)}, u32[]{:S(2)}, u32[]{:S(2)}) %collective-permute-start.20) | collective-permute-done | bytes 65568 | tf_op jit(solution)/shard_map/ppermute | solution.py:605
  62.2 2.6 %collective-permute-done.22.one_ref = bf16[4,2,64,128]{3,2,1,0:T(8,128)(2,1)S(1)} collective-permute-done((bf16[4,2,64,128]{3,2,1,0:T(8,128)(2,1)S(1)}, bf16[4,2,64,128]{3,2,1,0:T(8,128)(2,1)S(1)}, u32[]{:S(2)}, u32[]{:S(2)}) %collective-permute-start.22) | collective-permute-done | bytes 131104 | tf_op jit(solution)/shard_map/ppermute | solution.py:585
  64.8 4.5 %collective-permute-done.23.two_ref = bf16[4,2,64,128]{3,2,1,0:T(8,128)(2,1)S(1)} collective-permute-done((bf16[4,2,64,128]{3,2,1,0:T(8,128)(2,1)S(1)}, bf16[4,2,64,128]{3,2,1,0:T(8,128)(2,1)S(1)}, u32[]{:S(2)}, u32[]{:S(2)}) %collective-permute-start.23) | collective-permute-done | bytes 131104 | tf_op jit(solution)/shard_map/ppermute | solution.py:585
  70.2 3.8 %collective-permute-start.24 = (bf16[2,1,2,64,128]{4,3,2,1,0:T(8,128)(2,1)S(1)}, bf16[2,1,2,64,128]{4,3,2,1,0:T(8,128)(2,1)S(1)}, u32[]{:S(2)}, u32[]{:S(2)}) collective-permute-start(bf16[2,1,2,64,128]{4,3,2,1,0:T(8,128)(2,1)S(1)} %get-tuple-element.107), channel_id=1, source_target_pairs={{0,6},{2,4},{4,2},{6,0},{1,7},{3,5},{5,3},{7,1},{8,14},{10,12},{12... | collective-permute-start | bytes 196616 | tf_op jit(solution)/shard_map/ppermute | solution.py:605
  74.6 1.7 %collective-permute-done.24.refs_0_ = bf16[2,1,2,64,128]{4,3,2,1,0:T(8,128)(2,1)S(1)} collective-permute-done((bf16[2,1,2,64,128]{4,3,2,1,0:T(8,128)(2,1)S(1)}, bf16[2,1,2,64,128]{4,3,2,1,0:T(8,128)(2,1)S(1)}, u32[]{:S(2)}, u32[]{:S(2)}) %collective-permute-start.24) | collective-permute-done | bytes 65568 | tf_op jit(solution)/shard_map/ppermute | solution.py:605
  76.3 2.8 %collective-permute-done.25.refs_1_ = bf16[2,1,2,64,128]{4,3,2,1,0:T(8,128)(2,1)S(1)} collective-permute-done((bf16[2,1,2,64,128]{4,3,2,1,0:T(8,128)(2,1)S(1)}, bf16[2,1,2,64,128]{4,3,2,1,0:T(8,128)(2,1)S(1)}, u32[]{:S(2)}, u32[]{:S(2)}) %collective-permute-start.25) | collective-permute-done | bytes 65568 | tf_op jit(solution)/shard_map/ppermute | solution.py:605
  79.1 2.0 %prolong.1 = f32[8,2,2,64,128]{4,3,2,1,0:T(8,128)} custom-call(s32[2,2,8]{2,1,0:T(2,128)} %bitcast.54, bf16[16,64,128]{2,1,0:T(8,128)(2,1)S(1)} %bitcast.48, f32[8,2,2,64,128]{4,3,2,1,0:T(8,128)S(1)} %get-tuple-element.81.iterate_ref, f32[2,2,2,64,128]{4,3,2,1,0:T(8,128)S(1)} %get-tuple-element.86.ends_ref, ...), custom_call_target="tpu_custom_call" | custom-call | tf_op jit(solution)/shard_map/prolong/pallas_call | solution.py:569
  (68 shorter events, 20.6 us)
Async XLA Ops:
  1.4 11.1 %collective-permute-start = (bf16[8,2,64,128]{3,2,1,0:T(8,128)(2,1)S(1)}, bf16[8,2,64,128]{3,2,1,0:T(8,128)(2,1)S(1)}, u32[]{:S(2)}, u32[]{:S(2)}) collective-permute-start(bf16[8,2,64,128]{3,2,1,0:T(8,128)(2,1)S(1)} %get-tuple-element.63), channel_id=1, source_target_pairs={{0,2},{2,4},{4,6},{6,7},{7,5},{5,3},{3,1},{1,0},{8,10},{10,12},{12... | collective-permute-start | bytes 786440 | tf_op jit(solution)/shard_map/ppermute | solution.py:585
  4.4 8.0 %collective-permute-start.1 = (bf16[8,2,64,128]{3,2,1,0:T(8,128)(2,1)S(1)}, bf16[8,2,64,128]{3,2,1,0:T(8,128)(2,1)S(1)}, u32[]{:S(2)}, u32[]{:S(2)}) collective-permute-start(bf16[8,2,64,128]{3,2,1,0:T(8,128)(2,1)S(1)} %get-tuple-element.64), channel_id=1, source_target_pairs={{2,0},{4,2},{6,4},{7,6},{5,7},{3,5},{1,3},{0,1},{10,8},{12,10},{14... | collective-permute-start | bytes 786440 | tf_op jit(solution)/shard_map/ppermute | solution.py:585
  9.9 6.8 %collective-permute-start.3 = (bf16[2,2,64,128]{3,2,1,0:T(8,128)(2,1)S(1)}, bf16[2,2,64,128]{3,2,1,0:T(8,128)(2,1)S(1)}, u32[]{:S(2)}, u32[]{:S(2)}) collective-permute-start(bf16[2,2,64,128]{3,2,1,0:T(8,128)(2,1)S(1)} %get-tuple-element.111), channel_id=1, source_target_pairs={{8,0},{16,8},{24,16},{0,24},{9,1},{17,9},{25,17},{1,25},{10,2},{18... | collective-permute-start | bytes 196616 | tf_op jit(solution)/shard_map/ppermute | solution.py:595
  12.4 5.8 %collective-permute-start.2 = (bf16[2,2,64,128]{3,2,1,0:T(8,128)(2,1)S(1)}, bf16[2,2,64,128]{3,2,1,0:T(8,128)(2,1)S(1)}, u32[]{:S(2)}, u32[]{:S(2)}) collective-permute-start(bf16[2,2,64,128]{3,2,1,0:T(8,128)(2,1)S(1)} %get-tuple-element.112), channel_id=1, source_target_pairs={{0,8},{8,16},{16,24},{24,0},{1,9},{9,17},{17,25},{25,1},{2,10},{10... | collective-permute-start | bytes 196616 | tf_op jit(solution)/shard_map/ppermute | solution.py:594
  12.5 6.5 %collective-permute-start.4 = (bf16[2,2,64,128]{3,2,1,0:T(8,128)(2,1)S(1)}, bf16[2,2,64,128]{3,2,1,0:T(8,128)(2,1)S(1)}, u32[]{:S(2)}, u32[]{:S(2)}) collective-permute-start(bf16[2,2,64,128]{3,2,1,0:T(8,128)(2,1)S(1)} %pad_maximum_fusion), channel_id=1, source_target_pairs={{0,8},{8,16},{16,24},{24,0},{1,9},{9,17},{17,25},{25,1},{2,10},{10... | collective-permute-start | bytes 196616 | tf_op jit(solution)/shard_map/ppermute | solution.py:594
  19.6 8.1 %collective-permute-start.6 = (bf16[8,2,64,128]{3,2,1,0:T(8,128)(2,1)S(1)}, bf16[8,2,64,128]{3,2,1,0:T(8,128)(2,1)S(1)}, u32[]{:S(2)}, u32[]{:S(2)}) collective-permute-start(bf16[8,2,64,128]{3,2,1,0:T(8,128)(2,1)S(1)} %get-tuple-element.74), channel_id=1, source_target_pairs={{0,2},{2,4},{4,6},{6,7},{7,5},{5,3},{3,1},{1,0},{8,10},{10,12},{12... | collective-permute-start | bytes 786440 | tf_op jit(solution)/shard_map/ppermute | solution.py:585
  21.5 6.4 %collective-permute-start.7 = (bf16[8,2,64,128]{3,2,1,0:T(8,128)(2,1)S(1)}, bf16[8,2,64,128]{3,2,1,0:T(8,128)(2,1)S(1)}, u32[]{:S(2)}, u32[]{:S(2)}) collective-permute-start(bf16[8,2,64,128]{3,2,1,0:T(8,128)(2,1)S(1)} %get-tuple-element.75), channel_id=1, source_target_pairs={{2,0},{4,2},{6,4},{7,6},{5,7},{3,5},{1,3},{0,1},{10,8},{12,10},{14... | collective-permute-start | bytes 786440 | tf_op jit(solution)/shard_map/ppermute | solution.py:585
  22.6 9.6 %collective-permute-start.9 = (bf16[2,2,64,128]{3,2,1,0:T(8,128)(2,1)S(1)}, bf16[2,2,64,128]{3,2,1,0:T(8,128)(2,1)S(1)}, u32[]{:S(2)}, u32[]{:S(2)}) collective-permute-start(bf16[2,2,64,128]{3,2,1,0:T(8,128)(2,1)S(1)} %get-tuple-element.127), channel_id=1, source_target_pairs={{8,0},{16,8},{24,16},{0,24},{9,1},{17,9},{25,17},{1,25},{10,2},{18... | collective-permute-start | bytes 196616 | tf_op jit(solution)/shard_map/ppermute | solution.py:595
  24.7 7.5 %collective-permute-start.8 = (bf16[2,2,64,128]{3,2,1,0:T(8,128)(2,1)S(1)}, bf16[2,2,64,128]{3,2,1,0:T(8,128)(2,1)S(1)}, u32[]{:S(2)}, u32[]{:S(2)}) collective-permute-start(bf16[2,2,64,128]{3,2,1,0:T(8,128)(2,1)S(1)} %get-tuple-element.128), channel_id=1, source_target_pairs={{0,8},{8,16},{16,24},{24,0},{1,9},{9,17},{17,25},{25,1},{2,10},{10... | collective-permute-start | bytes 196616 | tf_op jit(solution)/shard_map/ppermute | solution.py:594
  27.9 32.8 %collective-permute-start.12 = (bf16[8,320,256]{2,1,0:T(8,128)(2,1)S(1)}, bf16[8,320,256]{2,1,0:T(8,128)(2,1)S(1)}, u32[]{:S(2)}, u32[]{:S(2)}) collective-permute-start(bf16[8,320,256]{2,1,0:T(8,128)(2,1)S(1)} %sort_coarse.1.own_ref.refs_0_), channel_id=1, source_target_pairs={{0,1},{1,0},{2,3},{3,2},{4,5},{5,4},{6,7},{7,6},{8,9},{9,8},{10,11... | collective-permute-start | bytes 3932168 | tf_op jit(solution)/shard_map/ppermute | solution.py:658
  28.0 5.6 %collective-permute-start.10 = (bf16[2,2,64,128]{3,2,1,0:T(8,128)(2,1)S(1)}, bf16[2,2,64,128]{3,2,1,0:T(8,128)(2,1)S(1)}, u32[]{:S(2)}, u32[]{:S(2)}) collective-permute-start(bf16[2,2,64,128]{3,2,1,0:T(8,128)(2,1)S(1)} %pad_maximum_fusion.2), channel_id=1, source_target_pairs={{0,8},{8,16},{16,24},{24,0},{1,9},{9,17},{17,25},{25,1},{2,10},{10... | collective-permute-start | bytes 196616 | tf_op jit(solution)/shard_map/ppermute | solution.py:594
  30.4 4.5 %collective-permute-start.11 = (bf16[2,2,64,128]{3,2,1,0:T(8,128)(2,1)S(1)}, bf16[2,2,64,128]{3,2,1,0:T(8,128)(2,1)S(1)}, u32[]{:S(2)}, u32[]{:S(2)}) collective-permute-start(bf16[2,2,64,128]{3,2,1,0:T(8,128)(2,1)S(1)} %pad_maximum_fusion.3), channel_id=1, source_target_pairs={{8,0},{16,8},{24,16},{0,24},{9,1},{17,9},{25,17},{1,25},{10,2},{18... | collective-permute-start | bytes 196616 | tf_op jit(solution)/shard_map/ppermute | solution.py:595
  35.5 7.1 %collective-permute-start.15 = (bf16[8,2,64,128]{3,2,1,0:T(8,128)(2,1)S(1)}, bf16[8,2,64,128]{3,2,1,0:T(8,128)(2,1)S(1)}, u32[]{:S(2)}, u32[]{:S(2)}) collective-permute-start(bf16[8,2,64,128]{3,2,1,0:T(8,128)(2,1)S(1)} %get-tuple-element.91), channel_id=1, source_target_pairs={{0,2},{2,4},{4,6},{6,7},{7,5},{5,3},{3,1},{1,0},{8,10},{10,12},{12... | collective-permute-start | bytes 786440 | tf_op jit(solution)/shard_map/ppermute | solution.py:585
  37.4 6.4 %collective-permute-start.16 = (bf16[8,2,64,128]{3,2,1,0:T(8,128)(2,1)S(1)}, bf16[8,2,64,128]{3,2,1,0:T(8,128)(2,1)S(1)}, u32[]{:S(2)}, u32[]{:S(2)}) collective-permute-start(bf16[8,2,64,128]{3,2,1,0:T(8,128)(2,1)S(1)} %get-tuple-element.92), channel_id=1, source_target_pairs={{2,0},{4,2},{6,4},{7,6},{5,7},{3,5},{1,3},{0,1},{10,8},{12,10},{14... | collective-permute-start | bytes 786440 | tf_op jit(solution)/shard_map/ppermute | solution.py:585
  38.5 10.5 %collective-permute-start.14 = (bf16[2,2,64,128]{3,2,1,0:T(8,128)(2,1)S(1)}, bf16[2,2,64,128]{3,2,1,0:T(8,128)(2,1)S(1)}, u32[]{:S(2)}, u32[]{:S(2)}) collective-permute-start(bf16[2,2,64,128]{3,2,1,0:T(8,128)(2,1)S(1)} %get-tuple-element.125), channel_id=1, source_target_pairs={{8,0},{16,8},{24,16},{0,24},{9,1},{17,9},{25,17},{1,25},{10,2},{18... | collective-permute-start | bytes 196616 | tf_op jit(solution)/shard_map/ppermute | solution.py:595
  41.1 7.8 %collective-permute-start.13 = (bf16[2,2,64,128]{3,2,1,0:T(8,128)(2,1)S(1)}, bf16[2,2,64,128]{3,2,1,0:T(8,128)(2,1)S(1)}, u32[]{:S(2)}, u32[]{:S(2)}) collective-permute-start(bf16[2,2,64,128]{3,2,1,0:T(8,128)(2,1)S(1)} %get-tuple-element.126), channel_id=1, source_target_pairs={{0,8},{8,16},{16,24},{24,0},{1,9},{9,17},{17,25},{25,1},{2,10},{10... | collective-permute-start | bytes 196616 | tf_op jit(solution)/shard_map/ppermute | solution.py:594
  43.8 5.2 %collective-permute-start.17 = (bf16[2,2,64,128]{3,2,1,0:T(8,128)(2,1)S(1)}, bf16[2,2,64,128]{3,2,1,0:T(8,128)(2,1)S(1)}, u32[]{:S(2)}, u32[]{:S(2)}) collective-permute-start(bf16[2,2,64,128]{3,2,1,0:T(8,128)(2,1)S(1)} %pad_maximum_fusion.4), channel_id=1, source_target_pairs={{0,8},{8,16},{16,24},{24,0},{1,9},{9,17},{17,25},{25,1},{2,10},{10... | collective-permute-start | bytes 196616 | tf_op jit(solution)/shard_map/ppermute | solution.py:594
  51.6 6.2 %collective-permute-start.19 = (bf16[2,1,2,64,128]{4,3,2,1,0:T(8,128)(2,1)S(1)}, bf16[2,1,2,64,128]{4,3,2,1,0:T(8,128)(2,1)S(1)}, u32[]{:S(2)}, u32[]{:S(2)}) collective-permute-start(bf16[2,1,2,64,128]{4,3,2,1,0:T(8,128)(2,1)S(1)} %get-tuple-element.98), channel_id=1, source_target_pairs={{0,6},{2,4},{4,2},{6,0},{1,7},{3,5},{5,3},{7,1},{8,14},{10,12},{12... | collective-permute-start | bytes 196616 | tf_op jit(solution)/shard_map/ppermute | solution.py:605
  55.4 5.2 %collective-permute-start.20 = (bf16[2,1,2,64,128]{4,3,2,1,0:T(8,128)(2,1)S(1)}, bf16[2,1,2,64,128]{4,3,2,1,0:T(8,128)(2,1)S(1)}, u32[]{:S(2)}, u32[]{:S(2)}) collective-permute-start(bf16[2,1,2,64,128]{4,3,2,1,0:T(8,128)(2,1)S(1)} %get-tuple-element.99), channel_id=1, source_target_pairs={{0,4},{2,6},{4,0},{6,2},{1,5},{3,7},{5,1},{7,3},{8,12},{10,14},{12... | collective-permute-start | bytes 196616 | tf_op jit(solution)/shard_map/ppermute | solution.py:605
  55.4 5.2 %collective-permute-start.21 = (bf16[2,1,2,64,128]{4,3,2,1,0:T(8,128)(2,1)S(1)}, bf16[2,1,2,64,128]{4,3,2,1,0:T(8,128)(2,1)S(1)}, u32[]{:S(2)}, u32[]{:S(2)}) collective-permute-start(bf16[2,1,2,64,128]{4,3,2,1,0:T(8,128)(2,1)S(1)} %get-tuple-element.100), channel_id=1, source_target_pairs={{0,2},{2,0},{4,6},{6,4},{1,3},{3,1},{5,7},{7,5},{8,10},{10,8},{12,... | collective-permute-start | bytes 196616 | tf_op jit(solution)/shard_map/ppermute | solution.py:605
  61.6 7.8 %collective-permute-start.23 = (bf16[4,2,64,128]{3,2,1,0:T(8,128)(2,1)S(1)}, bf16[4,2,64,128]{3,2,1,0:T(8,128)(2,1)S(1)}, u32[]{:S(2)}, u32[]{:S(2)}) collective-permute-start(bf16[4,2,64,128]{3,2,1,0:T(8,128)(2,1)S(1)} %get-tuple-element.103), channel_id=1, source_target_pairs={{2,0},{4,2},{6,4},{8,6},{10,8},{12,10},{14,12},{16,14},{18,16},{20... | collective-permute-start | bytes 393224 | tf_op jit(solution)/shard_map/ppermute | solution.py:585
  70.2 6.1 %collective-permute-start.24 = (bf16[2,1,2,64,128]{4,3,2,1,0:T(8,128)(2,1)S(1)}, bf16[2,1,2,64,128]{4,3,2,1,0:T(8,128)(2,1)S(1)}, u32[]{:S(2)}, u32[]{:S(2)}) collective-permute-start(bf16[2,1,2,64,128]{4,3,2,1,0:T(8,128)(2,1)S(1)} %get-tuple-element.107), channel_id=1, source_target_pairs={{0,6},{2,4},{4,2},{6,0},{1,7},{3,5},{5,3},{7,1},{8,14},{10,12},{12... | collective-permute-start | bytes 196616 | tf_op jit(solution)/shard_map/ppermute | solution.py:605
  74.0 5.2 %collective-permute-start.25 = (bf16[2,1,2,64,128]{4,3,2,1,0:T(8,128)(2,1)S(1)}, bf16[2,1,2,64,128]{4,3,2,1,0:T(8,128)(2,1)S(1)}, u32[]{:S(2)}, u32[]{:S(2)}) collective-permute-start(bf16[2,1,2,64,128]{4,3,2,1,0:T(8,128)(2,1)S(1)} %get-tuple-element.108), channel_id=1, source_target_pairs={{0,4},{2,6},{4,0},{6,2},{1,5},{3,7},{5,1},{7,3},{8,12},{10,14},{12... | collective-permute-start | bytes 196616 | tf_op jit(solution)/shard_map/ppermute | solution.py:605
  74.0 5.2 %collective-permute-start.26 = (bf16[2,1,2,64,128]{4,3,2,1,0:T(8,128)(2,1)S(1)}, bf16[2,1,2,64,128]{4,3,2,1,0:T(8,128)(2,1)S(1)}, u32[]{:S(2)}, u32[]{:S(2)}) collective-permute-start(bf16[2,1,2,64,128]{4,3,2,1,0:T(8,128)(2,1)S(1)} %get-tuple-element.109), channel_id=1, source_target_pairs={{0,2},{2,0},{4,6},{6,4},{1,3},{3,1},{5,7},{7,5},{8,10},{10,8},{12,... | collective-permute-start | bytes 196616 | tf_op jit(solution)/shard_map/ppermute | solution.py:605
  (7 other events, 42.1 us)

commit v5 on v4

--- a/solution.py
+++ b/solution.py
@@ -337,6 +337,8 @@
         place = (odd if near < 0 else 1 - odd) if corner else near
         for end, inside in ((0, at > 0), (1, at < count - 1)):
             cells = given_refs[2 * corner + end][place]
+            if not corner:
+                cells = jnp.where(odd == end, given_refs[0][place], given_refs[1][place])
             cells = jnp.where(inside, cells, jnp.zeros_like(cells))
             if corner:
                 cells = inside_track(cells, near < 0)
@@ -596,6 +598,11 @@
     return before, after
 
 
+def swap_tips(last, first):
+    even = lax.axis_index("depth") % 2 == 0
+    return swap_round(jnp.where(even, last, first), jnp.where(even, first, last), ("track",))
+
+
 def swap_corners(one, two):
     return swap_ends(jnp.concatenate([one[-1:], two[-1:]], axis=0), jnp.concatenate([one[:1], two[:1]], axis=0))
 
@@ -650,7 +657,7 @@
     for sweep in range(SWEEPS + 1):
         inner = inner_of(rounded, tips, [fine_ops], Fine)
         inner, tips = lax.optimization_barrier((inner, tips))
-        near = swap_ends(tips[-1], tips[0])
+        near = swap_tips(tips[-1], tips[0])
         if sweep == 1:
             coarse_cols, inner = lax.optimization_barrier((coarse_cols, inner))
             own_ops = sort_coarse(coarse_blocks, coarse_cols, coarse_mass, coarse_smoother)

time: 81.6 us -> 81.8 us (level)
  starting transfers between devices: 32.7 us -> 34.9 us
  waiting for transfers between devices: 25.2 us -> 23.2 us
    ppermute x6 -> x3, starting transfers between devices: 9.93 us -> 3.1 us  [swap_ends(): lax.ppermute(first, 'track', [((i + 1) % count, i) for i in range(count)])]
    ppermute x4 -> x7, starting transfers between devices: 7.28 us -> 13.3 us  [swap_round(): lax.ppermute(one, (*axes, 'depth'), onward)]
    ppermute x6, starting transfers between devices: 8.92 us -> 12.1 us  [swap_pieces(): lax.ppermute(pieces[step], 'lateral', [(i, i ^ step) for i in range(count)])]
    ppermute x4 -> x7, waiting for transfers between devices: 5.78 us -> 4.28 us  [swap_round(): lax.ppermute(two, (*axes, 'depth'), back)]
    ppermute x6 -> x3, starting transfers between devices: 6.49 us -> 5.97 us  [swap_ends(): lax.ppermute(last, 'track', [(i, (i + 1) % count) for i in range(count)])]
    ppermute x6 -> x3, waiting for transfers between devices: 3.69 us -> 3.33 us  [swap_ends(): lax.ppermute(last, 'track', [(i, (i + 1) % count) for i in range(count)])]
    ppermute x6 -> x3, waiting for transfers between devices: 2.49 us -> 2.36 us  [swap_ends(): lax.ppermute(first, 'track', [((i + 1) % count, i) for i in range(count)])]
    ppermute x4 -> x7, waiting for transfers between devices: 4.12 us -> 4.16 us  [swap_round(): lax.ppermute(one, (*axes, 'depth'), onward)]
where the time goes in v5:
time: 81.8 us; the launch traced here: 81.5 us
  starting transfers between devices  34.9 us (43%)
  waiting for transfers between devices  23.2 us (28%)
  Pallas kernels  22.8 us (28%)
    pallas_call x13, Pallas kernels, call(): pl.pallas_call(kernel, in_specs=[SMEM] * len(scalars) + [VMEM] * len(oper...  14 us
    ppermute x7, starting transfers between devices, swap_round(): lax.ppermute(one, (*axes, 'depth'), onward)  13.3 us
    ppermute x6, starting transfers between devices, swap_pieces(): lax.ppermute(pieces[step], 'lateral', [(i, i ^ step) for i in range(count)])  12.1 us
    ppermute x6, waiting for transfers between devices, swap_pieces(): lax.ppermute(pieces[step], 'lateral', [(i, i ^ step) for i in range(count)])  9.05 us
    ppermute x3, starting transfers between devices, swap_ends(): lax.ppermute(last, 'track', [(i, (i + 1) % count) for i in range(count)])  5.97 us
    pallas_call x1, Pallas kernels, sort_fine(): pl.pallas_call(fine_sort_kernel, in_specs=[SMEM, VMEM, pl.BlockSpec(memor...  4.38 us
    ppermute x7, waiting for transfers between devices, swap_round(): lax.ppermute(two, (*axes, 'depth'), back)  4.28 us
    ppermute x7, waiting for transfers between devices, swap_round(): lax.ppermute(one, (*axes, 'depth'), onward)  4.16 us
  transfers between devices with their start and end apart: 27, of which 15 were waited for; matrix products, arithmetic and copies ran while one was open for 0% of the time, Pallas kernels for 22%

profile of v5, /device:TPU:0, one launch (start us, length us, event | category | flops | bytes accessed | tf_op | source)
XLA Modules:
  0.0 81.5 jit_solution(18050829556495419697)
XLA Ops:
  1.4 3.0 %collective-permute-start = (bf16[8,2,64,128]{3,2,1,0:T(8,128)(2,1)S(1)}, bf16[8,2,64,128]{3,2,1,0:T(8,128)(2,1)S(1)}, u32[]{:S(2)}, u32[]{:S(2)}) collective-permute-start(bf16[8,2,64,128]{3,2,1,0:T(8,128)(2,1)S(1)} %get-tuple-element.63), channel_id=1, source_target_pairs={{0,2},{2,4},{4,6},{6,7},{7,5},{5,3},{3,1},{1,0},{8,10},{10,12},{12... | collective-permute-start | bytes 786440 | tf_op jit(solution)/shard_map/ppermute | solution.py:587
  4.4 4.4 %sort_fine.1.refs_0_.ops_ref = bf16[16,640,256]{2,1,0:T(8,128)(2,1)S(1)} custom-call(s32[32,27]{1,0:T(8,128)} %bitcast.55, bf16[16,2,64]{2,1,0:T(2,128)(2,1)} %bitcast.56, bf16[16,27,64,128]{3,2,1,0:T(8,128)(2,1)} %bitcast.49), custom_call_target="tpu_custom_call" | custom-call | tf_op jit(solution)/shard_map/sort_fine/pallas_call | solution.py:99
  10.0 2.0 %collective-permute-start.2 = (bf16[2,2,64,128]{3,2,1,0:T(8,128)(2,1)S(1)}, bf16[2,2,64,128]{3,2,1,0:T(8,128)(2,1)S(1)}, u32[]{:S(2)}, u32[]{:S(2)}) collective-permute-start(bf16[2,2,64,128]{3,2,1,0:T(8,128)(2,1)S(1)} %get-tuple-element.112), channel_id=1, source_target_pairs={{0,8},{8,16},{16,24},{24,25},{25,17},{17,9},{9,1},{1,0},{2,10},{10... | collective-permute-start | bytes 196616 | tf_op jit(solution)/shard_map/ppermute | solution.py:587
  12.1 2.4 %collective-permute-start.4 = (bf16[2,2,64,128]{3,2,1,0:T(8,128)(2,1)S(1)}, bf16[2,2,64,128]{3,2,1,0:T(8,128)(2,1)S(1)}, u32[]{:S(2)}, u32[]{:S(2)}) collective-permute-start(bf16[2,2,64,128]{3,2,1,0:T(8,128)(2,1)S(1)} %pad_maximum_fusion), channel_id=1, source_target_pairs={{0,8},{8,16},{16,24},{24,0},{1,9},{9,17},{17,25},{25,1},{2,10},{10... | collective-permute-start | bytes 196616 | tf_op jit(solution)/shard_map/ppermute | solution.py:596
  16.3 1.7 %collective-permute-done.4.corner_before_ref = bf16[2,2,64,128]{3,2,1,0:T(8,128)(2,1)S(1)} collective-permute-done((bf16[2,2,64,128]{3,2,1,0:T(8,128)(2,1)S(1)}, bf16[2,2,64,128]{3,2,1,0:T(8,128)(2,1)S(1)}, u32[]{:S(2)}, u32[]{:S(2)}) %collective-permute-start.4) | collective-permute-done | bytes 65568 | tf_op jit(solution)/shard_map/ppermute | solution.py:596
  19.9 1.6 %collective-permute-start.6 = (bf16[8,2,64,128]{3,2,1,0:T(8,128)(2,1)S(1)}, bf16[8,2,64,128]{3,2,1,0:T(8,128)(2,1)S(1)}, u32[]{:S(2)}, u32[]{:S(2)}) collective-permute-start(bf16[8,2,64,128]{3,2,1,0:T(8,128)(2,1)S(1)} %get-tuple-element.74), channel_id=1, source_target_pairs={{0,2},{2,4},{4,6},{6,7},{7,5},{5,3},{3,1},{1,0},{8,10},{10,12},{12... | collective-permute-start | bytes 786440 | tf_op jit(solution)/shard_map/ppermute | solution.py:587
  22.7 2.0 %collective-permute-start.8 = (bf16[2,2,64,128]{3,2,1,0:T(8,128)(2,1)S(1)}, bf16[2,2,64,128]{3,2,1,0:T(8,128)(2,1)S(1)}, u32[]{:S(2)}, u32[]{:S(2)}) collective-permute-start(bf16[2,2,64,128]{3,2,1,0:T(8,128)(2,1)S(1)} %get-tuple-element.128), channel_id=1, source_target_pairs={{0,8},{8,16},{16,24},{24,25},{25,17},{17,9},{9,1},{1,0},{2,10},{10... | collective-permute-start | bytes 196616 | tf_op jit(solution)/shard_map/ppermute | solution.py:587
  24.7 3.0 %sort_coarse.1.own_ref.refs_0_ = bf16[8,320,256]{2,1,0:T(8,128)(2,1)S(1)} custom-call(s32[8,27]{1,0:T(8,128)} %bitcast.57, bf16[2,4,64]{2,1,0:T(4,128)(2,1)} %bitcast.58, bf16[2,128,128]{2,1,0:T(8,128)(2,1)} %bitcast.51, bf16[2,27,128,128]{3,2,1,0:T(8,128)(2,1)} %bitcast.50), custom_call_target="tpu_custom_call" | custom-call | tf_op jit(solution)/shard_map/sort_coarse/pallas_call | solution.py:117
  28.0 2.3 %collective-permute-start.10 = (bf16[2,2,64,128]{3,2,1,0:T(8,128)(2,1)S(1)}, bf16[2,2,64,128]{3,2,1,0:T(8,128)(2,1)S(1)}, u32[]{:S(2)}, u32[]{:S(2)}) collective-permute-start(bf16[2,2,64,128]{3,2,1,0:T(8,128)(2,1)S(1)} %pad_maximum_fusion.2), channel_id=1, source_target_pairs={{0,8},{8,16},{16,24},{24,0},{1,9},{9,17},{17,25},{25,1},{2,10},{10... | collective-permute-start | bytes 196616 | tf_op jit(solution)/shard_map/ppermute | solution.py:596
  32.2 1.6 %collective-permute-done.10.corner_before_ref = bf16[2,2,64,128]{3,2,1,0:T(8,128)(2,1)S(1)} collective-permute-done((bf16[2,2,64,128]{3,2,1,0:T(8,128)(2,1)S(1)}, bf16[2,2,64,128]{3,2,1,0:T(8,128)(2,1)S(1)}, u32[]{:S(2)}, u32[]{:S(2)}) %collective-permute-start.10) | collective-permute-done | bytes 65568 | tf_op jit(solution)/shard_map/ppermute | solution.py:596
  35.3 2.0 %collective-permute-start.15 = (bf16[8,2,64,128]{3,2,1,0:T(8,128)(2,1)S(1)}, bf16[8,2,64,128]{3,2,1,0:T(8,128)(2,1)S(1)}, u32[]{:S(2)}, u32[]{:S(2)}) collective-permute-start(bf16[8,2,64,128]{3,2,1,0:T(8,128)(2,1)S(1)} %get-tuple-element.91), channel_id=1, source_target_pairs={{0,2},{2,4},{4,6},{6,7},{7,5},{5,3},{3,1},{1,0},{8,10},{10,12},{12... | collective-permute-start | bytes 786440 | tf_op jit(solution)/shard_map/ppermute | solution.py:587
  38.6 2.0 %collective-permute-start.13 = (bf16[2,2,64,128]{3,2,1,0:T(8,128)(2,1)S(1)}, bf16[2,2,64,128]{3,2,1,0:T(8,128)(2,1)S(1)}, u32[]{:S(2)}, u32[]{:S(2)}) collective-permute-start(bf16[2,2,64,128]{3,2,1,0:T(8,128)(2,1)S(1)} %get-tuple-element.126), channel_id=1, source_target_pairs={{0,8},{8,16},{16,24},{24,25},{25,17},{17,9},{9,1},{1,0},{2,10},{10... | collective-permute-start | bytes 196616 | tf_op jit(solution)/shard_map/ppermute | solution.py:587
  40.7 1.5 %collective-permute-done.15.one_ref = bf16[8,2,64,128]{3,2,1,0:T(8,128)(2,1)S(1)} collective-permute-done((bf16[8,2,64,128]{3,2,1,0:T(8,128)(2,1)S(1)}, bf16[8,2,64,128]{3,2,1,0:T(8,128)(2,1)S(1)}, u32[]{:S(2)}, u32[]{:S(2)}) %collective-permute-start.15) | collective-permute-done | bytes 262176 | tf_op jit(solution)/shard_map/ppermute | solution.py:587
  44.9 1.8 %collective-permute-start.18 = (bf16[2,2,64,128]{3,2,1,0:T(8,128)(2,1)S(1)}, bf16[2,2,64,128]{3,2,1,0:T(8,128)(2,1)S(1)}, u32[]{:S(2)}, u32[]{:S(2)}) collective-permute-start(bf16[2,2,64,128]{3,2,1,0:T(8,128)(2,1)S(1)} %pad_maximum_fusion.5), channel_id=1, source_target_pairs={{8,0},{16,8},{24,16},{0,24},{9,1},{17,9},{25,17},{1,25},{10,2},{18... | collective-permute-start | bytes 196616 | tf_op jit(solution)/shard_map/ppermute | solution.py:597
  46.7 2.1 %restrict_inside.1 = (f32[2,2,2,64,128]{4,3,2,1,0:T(8,128)S(1)}, f32[8,1,2,64,128]{4,3,2,1,0:T(8,128)S(1)}) custom-call(s32[2,2,8]{2,1,0:T(2,128)} %bitcast.52, bf16[8,2,64,128]{3,2,1,0:T(8,128)(2,1)S(1)} %collective-permute-done.15.one_ref, bf16[8,2,64,128]{3,2,1,0:T(8,128)(2,1)S(1)} %collective-permute-done.16.two_ref, ...), custom_call_target="tpu_custom_call" | custom-call | tf_op jit(solution)/shard_map/restrict_inside/pallas_call | solution.py:571
  50.6 3.8 %collective-permute-start.19 = (bf16[2,1,2,64,128]{4,3,2,1,0:T(8,128)(2,1)S(1)}, bf16[2,1,2,64,128]{4,3,2,1,0:T(8,128)(2,1)S(1)}, u32[]{:S(2)}, u32[]{:S(2)}) collective-permute-start(bf16[2,1,2,64,128]{4,3,2,1,0:T(8,128)(2,1)S(1)} %get-tuple-element.98), channel_id=1, source_target_pairs={{0,6},{2,4},{4,2},{6,0},{1,7},{3,5},{5,3},{7,1},{8,14},{10,12},{12... | collective-permute-start | bytes 196616 | tf_op jit(solution)/shard_map/ppermute | solution.py:612
  55.0 1.8 %collective-permute-done.19.refs_0_ = bf16[2,1,2,64,128]{4,3,2,1,0:T(8,128)(2,1)S(1)} collective-permute-done((bf16[2,1,2,64,128]{4,3,2,1,0:T(8,128)(2,1)S(1)}, bf16[2,1,2,64,128]{4,3,2,1,0:T(8,128)(2,1)S(1)}, u32[]{:S(2)}, u32[]{:S(2)}) %collective-permute-start.19) | collective-permute-done | bytes 65568 | tf_op jit(solution)/shard_map/ppermute | solution.py:612
  56.8 2.8 %collective-permute-done.20.refs_1_ = bf16[2,1,2,64,128]{4,3,2,1,0:T(8,128)(2,1)S(1)} collective-permute-done((bf16[2,1,2,64,128]{4,3,2,1,0:T(8,128)(2,1)S(1)}, bf16[2,1,2,64,128]{4,3,2,1,0:T(8,128)(2,1)S(1)}, u32[]{:S(2)}, u32[]{:S(2)}) %collective-permute-start.20) | collective-permute-done | bytes 65568 | tf_op jit(solution)/shard_map/ppermute | solution.py:612
  61.2 2.6 %collective-permute-done.22.one_ref = bf16[4,2,64,128]{3,2,1,0:T(8,128)(2,1)S(1)} collective-permute-done((bf16[4,2,64,128]{3,2,1,0:T(8,128)(2,1)S(1)}, bf16[4,2,64,128]{3,2,1,0:T(8,128)(2,1)S(1)}, u32[]{:S(2)}, u32[]{:S(2)}) %collective-permute-start.22) | collective-permute-done | bytes 131104 | tf_op jit(solution)/shard_map/ppermute | solution.py:587
  63.8 2.6 %collective-permute-done.23.two_ref = bf16[4,2,64,128]{3,2,1,0:T(8,128)(2,1)S(1)} collective-permute-done((bf16[4,2,64,128]{3,2,1,0:T(8,128)(2,1)S(1)}, bf16[4,2,64,128]{3,2,1,0:T(8,128)(2,1)S(1)}, u32[]{:S(2)}, u32[]{:S(2)}) %collective-permute-start.23) | collective-permute-done | bytes 131104 | tf_op jit(solution)/shard_map/ppermute | solution.py:587
  67.2 7.0 %collective-permute-start.24 = (bf16[2,1,2,64,128]{4,3,2,1,0:T(8,128)(2,1)S(1)}, bf16[2,1,2,64,128]{4,3,2,1,0:T(8,128)(2,1)S(1)}, u32[]{:S(2)}, u32[]{:S(2)}) collective-permute-start(bf16[2,1,2,64,128]{4,3,2,1,0:T(8,128)(2,1)S(1)} %get-tuple-element.107), channel_id=1, source_target_pairs={{0,6},{2,4},{4,2},{6,0},{1,7},{3,5},{5,3},{7,1},{8,14},{10,12},{12... | collective-permute-start | bytes 196616 | tf_op jit(solution)/shard_map/ppermute | solution.py:612
  74.8 1.6 %collective-permute-done.24.refs_0_ = bf16[2,1,2,64,128]{4,3,2,1,0:T(8,128)(2,1)S(1)} collective-permute-done((bf16[2,1,2,64,128]{4,3,2,1,0:T(8,128)(2,1)S(1)}, bf16[2,1,2,64,128]{4,3,2,1,0:T(8,128)(2,1)S(1)}, u32[]{:S(2)}, u32[]{:S(2)}) %collective-permute-start.24) | collective-permute-done | bytes 65568 | tf_op jit(solution)/shard_map/ppermute | solution.py:612
  76.4 2.9 %collective-permute-done.25.refs_1_ = bf16[2,1,2,64,128]{4,3,2,1,0:T(8,128)(2,1)S(1)} collective-permute-done((bf16[2,1,2,64,128]{4,3,2,1,0:T(8,128)(2,1)S(1)}, bf16[2,1,2,64,128]{4,3,2,1,0:T(8,128)(2,1)S(1)}, u32[]{:S(2)}, u32[]{:S(2)}) %collective-permute-start.25) | collective-permute-done | bytes 65568 | tf_op jit(solution)/shard_map/ppermute | solution.py:612
  79.3 2.0 %prolong.1 = f32[8,2,2,64,128]{4,3,2,1,0:T(8,128)} custom-call(s32[2,2,8]{2,1,0:T(2,128)} %bitcast.54, bf16[16,64,128]{2,1,0:T(8,128)(2,1)S(1)} %bitcast.48, f32[8,2,2,64,128]{4,3,2,1,0:T(8,128)S(1)} %get-tuple-element.81.iterate_ref, f32[2,2,2,64,128]{4,3,2,1,0:T(8,128)S(1)} %get-tuple-element.86.ends_ref, ...), custom_call_target="tpu_custom_call" | custom-call | tf_op jit(solution)/shard_map/prolong/pallas_call | solution.py:571
  (68 shorter events, 20.3 us)
Async XLA Ops:
  1.4 10.6 %collective-permute-start = (bf16[8,2,64,128]{3,2,1,0:T(8,128)(2,1)S(1)}, bf16[8,2,64,128]{3,2,1,0:T(8,128)(2,1)S(1)}, u32[]{:S(2)}, u32[]{:S(2)}) collective-permute-start(bf16[8,2,64,128]{3,2,1,0:T(8,128)(2,1)S(1)} %get-tuple-element.63), channel_id=1, source_target_pairs={{0,2},{2,4},{4,6},{6,7},{7,5},{5,3},{3,1},{1,0},{8,10},{10,12},{12... | collective-permute-start | bytes 786440 | tf_op jit(solution)/shard_map/ppermute | solution.py:587
  4.4 7.6 %collective-permute-start.1 = (bf16[8,2,64,128]{3,2,1,0:T(8,128)(2,1)S(1)}, bf16[8,2,64,128]{3,2,1,0:T(8,128)(2,1)S(1)}, u32[]{:S(2)}, u32[]{:S(2)}) collective-permute-start(bf16[8,2,64,128]{3,2,1,0:T(8,128)(2,1)S(1)} %get-tuple-element.64), channel_id=1, source_target_pairs={{2,0},{4,2},{6,4},{7,6},{5,7},{3,5},{1,3},{0,1},{10,8},{12,10},{14... | collective-permute-start | bytes 786440 | tf_op jit(solution)/shard_map/ppermute | solution.py:587
  9.9 6.4 %collective-permute-start.3 = (bf16[2,2,64,128]{3,2,1,0:T(8,128)(2,1)S(1)}, bf16[2,2,64,128]{3,2,1,0:T(8,128)(2,1)S(1)}, u32[]{:S(2)}, u32[]{:S(2)}) collective-permute-start(bf16[2,2,64,128]{3,2,1,0:T(8,128)(2,1)S(1)} %get-tuple-element.111), channel_id=1, source_target_pairs={{8,0},{16,8},{24,16},{25,24},{17,25},{9,17},{1,9},{0,1},{10,2},{18... | collective-permute-start | bytes 196616 | tf_op jit(solution)/shard_map/ppermute | solution.py:587
  10.0 6.3 %collective-permute-start.2 = (bf16[2,2,64,128]{3,2,1,0:T(8,128)(2,1)S(1)}, bf16[2,2,64,128]{3,2,1,0:T(8,128)(2,1)S(1)}, u32[]{:S(2)}, u32[]{:S(2)}) collective-permute-start(bf16[2,2,64,128]{3,2,1,0:T(8,128)(2,1)S(1)} %get-tuple-element.112), channel_id=1, source_target_pairs={{0,8},{8,16},{16,24},{24,25},{25,17},{17,9},{9,1},{1,0},{2,10},{10... | collective-permute-start | bytes 196616 | tf_op jit(solution)/shard_map/ppermute | solution.py:587
  12.1 5.9 %collective-permute-start.4 = (bf16[2,2,64,128]{3,2,1,0:T(8,128)(2,1)S(1)}, bf16[2,2,64,128]{3,2,1,0:T(8,128)(2,1)S(1)}, u32[]{:S(2)}, u32[]{:S(2)}) collective-permute-start(bf16[2,2,64,128]{3,2,1,0:T(8,128)(2,1)S(1)} %pad_maximum_fusion), channel_id=1, source_target_pairs={{0,8},{8,16},{16,24},{24,0},{1,9},{9,17},{17,25},{25,1},{2,10},{10... | collective-permute-start | bytes 196616 | tf_op jit(solution)/shard_map/ppermute | solution.py:596
  14.5 4.7 %collective-permute-start.5 = (bf16[2,2,64,128]{3,2,1,0:T(8,128)(2,1)S(1)}, bf16[2,2,64,128]{3,2,1,0:T(8,128)(2,1)S(1)}, u32[]{:S(2)}, u32[]{:S(2)}) collective-permute-start(bf16[2,2,64,128]{3,2,1,0:T(8,128)(2,1)S(1)} %pad_maximum_fusion.1), channel_id=1, source_target_pairs={{8,0},{16,8},{24,16},{0,24},{9,1},{17,9},{25,17},{1,25},{10,2},{18... | collective-permute-start | bytes 196616 | tf_op jit(solution)/shard_map/ppermute | solution.py:597
  19.9 7.8 %collective-permute-start.6 = (bf16[8,2,64,128]{3,2,1,0:T(8,128)(2,1)S(1)}, bf16[8,2,64,128]{3,2,1,0:T(8,128)(2,1)S(1)}, u32[]{:S(2)}, u32[]{:S(2)}) collective-permute-start(bf16[8,2,64,128]{3,2,1,0:T(8,128)(2,1)S(1)} %get-tuple-element.74), channel_id=1, source_target_pairs={{0,2},{2,4},{4,6},{6,7},{7,5},{5,3},{3,1},{1,0},{8,10},{10,12},{12... | collective-permute-start | bytes 786440 | tf_op jit(solution)/shard_map/ppermute | solution.py:587
  21.5 6.4 %collective-permute-start.7 = (bf16[8,2,64,128]{3,2,1,0:T(8,128)(2,1)S(1)}, bf16[8,2,64,128]{3,2,1,0:T(8,128)(2,1)S(1)}, u32[]{:S(2)}, u32[]{:S(2)}) collective-permute-start(bf16[8,2,64,128]{3,2,1,0:T(8,128)(2,1)S(1)} %get-tuple-element.75), channel_id=1, source_target_pairs={{2,0},{4,2},{6,4},{7,6},{5,7},{3,5},{1,3},{0,1},{10,8},{12,10},{14... | collective-permute-start | bytes 786440 | tf_op jit(solution)/shard_map/ppermute | solution.py:587
  22.6 9.6 %collective-permute-start.9 = (bf16[2,2,64,128]{3,2,1,0:T(8,128)(2,1)S(1)}, bf16[2,2,64,128]{3,2,1,0:T(8,128)(2,1)S(1)}, u32[]{:S(2)}, u32[]{:S(2)}) collective-permute-start(bf16[2,2,64,128]{3,2,1,0:T(8,128)(2,1)S(1)} %get-tuple-element.127), channel_id=1, source_target_pairs={{8,0},{16,8},{24,16},{25,24},{17,25},{9,17},{1,9},{0,1},{10,2},{18... | collective-permute-start | bytes 196616 | tf_op jit(solution)/shard_map/ppermute | solution.py:587
  22.7 9.6 %collective-permute-start.8 = (bf16[2,2,64,128]{3,2,1,0:T(8,128)(2,1)S(1)}, bf16[2,2,64,128]{3,2,1,0:T(8,128)(2,1)S(1)}, u32[]{:S(2)}, u32[]{:S(2)}) collective-permute-start(bf16[2,2,64,128]{3,2,1,0:T(8,128)(2,1)S(1)} %get-tuple-element.128), channel_id=1, source_target_pairs={{0,8},{8,16},{16,24},{24,25},{25,17},{17,9},{9,1},{1,0},{2,10},{10... | collective-permute-start | bytes 196616 | tf_op jit(solution)/shard_map/ppermute | solution.py:587
  27.9 31.7 %collective-permute-start.12 = (bf16[8,320,256]{2,1,0:T(8,128)(2,1)S(1)}, bf16[8,320,256]{2,1,0:T(8,128)(2,1)S(1)}, u32[]{:S(2)}, u32[]{:S(2)}) collective-permute-start(bf16[8,320,256]{2,1,0:T(8,128)(2,1)S(1)} %sort_coarse.1.own_ref.refs_0_), channel_id=1, source_target_pairs={{0,1},{1,0},{2,3},{3,2},{4,5},{5,4},{6,7},{7,6},{8,9},{9,8},{10,11... | collective-permute-start | bytes 3932168 | tf_op jit(solution)/shard_map/ppermute | solution.py:665
  28.0 5.8 %collective-permute-start.10 = (bf16[2,2,64,128]{3,2,1,0:T(8,128)(2,1)S(1)}, bf16[2,2,64,128]{3,2,1,0:T(8,128)(2,1)S(1)}, u32[]{:S(2)}, u32[]{:S(2)}) collective-permute-start(bf16[2,2,64,128]{3,2,1,0:T(8,128)(2,1)S(1)} %pad_maximum_fusion.2), channel_id=1, source_target_pairs={{0,8},{8,16},{16,24},{24,0},{1,9},{9,17},{17,25},{25,1},{2,10},{10... | collective-permute-start | bytes 196616 | tf_op jit(solution)/shard_map/ppermute | solution.py:596
  35.3 6.9 %collective-permute-start.15 = (bf16[8,2,64,128]{3,2,1,0:T(8,128)(2,1)S(1)}, bf16[8,2,64,128]{3,2,1,0:T(8,128)(2,1)S(1)}, u32[]{:S(2)}, u32[]{:S(2)}) collective-permute-start(bf16[8,2,64,128]{3,2,1,0:T(8,128)(2,1)S(1)} %get-tuple-element.91), channel_id=1, source_target_pairs={{0,2},{2,4},{4,6},{6,7},{7,5},{5,3},{3,1},{1,0},{8,10},{10,12},{12... | collective-permute-start | bytes 786440 | tf_op jit(solution)/shard_map/ppermute | solution.py:587
  37.3 6.4 %collective-permute-start.16 = (bf16[8,2,64,128]{3,2,1,0:T(8,128)(2,1)S(1)}, bf16[8,2,64,128]{3,2,1,0:T(8,128)(2,1)S(1)}, u32[]{:S(2)}, u32[]{:S(2)}) collective-permute-start(bf16[8,2,64,128]{3,2,1,0:T(8,128)(2,1)S(1)} %get-tuple-element.92), channel_id=1, source_target_pairs={{2,0},{4,2},{6,4},{7,6},{5,7},{3,5},{1,3},{0,1},{10,8},{12,10},{14... | collective-permute-start | bytes 786440 | tf_op jit(solution)/shard_map/ppermute | solution.py:587
  38.4 10.5 %collective-permute-start.14 = (bf16[2,2,64,128]{3,2,1,0:T(8,128)(2,1)S(1)}, bf16[2,2,64,128]{3,2,1,0:T(8,128)(2,1)S(1)}, u32[]{:S(2)}, u32[]{:S(2)}) collective-permute-start(bf16[2,2,64,128]{3,2,1,0:T(8,128)(2,1)S(1)} %get-tuple-element.125), channel_id=1, source_target_pairs={{8,0},{16,8},{24,16},{25,24},{17,25},{9,17},{1,9},{0,1},{10,2},{18... | collective-permute-start | bytes 196616 | tf_op jit(solution)/shard_map/ppermute | solution.py:587
  38.6 10.2 %collective-permute-start.13 = (bf16[2,2,64,128]{3,2,1,0:T(8,128)(2,1)S(1)}, bf16[2,2,64,128]{3,2,1,0:T(8,128)(2,1)S(1)}, u32[]{:S(2)}, u32[]{:S(2)}) collective-permute-start(bf16[2,2,64,128]{3,2,1,0:T(8,128)(2,1)S(1)} %get-tuple-element.126), channel_id=1, source_target_pairs={{0,8},{8,16},{16,24},{24,25},{25,17},{17,9},{9,1},{1,0},{2,10},{10... | collective-permute-start | bytes 196616 | tf_op jit(solution)/shard_map/ppermute | solution.py:587
  43.7 5.2 %collective-permute-start.17 = (bf16[2,2,64,128]{3,2,1,0:T(8,128)(2,1)S(1)}, bf16[2,2,64,128]{3,2,1,0:T(8,128)(2,1)S(1)}, u32[]{:S(2)}, u32[]{:S(2)}) collective-permute-start(bf16[2,2,64,128]{3,2,1,0:T(8,128)(2,1)S(1)} %pad_maximum_fusion.4), channel_id=1, source_target_pairs={{0,8},{8,16},{16,24},{24,0},{1,9},{9,17},{17,25},{25,1},{2,10},{10... | collective-permute-start | bytes 196616 | tf_op jit(solution)/shard_map/ppermute | solution.py:596
  50.6 6.2 %collective-permute-start.19 = (bf16[2,1,2,64,128]{4,3,2,1,0:T(8,128)(2,1)S(1)}, bf16[2,1,2,64,128]{4,3,2,1,0:T(8,128)(2,1)S(1)}, u32[]{:S(2)}, u32[]{:S(2)}) collective-permute-start(bf16[2,1,2,64,128]{4,3,2,1,0:T(8,128)(2,1)S(1)} %get-tuple-element.98), channel_id=1, source_target_pairs={{0,6},{2,4},{4,2},{6,0},{1,7},{3,5},{5,3},{7,1},{8,14},{10,12},{12... | collective-permute-start | bytes 196616 | tf_op jit(solution)/shard_map/ppermute | solution.py:612
  54.4 5.2 %collective-permute-start.20 = (bf16[2,1,2,64,128]{4,3,2,1,0:T(8,128)(2,1)S(1)}, bf16[2,1,2,64,128]{4,3,2,1,0:T(8,128)(2,1)S(1)}, u32[]{:S(2)}, u32[]{:S(2)}) collective-permute-start(bf16[2,1,2,64,128]{4,3,2,1,0:T(8,128)(2,1)S(1)} %get-tuple-element.99), channel_id=1, source_target_pairs={{0,4},{2,6},{4,0},{6,2},{1,5},{3,7},{5,1},{7,3},{8,12},{10,14},{12... | collective-permute-start | bytes 196616 | tf_op jit(solution)/shard_map/ppermute | solution.py:612
  54.4 5.2 %collective-permute-start.21 = (bf16[2,1,2,64,128]{4,3,2,1,0:T(8,128)(2,1)S(1)}, bf16[2,1,2,64,128]{4,3,2,1,0:T(8,128)(2,1)S(1)}, u32[]{:S(2)}, u32[]{:S(2)}) collective-permute-start(bf16[2,1,2,64,128]{4,3,2,1,0:T(8,128)(2,1)S(1)} %get-tuple-element.100), channel_id=1, source_target_pairs={{0,2},{2,0},{4,6},{6,4},{1,3},{3,1},{5,7},{7,5},{8,10},{10,8},{12,... | collective-permute-start | bytes 196616 | tf_op jit(solution)/shard_map/ppermute | solution.py:612
  60.6 5.8 %collective-permute-start.23 = (bf16[4,2,64,128]{3,2,1,0:T(8,128)(2,1)S(1)}, bf16[4,2,64,128]{3,2,1,0:T(8,128)(2,1)S(1)}, u32[]{:S(2)}, u32[]{:S(2)}) collective-permute-start(bf16[4,2,64,128]{3,2,1,0:T(8,128)(2,1)S(1)} %get-tuple-element.103), channel_id=1, source_target_pairs={{2,0},{4,2},{6,4},{8,6},{10,8},{12,10},{14,12},{16,14},{18,16},{20... | collective-permute-start | bytes 393224 | tf_op jit(solution)/shard_map/ppermute | solution.py:587
  67.2 9.2 %collective-permute-start.24 = (bf16[2,1,2,64,128]{4,3,2,1,0:T(8,128)(2,1)S(1)}, bf16[2,1,2,64,128]{4,3,2,1,0:T(8,128)(2,1)S(1)}, u32[]{:S(2)}, u32[]{:S(2)}) collective-permute-start(bf16[2,1,2,64,128]{4,3,2,1,0:T(8,128)(2,1)S(1)} %get-tuple-element.107), channel_id=1, source_target_pairs={{0,6},{2,4},{4,2},{6,0},{1,7},{3,5},{5,3},{7,1},{8,14},{10,12},{12... | collective-permute-start | bytes 196616 | tf_op jit(solution)/shard_map/ppermute | solution.py:612
  74.1 5.2 %collective-permute-start.25 = (bf16[2,1,2,64,128]{4,3,2,1,0:T(8,128)(2,1)S(1)}, bf16[2,1,2,64,128]{4,3,2,1,0:T(8,128)(2,1)S(1)}, u32[]{:S(2)}, u32[]{:S(2)}) collective-permute-start(bf16[2,1,2,64,128]{4,3,2,1,0:T(8,128)(2,1)S(1)} %get-tuple-element.108), channel_id=1, source_target_pairs={{0,4},{2,6},{4,0},{6,2},{1,5},{3,7},{5,1},{7,3},{8,12},{10,14},{12... | collective-permute-start | bytes 196616 | tf_op jit(solution)/shard_map/ppermute | solution.py:612
  74.1 5.2 %collective-permute-start.26 = (bf16[2,1,2,64,128]{4,3,2,1,0:T(8,128)(2,1)S(1)}, bf16[2,1,2,64,128]{4,3,2,1,0:T(8,128)(2,1)S(1)}, u32[]{:S(2)}, u32[]{:S(2)}) collective-permute-start(bf16[2,1,2,64,128]{4,3,2,1,0:T(8,128)(2,1)S(1)} %get-tuple-element.109), channel_id=1, source_target_pairs={{0,2},{2,0},{4,6},{6,4},{1,3},{3,1},{5,7},{7,5},{8,10},{10,8},{12,... | collective-permute-start | bytes 196616 | tf_op jit(solution)/shard_map/ppermute | solution.py:612
  (7 other events, 40.7 us)
